TPU v7x, 256 devices: a whole 4x4x8 slice. The times are simulated.
256 devices in a mesh: group: 2 (over core), ep: 128 (over x, y, z).
Axes of the slice: x: 4, y: 4, z: 8, core: 2. Of those that a mesh axis runs over, the one named last changes fastest.
Arguments:
- thinker_rows: bfloat16 [16384, 2048], P('ep', 'group'), may hold values from -6 to 6
- owner_map: int32 [16384, 1], P('ep'), may hold values from 0 to 127, as said below
- talker_ids: int32 [16384, 8], P('ep'), may hold values from 0 to 127, all different within a row; in each aligned block of 128 rows (0 to 127, 128 to 255, ...) at most 12 rows name the same one
- project_weight: bfloat16 [2048, 1024], P('group'), may hold values from -0.125 to 0.125
- router_weight: bfloat16 [1024, 128], replicated, may hold values from -0.1875 to 0.1875
- expert_gate: bfloat16 [128, 1024, 384], P('ep'), may hold values from -0.1875 to 0.1875
- expert_up: bfloat16 [128, 1024, 384], P('ep'), may hold values from -0.1875 to 0.1875
- expert_down: bfloat16 [128, 384, 1024], P('ep'), may hold values from -0.3125 to 0.3125
Outputs:
- talker_out: bfloat16 [16384, 1024], P('ep', 'group')
Inputs may be any that keep to these rules, and one draw needn't show every extreme that they name: `owner_map`: of the 128 rows of one ep index, exactly 1 have each owner. `talker_ids`: each slot names 8 different experts; in each aligned block of 128 slots (one owner's) no expert is named more than 12 times, and in some block some expert is named exactly 12 times.
All inputs are finite; a program needn't handle non-finite values.
Results may differ from a plain program's by a relative error of at most 0.0057.
Values may be sent and summed in bfloat16 or wider, within the bound.
No kernel may reach another device: no remote copies, remote signals or barrier semaphores. Data moves between devices by JAX's collectives and lax.ppermute only.
A program may use at most 64 MiB of HBM per device.

v0:
```python
import jax
import jax.numpy as jnp
from jax import lax
from jax.sharding import PartitionSpec as P

QB = 32


def block_quantize(values):
    row_total, feature_total = values.shape
    blocks = values.astype(jnp.float32).reshape(row_total, feature_total // QB, QB)
    largest = jnp.max(jnp.abs(blocks), axis=2)
    scales = jnp.full(largest.shape, 16.0, jnp.float32)
    for exponent in range(3, -31, -1):
        scales = jnp.where(448.0 * 2.0**exponent >= largest, 2.0**exponent, scales)
    ratios = blocks / scales[:, :, None]
    magnitude = jnp.abs(ratios)
    spacing = jnp.full(ratios.shape, 2.0 ** (-9), jnp.float32)
    for exponent in range(-6, 9):
        spacing = jnp.where(magnitude >= 2.0**exponent, 2.0 ** (exponent - 3), spacing)
    scaled = (jnp.floor(ratios / spacing + 0.5) * spacing).astype(jnp.bfloat16)
    return (scaled, scales.astype(jnp.bfloat16))


def dequantize(scaled, scales):
    row_total = scaled.shape[0]
    restored = scaled.astype(jnp.float32) * scales.astype(jnp.float32)[:, :, None]
    return restored.astype(jnp.bfloat16).reshape(row_total, -1)


def slot_positions(targets, target_count):
    onehot = (targets[:, None] == jnp.arange(target_count, dtype=jnp.int32)[None, :]).astype(
        jnp.int32
    )
    before = jnp.cumsum(onehot, axis=0) - onehot
    return jnp.sum(before * onehot, axis=1)


def with_zero_row(values):
    return jnp.concatenate([values, jnp.zeros((1, values.shape[1]), values.dtype)], axis=0)


def body(
    thinker_rows,
    owner_map,
    talker_ids,
    project_weight,
    router_weight,
    expert_gate,
    expert_up,
    expert_down,
):
    ep_count = lax.axis_size("ep")
    core_count = lax.axis_size("group")
    my_core = lax.axis_index("group")
    row_count, feature_half = thinker_rows.shape
    slot_count, top_count = talker_ids.shape
    owner_capacity = slot_count // ep_count
    expert_capacity = 2 * ((3 * slot_count * top_count + 4 * ep_count - 1) // (4 * ep_count))
    half_capacity = expert_capacity // core_count
    model_width = router_weight.shape[0]
    half_width = model_width // core_count
    block_count = feature_half // QB
    owners = owner_map[:, 0]
    owner_places = owners * owner_capacity + slot_positions(owners, ep_count)
    send_order = (
        jnp.zeros((row_count,), jnp.int32)
        .at[owner_places]
        .set(jnp.arange(row_count, dtype=jnp.int32))
    )
    scaled, scales = block_quantize(thinker_rows)
    send_scaled = jnp.take(scaled.reshape(row_count, feature_half), send_order, axis=0).reshape(
        ep_count, owner_capacity, feature_half
    )
    send_scales = jnp.take(scales, send_order, axis=0).reshape(
        ep_count, owner_capacity, block_count
    )
    got_scaled, got_scales = (
        lax.all_to_all(send_scaled, "ep", split_axis=0, concat_axis=0, tiled=True),
        lax.all_to_all(send_scales, "ep", split_axis=0, concat_axis=0, tiled=True),
    )
    restored = dequantize(
        got_scaled.reshape(slot_count, block_count, QB), got_scales.reshape(slot_count, block_count)
    )
    partial_sum = jnp.dot(restored, project_weight, preferred_element_type=jnp.float32)
    talker_rows = lax.psum(partial_sum, "group").astype(jnp.bfloat16)
    talker_float = talker_rows.astype(jnp.float32)
    inverse = lax.rsqrt(jnp.mean(talker_float * talker_float, axis=1, keepdims=True) + 1e-06)
    normed = (talker_float * inverse).astype(jnp.bfloat16)
    logits = jnp.dot(normed, router_weight, preferred_element_type=jnp.float32)
    weights = jnp.exp(jnp.take_along_axis(logits, talker_ids, axis=1))
    slot_gates = weights / jnp.sum(weights, axis=1, keepdims=True)
    flat_ids = talker_ids.reshape(-1)
    assignment_count = slot_count * top_count
    positions = flat_ids * expert_capacity + slot_positions(flat_ids, ep_count)
    inverse_map = (
        jnp.full((ep_count * expert_capacity,), assignment_count, jnp.int32)
        .at[positions]
        .set(jnp.arange(assignment_count, dtype=jnp.int32))
    )
    own_items = lax.dynamic_slice_in_dim(
        inverse_map.reshape(ep_count, expert_capacity), my_core * half_capacity, half_capacity, 1
    )
    send_buffer = jnp.take(with_zero_row(normed), own_items // top_count, axis=0)
    received = lax.all_to_all(send_buffer, "ep", split_axis=0, concat_axis=0, tiled=True)
    item_count = received.shape[1]
    flat_rows = received.reshape(-1, model_width)
    gate_part = jnp.dot(flat_rows, expert_gate[0], preferred_element_type=jnp.float32)
    up_part = jnp.dot(flat_rows, expert_up[0], preferred_element_type=jnp.float32)
    hidden = (jax.nn.silu(gate_part) * up_part).astype(jnp.bfloat16)
    expert_out = jnp.dot(hidden, expert_down[0], preferred_element_type=jnp.float32).astype(
        jnp.bfloat16
    )
    expert_out = expert_out.reshape(ep_count, item_count, model_width)
    stacked = expert_out.reshape(ep_count, item_count, 1, model_width)
    returned = lax.all_to_all(
        lax.all_to_all(stacked, "group", split_axis=3, concat_axis=2, tiled=True),
        "ep",
        split_axis=0,
        concat_axis=0,
        tiled=True,
    )
    item_index = positions % expert_capacity
    expert_index = positions // expert_capacity
    picked_rows = (
        expert_index * expert_capacity
        + item_index % half_capacity * core_count
        + item_index // half_capacity
    )
    picked = (
        jnp.take(returned.reshape(-1, half_width), picked_rows, axis=0)
        .astype(jnp.float32)
        .reshape(slot_count, top_count, half_width)
    )
    mixed_rows = jnp.sum(slot_gates[:, :, None] * picked, axis=1)
    own_part = lax.dynamic_slice_in_dim(talker_float, my_core * half_width, half_width, 1)
    return (own_part + mixed_rows).astype(jnp.bfloat16)


def solution(mesh):
    return jax.shard_map(
        body,
        mesh=mesh,
        in_specs=(
            P("ep", "group"),
            P("ep", None),
            P("ep", None),
            P("group", None),
            P(),
            P("ep", None, None),
            P("ep", None, None),
            P("ep", None, None),
        ),
        out_specs=P("ep", "group"),
        check_vma=False,
    )
```

profile of v0, /device:TPU:1, one launch (start us, length us, event | category | flops | bytes accessed | tf_op | source)
XLA Modules:
  0.0 231.1 jit_solution(5231327847243887301)
XLA Ops:
  0.0 0.9 fusion.18
  0.9 0.2 reduce_window_sum.26
  1.1 0.8 select_reduce_fusion
  1.9 0.7 fusion.32
  2.6 1.0 scatter_custom_fusion
  3.6 1.0 convert_abs_fusion
  4.6 0.2 copy.139
  5.0 0.2 fusion.37
  5.1 0.7 gather_fusion.1
  5.9 0.7 copy.179
  6.6 16.3 %all-to-all-start.1 = ((bf16[128,1,32]{2,1,0:T(2,128)(2,1)}), bf16[128,1,32]{2,1,0:T(2,128)(2,1)S(1)}, u32[]{:S(2)}, u32[]{:S(2)}) async-start(bf16[128,1,32]{2,1,0:T(2,128)(2,1)} %copy.179), calls=%async_computation.1 | async-start | bytes 131072 | tf_op jit(solution)/shard_map/all_to_all | solution.py:80
  23.4 0.2 fusion.14
  23.9 1.0 copy.176
  24.9 1.8 fusion.16
  26.7 0.9 gather_fusion
  27.6 0.4 fusion.12
  28.2 0.6 broadcast.721
  28.8 0.8 reduce
  29.6 0.9 reshape.428
  30.5 3.0 %all-to-all-done.1 = bf16[128,1,32]{2,1,0:T(2,128)(2,1)S(1)} async-done(((bf16[128,1,32]{2,1,0:T(2,128)(2,1)}), bf16[128,1,32]{2,1,0:T(2,128)(2,1)S(1)}, u32[]{:S(2)}, u32[]{:S(2)}) %all-to-all-start.1) | async-done | bytes 8224 | tf_op jit(solution)/shard_map/all_to_all | solution.py:80
  33.5 10.3 %all-to-all-start = ((bf16[128,2,512]{2,1,0:T(2,128)(2,1)}), bf16[128,2,512]{2,1,0:T(2,128)(2,1)S(1)}, u32[]{:S(2)}, u32[]{:S(2)}) async-start(bf16[128,2,512]{2,1,0:T(2,128)(2,1)} %reshape.428), calls=%async_computation | async-start | bytes 524288 | tf_op jit(solution)/shard_map/all_to_all | solution.py:79
  43.9 4.3 %scatter_custom_fusion.1 = s32[1536]{0:T(1024)S(1)} fusion(s32[1024]{0:T(1024)S(1)} %bitcast.65, s32[1024]{0:T(1024)S(1)} %iota.17, s32[]{:T(128)} %constant.296.clone.1), kind=kCustom, calls=%fused_computation.77 | custom fusion | bytes 6148 | tf_op jit(solution)/shard_map/scatter | solution.py:99
  48.5 0.1 copy.192
  49.0 7.7 %all-to-all-done = bf16[128,2,512]{2,1,0:T(2,128)(2,1)S(1)} async-done(((bf16[128,2,512]{2,1,0:T(2,128)(2,1)}), bf16[128,2,512]{2,1,0:T(2,128)(2,1)S(1)}, u32[]{:S(2)}, u32[]{:S(2)}) %all-to-all-start) | async-done | bytes 262176 | tf_op jit(solution)/shard_map/all_to_all | solution.py:79
  56.8 0.2 reshape.429
  57.0 0.4 copy.178
  57.5 0.5 fusion.38
  58.0 7.7 %all-reduce.2 = bf16[128,1024]{1,0:T(8,128)(2,1)S(1)} all-reduce(f32[128,1024]{1,0:T(8,128)S(1)} %fusion.38), channel_id=1, replica_groups=mesh['group'=2,'ep'=128] {'group'}, use_global_device_ids=true, to_apply=%region_4.5 | all-reduce | flops 131072 | bytes 786432 | tf_op jit(solution)/shard_map/psum | solution.py:86
  66.0 3.6 %gather_fusion.2 = bf16[768,1024]{1,0:T(8,128)(2,1)} fusion(bf16[129,1024]{1,0:T(8,128)(2,1)S(1)} %concatenate.3, s32[1024]{0:T(1024)S(1)} %pad_clamp_fusion), kind=kCustom, calls=%fused_computation.2 | custom fusion | bytes 3148800 | tf_op jit(solution)/shard_map/jit(_take)/gather | solution.py:104
  69.5 3.7 %reshape.378 = bf16[128,6,1024]{2,1,0:T(8,128)(2,1)} reshape(bf16[768,1024]{1,0:T(8,128)(2,1)} %gather_fusion.2) | data formatting | bytes 3145728 | tf_op jit(solution)/shard_map/jit(_take)/gather | solution.py:104
  73.3 1.9 broadcast_select_fusion
  75.2 59.6 %all_to_all.32 = bf16[128,6,1024]{2,1,0:T(8,128)(2,1)} all-to-all(bf16[128,6,1024]{2,1,0:T(8,128)(2,1)S(1)} %broadcast_select_fusion), channel_id=1, replica_groups=mesh['group'=2,'ep'=128] {'ep'}, dimensions={0} | all-to-all | bytes 3145728 | tf_op jit(solution)/shard_map/all_to_all | solution.py:105
  134.8 3.7 %reshape.357 = bf16[768,1024]{1,0:T(8,128)(2,1)} reshape(bf16[128,6,1024]{2,1,0:T(8,128)(2,1)} %all_to_all.32) | data formatting | bytes 3145728 | tf_op jit(solution)/shard_map/reshape | solution.py:107
  138.5 3.6 %fusion.4 = f32[768,384]{1,0:T(8,128)} fusion(bf16[768,1024]{1,0:T(8,128)(2,1)} %reshape.357, bf16[1,1024,384]{2,1,0:T(8,128)(2,1)} %param.13), kind=kOutput, calls=%fused_computation.15 | convolution fusion | flops 603979776 | bytes 3538944 | tf_op jit(solution)/shard_map/dot_general | solution.py:108
  142.1 5.2 %convolution_convert_fusion = bf16[768,1024]{1,0:T(8,128)(2,1)} fusion(bf16[768,1024]{1,0:T(8,128)(2,1)} %reshape.357, f32[768,384]{1,0:T(8,128)} %fusion.4, bf16[1,384,1024]{2,1,0:T(8,128)(2,1)} %param.15, bf16[1,1024,384]{2,1,0:T(8,128)(2,1)} %param.14), kind=kOutput, calls=%fused_computation.9 | convolution fusion | flops 1210515456 | bytes 5898240 | tf_op jit(solution)/shard_map/dot_general | solution.py:111
  147.3 3.7 %reshape_reshape.3 = bf16[128,6,1,1024]{3,1,0,2:T(8,128)(2,1)} reshape(bf16[768,1024]{1,0:T(8,128)(2,1)} %convolution_convert_fusion) | data formatting | bytes 3145728 | tf_op jit(solution)/shard_map/reshape;reshape | solution.py:115
  151.0 4.5 %copy.194 = bf16[128,6,1,1024]{0,1,2,3:T(8,128)(2,1)} copy(bf16[128,6,1,1024]{3,1,0,2:T(8,128)(2,1)} %reshape_reshape.3) | data formatting | bytes 3145728 | tf_op jit(solution)/shard_map/reshape;reshape | solution.py:115
  155.5 10.3 %all_to_all.33 = bf16[128,6,1,1024]{0,1,2,3:T(8,128)(2,1)} all-to-all(bf16[128,6,1,1024]{0,1,2,3:T(8,128)(2,1)} %copy.194), channel_id=1, replica_groups=mesh['group'=2,'ep'=128] {'group'}, dimensions={3} | all-to-all | bytes 3145728 | tf_op jit(solution)/shard_map/all_to_all | solution.py:117
  165.8 4.4 %copy.196 = bf16[128,6,2,512]{3,2,1,0:T(2,128)(2,1)} copy(bf16[128,6,2,512]{0,1,3,2:T(8,128)(2,1)} %bitcast.60) | data formatting | bytes 3145728 | tf_op jit(solution)/shard_map/all_to_all | solution.py:117
  170.2 7.4 %all-to-all-start.4 = ((bf16[128,6,2,512]{3,2,1,0:T(2,128)(2,1)}), bf16[128,6,2,512]{3,2,1,0:T(2,128)(2,1)}, u32[]{:S(2)}, u32[]{:S(2)}) async-start(bf16[128,6,2,512]{3,2,1,0:T(2,128)(2,1)} %copy.196), calls=%async_computation.4 | async-start | bytes 3145728 | tf_op jit(solution)/shard_map/all_to_all | solution.py:116
  178.2 0.9 convert_element_type.119
  179.0 0.2 fusion.39
  179.2 6.8 %gather_fusion.4 = f32[1024]{0:T(1024)S(1)} fusion(f32[128,128]{1,0:T(8,128)S(1)} %fusion.39, s32[1024]{0:T(1024)S(1)} %reshape.393), kind=kCustom, calls=%fused_computation.4 | custom fusion | bytes 16384 | tf_op jit(solution)/shard_map/jit(take_along_axis)/gather | solution.py:91
  186.4 33.1 %all-to-all-done.4 = bf16[128,6,2,512]{3,2,1,0:T(2,128)(2,1)} async-done(((bf16[128,6,2,512]{3,2,1,0:T(2,128)(2,1)}), bf16[128,6,2,512]{3,2,1,0:T(2,128)(2,1)}, u32[]{:S(2)}, u32[]{:S(2)}) %all-to-all-start.4) | async-done | bytes 1572896 | tf_op jit(solution)/shard_map/all_to_all | solution.py:116
  219.4 3.6 %reshape.358 = bf16[1536,512]{1,0:T(8,128)(2,1)} reshape(bf16[128,6,2,512]{3,2,1,0:T(2,128)(2,1)} %all-to-all-done.4) | data formatting | bytes 3145728 | tf_op jit(solution)/shard_map/reshape | solution.py:131
  223.1 5.6 %gather_fusion.3 = bf16[1024,512]{1,0:T(8,128)(2,1)S(1)} fusion(bf16[1536,512]{1,0:T(8,128)(2,1)} %reshape.358, s32[1024]{0:T(1024)S(1)} %broadcast_clamp_fusion), kind=kCustom, calls=%fused_computation.3 | custom fusion | bytes 2101248 | tf_op jit(solution)/shard_map/jit(_take)/gather | solution.py:131
  228.7 0.8 multiply_reduce_fusion
  229.5 1.7 add_convert_fusion
  (57 shorter events, 3.1 us)
Async XLA Ops:
  0.0 57.5 %copy-start = (bf16[1024,1024]{1,0:T(8,128)(2,1)S(1)}, bf16[1024,1024]{1,0:T(8,128)(2,1)}, u32[]{:S(2)}) copy-start(bf16[1024,1024]{1,0:T(8,128)(2,1)} %param.11) | copy-start | bytes 6291460
  3.6 19.4 %copy-start.2 = (s32[128,8]{0,1:T(8,128)S(1)}, s32[128,8]{0,1:T(8,128)}, u32[]{:S(2)}) copy-start(s32[128,8]{0,1:T(8,128)} %param.10) | copy-start | bytes 12292
  6.6 26.8 %all-to-all-start.1 = ((bf16[128,1,32]{2,1,0:T(2,128)(2,1)}), bf16[128,1,32]{2,1,0:T(2,128)(2,1)S(1)}, u32[]{:S(2)}, u32[]{:S(2)}) async-start(bf16[128,1,32]{2,1,0:T(2,128)(2,1)} %copy.179), calls=%async_computation.1 | async-start | bytes 131072 | tf_op jit(solution)/shard_map/all_to_all | solution.py:80
  33.5 23.3 %all-to-all-start = ((bf16[128,2,512]{2,1,0:T(2,128)(2,1)}), bf16[128,2,512]{2,1,0:T(2,128)(2,1)S(1)}, u32[]{:S(2)}, u32[]{:S(2)}) async-start(bf16[128,2,512]{2,1,0:T(2,128)(2,1)} %reshape.428), calls=%async_computation | async-start | bytes 524288 | tf_op jit(solution)/shard_map/all_to_all | solution.py:79
  170.2 8.8 %copy-start.1 = (bf16[1024,128]{1,0:T(8,128)(2,1)S(1)}, bf16[1024,128]{1,0:T(8,128)(2,1)}, u32[]{:S(2)}) copy-start(bf16[1024,128]{1,0:T(8,128)(2,1)} %param.12) | copy-start | bytes 786436
  170.2 49.2 %all-to-all-start.4 = ((bf16[128,6,2,512]{3,2,1,0:T(2,128)(2,1)}), bf16[128,6,2,512]{3,2,1,0:T(2,128)(2,1)}, u32[]{:S(2)}, u32[]{:S(2)}) async-start(bf16[128,6,2,512]{3,2,1,0:T(2,128)(2,1)} %copy.196), calls=%async_computation.4 | async-start | bytes 3145728 | tf_op jit(solution)/shard_map/all_to_all | solution.py:116
where the time goes:
time: 232 us; the launch traced here: 231 us
  blocking collectives  77.6 us (33%)
  local copies, waits for them, and re-layouts  52.8 us (23%)
  waiting for transfers between devices  43.8 us (19%)
  starting transfers between devices  34 us (15%)
  other arithmetic  13 us (6%)
  matrix products  9.47 us (4%)
    all_to_all x1, blocking collectives, body(): lax.all_to_all(send_buffer, 'ep', split_axis=0, concat_axis=0, tiled=True)  59.6 us
    all_to_all x1, waiting for transfers between devices, body(): lax.all_to_all(lax.all_to_all(stacked, 'group', split_axis=3, concat_axis...  33.1 us
    all_to_all x1, starting transfers between devices, body(): lax.all_to_all(send_scales, 'ep', split_axis=0, concat_axis=0, tiled=True)  16.3 us
    all_to_all x1, starting transfers between devices, body(): lax.all_to_all(send_scaled, 'ep', split_axis=0, concat_axis=0, tiled=True)  10.3 us
    all_to_all x1, blocking collectives, body(): lax.all_to_all(stacked, 'group', split_axis=3, concat_axis=2, tiled=True)  10.3 us
    another operation x2, local copies, waits for them, and re-layouts, body(): stacked = expert_out.reshape(ep_count, item_count, 1, model_width)  8.21 us
    all_to_all x1, waiting for transfers between devices, body(): lax.all_to_all(send_scaled, 'ep', split_axis=0, concat_axis=0, tiled=True)  7.74 us
    psum x1, blocking collectives, body(): talker_rows = lax.psum(partial_sum, 'group').astype(jnp.bfloat16)  7.69 us
  transfers between devices with their start and end apart: 3, of which 3 were waited for; matrix products, arithmetic and copies ran while one was open for 9% of the time, Pallas kernels for 0%

commit v1 on v0

v1 whole, which is shorter than its diff:
```python
import jax
import jax.numpy as jnp
from jax import lax
from jax.experimental import pallas as pl
from jax.experimental.pallas import tpu as pltpu
from jax.sharding import Mesh
from jax.sharding import PartitionSpec as P

F32 = jnp.float32
BF16 = jnp.bfloat16
I32 = jnp.int32
EP = ("x", "y", "zp", "zb")
REGION = ("x", "y", "zb")
SWAP = [(0, 1), (1, 0)]
SMEM = pl.BlockSpec(memory_space=pltpu.SMEM)
VMEM = pl.BlockSpec(memory_space=pltpu.VMEM)
ANY = pl.BlockSpec(memory_space=pl.ANY)
PARAMS = pltpu.CompilerParams(vmem_limit_bytes=40 * 1024 * 1024)


def iota(shape, dim):
    return lax.broadcasted_iota(I32, shape, dim)


def dot(a, b):
    return jnp.dot(a, b, preferred_element_type=F32)


def dot_nt(a, b):
    return lax.dot_general(a, b, (((1,), (1,)), ((), ())), preferred_element_type=F32)


def dot_tn(a, b):
    return lax.dot_general(a, b, (((0,), (0,)), ((), ())), preferred_element_type=F32)


def quantize(x):
    magnitude = jnp.abs(x)
    lane = iota(x.shape, 1)
    largest = magnitude
    for step in (1, 2, 4, 8, 16):
        before = pltpu.roll(largest, step, 1)
        after = pltpu.roll(largest, 128 - step, 1)
        largest = jnp.maximum(largest, jnp.where((lane & step) != 0, before, after))
    power = jnp.full(x.shape, 2.0**-31, F32)
    inverse = jnp.full(x.shape, 2.0**31, F32)
    for step in (32, 16, 8, 4, 2, 1):
        larger = power * 2.0**step
        below = larger * 448.0 < largest
        power = jnp.where(below, larger, power)
        inverse = jnp.where(below, inverse * 2.0**-step, inverse)
    scale = jnp.minimum(power * 2.0, 16.0)
    inverse = jnp.maximum(inverse * 0.5, 0.0625)
    level = scale * 2.0**-6
    inverse = inverse * 2.0**6
    for step in (8, 4, 2, 1):
        larger = level * 2.0**step
        reached = larger <= magnitude
        level = jnp.where(reached, larger, level)
        inverse = jnp.where(reached, inverse * 2.0**-step, inverse)
    return (jnp.floor(x * (inverse * 8.0) + 0.5) * (level * 0.125)).astype(BF16)


def project_kernel(place_ref, x_ref, w_hbm, keep_ref, give_ref, restored, weight, sem):
    core = place_ref[0]
    copy = pltpu.make_async_copy(w_hbm, weight, sem)
    copy.start()
    for block in range(8):
        lanes = pl.ds(block * 128, 128)
        restored[:, lanes] = quantize(x_ref[:, lanes].astype(F32))
    copy.wait()
    rows = restored[...]
    mine = pl.ds(pl.multiple_of(core * 512, 512), 512)
    other = pl.ds(pl.multiple_of((1 - core) * 512, 512), 512)
    give_ref[...] = dot(rows, weight[:, other])
    keep_ref[...] = dot(rows, weight[:, mine])


def spread_kernel(owner_ref, keep_ref, got_ref, out_ref):
    projected = (keep_ref[...] + got_ref[...]).astype(BF16)
    n = iota((128, 512), 1)
    e = n >> 2
    wanted = ((((e >> 3) << 2) + (n & 3)) << 1) + (e & 1)
    chosen = (owner_ref[...] == wanted).astype(BF16)
    rows = dot_tn(chosen, projected).astype(BF16)
    a = iota((256, 256), 0)
    b = iota((256, 256), 1)
    order = (b == ((((a >> 2) & 3) << 6) + ((a >> 4) << 2) + (a & 3))).astype(BF16)
    for g in range(8):
        part = rows[g * 64 : (g + 1) * 64]
        stack = jnp.concatenate([part[:, f * 128 : (f + 1) * 128] for f in range(4)], axis=0)
        out_ref[pl.ds(g * 256, 256), :] = dot(order, stack).astype(BF16)


def region_expert(n24, zp):
    return ((n24 >> 1) << 3) + zp * 2 + (n24 & 1)


def expand_matrix(zp):
    n = iota((768, 128), 0)
    e = (n * 2731) >> 16
    return (iota((768, 128), 1) == region_expert(e, zp)).astype(BF16)


def item_code(n, core):
    r = n - ((n * 2731) >> 16) * 24
    member = (r * 43) >> 8
    return (r - member * 6 + core * 6 + member * 16).astype(F32)


def index_kernel(place_ref, ids0, ids1, ids2, ids3, code_ref, pick_ref):
    core = place_ref[0]
    zp = place_ref[1]
    lane = iota((128, 128), 1)
    earlier = (lane < iota((128, 128), 0)).astype(BF16)
    expand = expand_matrix(zp)
    wanted = item_code(iota((768, 128), 0), core)
    for k, ids in enumerate((ids0, ids1, ids2, ids3)):
        member = (zp + 4 - k) & 3
        rows = pl.ds(pl.multiple_of(member * 128, 128), 128)
        named = lane == ids[:, 0:1]
        for t in range(1, 8):
            named = named | (lane == ids[:, t : t + 1])
        rank = dot(earlier, named.astype(F32).astype(BF16))
        code = jnp.where(named, rank + (member * 16).astype(F32), -1.0)
        code_ref[rows, :] = code
        found = dot_nt(expand, code.astype(BF16))
        pick_ref[:, rows] = (found == wanted).astype(F32).astype(BF16)


def dispatch_kernel(place_ref, own_ref, other_ref, pick_ref, send_ref, normed_ref, rest_ref, rows):
    core = place_ref[0]
    zp = place_ref[1]
    a = iota((256, 256), 0)
    b = iota((256, 256), 1)
    order = (b == (((a & 15) << 4) + (a >> 4))).astype(BF16)
    for ref, half in ((own_ref, core), (other_ref, 1 - core)):
        for g in range(8):
            part = dot(order, ref[pl.ds(g * 256, 256), :]).astype(BF16)
            for f in range(4):
                lanes = pl.ds(pl.multiple_of(half * 512 + f * 128, 128), 128)
                for member in range(4):
                    at = (f * 4 + member) * 16
                    rows[pl.ds(member * 128 + g * 16, 16), lanes] = part[at : at + 16]
    for member in range(4):
        at = pl.ds(member * 128, 128)
        value = rows[at, :].astype(F32)
        inverse = lax.rsqrt(jnp.mean(value * value, axis=1, keepdims=True) + 1e-06)
        normed_ref[at, :] = (value * inverse).astype(BF16)
    for part in range(4):
        at = pl.ds(part * 192, 192)
        send_ref[at, :] = dot(pick_ref[at, :], normed_ref[...]).astype(BF16)
    rest_ref[...] = rows[
        pl.ds(pl.multiple_of(zp * 128, 128), 128), pl.ds(pl.multiple_of(core * 512, 512), 512)
    ]


def gate_kernel(place_ref, normed_ref, router_ref, code_ref, mix_ref):
    core = place_ref[0]
    zp = place_ref[1]
    expand = expand_matrix(zp)
    wanted = item_code(iota((128, 768), 1), core)
    for member in range(4):
        at = pl.ds(member * 128, 128)
        code = code_ref[at, :]
        logits = dot(normed_ref[at, :], router_ref[...])
        weights = jnp.where(code >= 0.0, jnp.exp(logits), 0.0)
        gates = weights / jnp.sum(weights, axis=1, keepdims=True)
        found = dot_nt(code.astype(BF16), expand)
        spread = dot_nt(gates.astype(BF16), expand)
        mix_ref[at, :] = jnp.where(found == wanted, spread, 0.0).astype(BF16)


def expert_kernel(x_ref, gate_ref, up_ref, down_ref, out_ref):
    x = x_ref[...]
    gate = dot(x, gate_ref[0])
    up = dot(x, up_ref[0])
    hidden = (gate / (1.0 + jnp.exp(-gate)) * up).astype(BF16)
    out_ref[...] = dot(hidden, down_ref[0]).astype(BF16)


def mix_kernel(mine, place_ref, mix_ref, back_ref, out_ref):
    core = place_ref[0]
    half = core if mine else 1 - core
    lanes = pl.ds(pl.multiple_of(half * 512, 512), 512)
    out_ref[...] = dot(mix_ref[...], back_ref[:, lanes]).astype(out_ref.dtype)


def share_kernel(place_ref, keep_ref, got_ref, own_ref, one_ref, two_ref, three_ref):
    zp = place_ref[1]
    for k, ref in enumerate((own_ref, one_ref, two_ref, three_ref)):
        at = pl.ds(pl.multiple_of(((zp + k) & 3) * 128, 128), 128)
        ref[...] = (keep_ref[at, :] + got_ref[at, :].astype(F32)).astype(ref.dtype)


def call(kernel, outs, ins, scratch=(), specs=None):
    return pl.pallas_call(
        kernel,
        out_shape=[jax.ShapeDtypeStruct(shape, dtype) for shape, dtype in outs],
        in_specs=specs or [SMEM] + [VMEM] * (len(ins) - 1),
        out_specs=[VMEM] * len(outs),
        scratch_shapes=list(scratch),
        compiler_params=PARAMS,
    )(*ins)


def around(k):
    return [(i, (i + k) % 4) for i in range(4)]


def body(
    thinker_rows,
    owner_map,
    talker_ids,
    project_weight,
    router_weight,
    expert_gate,
    expert_up,
    expert_down,
):
    core = lax.axis_index("group")
    zp = lax.axis_index("zp")
    place = jnp.stack([core, zp]).astype(I32)
    keep, give = call(
        project_kernel,
        [((128, 512), F32)] * 2,
        (place, thinker_rows, project_weight),
        [pltpu.VMEM((128, 1024), BF16), pltpu.VMEM((1024, 1024), BF16), pltpu.SemaphoreType.DMA],
        [SMEM, VMEM, ANY],
    )
    got = lax.ppermute(give, "group", SWAP)
    (sent,) = call(
        spread_kernel, [((2048, 128), BF16)], (owner_map, keep, got), specs=[VMEM, VMEM, VMEM]
    )
    own = lax.all_to_all(sent.reshape(128, 16, 128), EP, 0, 0, tiled=True)
    ids = [talker_ids] + [lax.ppermute(talker_ids, "zp", around(k)) for k in (1, 2, 3)]
    code, pick = call(
        index_kernel, [((512, 128), F32), ((768, 512), BF16)], (place, *ids)
    )
    other = lax.ppermute(own, "group", SWAP)
    send, normed, rest = call(
        dispatch_kernel,
        [((768, 1024), BF16), ((512, 1024), BF16), ((128, 512), BF16)],
        (place, own.reshape(2048, 128), other.reshape(2048, 128), pick),
        [pltpu.VMEM((512, 1024), BF16)],
    )
    items = lax.all_to_all(send.reshape(32, 24, 1024), REGION, 0, 0, tiled=True)
    (mix,) = call(gate_kernel, [((512, 768), BF16)], (place, normed, router_weight, code))
    expert_out = pl.pallas_call(
        expert_kernel,
        grid=(4,),
        out_shape=jax.ShapeDtypeStruct((768, 1024), BF16),
        in_specs=[
            pl.BlockSpec((192, 1024), lambda i: (i, 0)),
            pl.BlockSpec((1, 1024, 384), lambda i: (0, 0, 0)),
            pl.BlockSpec((1, 1024, 384), lambda i: (0, 0, 0)),
            pl.BlockSpec((1, 384, 1024), lambda i: (0, 0, 0)),
        ],
        out_specs=pl.BlockSpec((192, 1024), lambda i: (i, 0)),
        compiler_params=PARAMS,
    )(items.reshape(768, 1024), expert_gate, expert_up, expert_down)
    back = lax.all_to_all(expert_out.reshape(32, 24, 1024), REGION, 0, 0, tiled=True)
    back = back.reshape(768, 1024)

    def mixed(mine, dtype):
        return call(
            lambda *refs: mix_kernel(mine, *refs), [((512, 512), dtype)], (place, mix, back)
        )[0]

    given = lax.ppermute(mixed(False, F32), "group", SWAP)
    kept = mixed(True, F32)
    own_part, one, two, three = call(
        share_kernel, [((128, 512), F32)] + [((128, 512), BF16)] * 3, (place, kept, given)
    )
    total = own_part
    for k, part in ((1, one), (2, two), (3, three)):
        total = total + lax.ppermute(part, "zp", around(k)).astype(F32)
    return (rest.astype(F32) + total).astype(BF16)


def solution(mesh):
    ep = ("x", "y", "zp", "zb")
    split = Mesh(mesh.devices.reshape(2, 4, 4, 4, 2), ("group",) + ep)
    return jax.shard_map(
        body,
        mesh=split,
        in_specs=(
            P(ep, "group"),
            P(ep, None),
            P(ep, None),
            P("group", None),
            P(),
            P(ep, None, None),
            P(ep, None, None),
            P(ep, None, None),
        ),
        out_specs=P(ep, "group"),
        check_vma=False,
    )
```

time: 232 us -> 146 us (0.63)
  local copies, waits for them, and re-layouts: 52.8 us -> 4.68 us
  Pallas kernels: 0 us -> 18.5 us
  blocking collectives: 77.6 us -> 60.1 us
  other arithmetic: 13 us -> 0.81 us
  starting transfers between devices: 34 us -> 22 us
  matrix products: 9.47 us -> 0 us
  waiting for transfers between devices: 43.8 us -> 39.8 us
    all_to_all x3 -> x1, starting transfers between devices: 34 us -> 3.97 us  [body(): lax.all_to_all(expert_out.reshape(32, 24, 1024), REGION, 0, 0, tiled=True)]
    all_to_all x3 -> x1, waiting for transfers between devices: 43.8 us -> 17.9 us  [body(): lax.all_to_all(expert_out.reshape(32, 24, 1024), REGION, 0, 0, tiled=True)]
    ppermute x0 -> x9, waiting for transfers between devices: none -> 21.9 us  [the longest x3 11.8 us: body(): total = total + lax.ppermute(part, 'zp', around(k)).astype(F32)]
    gather x10 -> x0, local copies, waits for them, and re-layouts: 21.6 us -> none  [the longest x2 7.26 us: body(): jnp.take(with_zero_row(normed), own_items // top_count, axis=0)]
    pallas_call x0 -> x9, Pallas kernels: none -> 18.5 us  [the longest x8 14.2 us: call(): pl.pallas_call(kernel, out_shape=[jax.ShapeDtypeStruct(shape, dtype) for...]
    ppermute x0 -> x9, starting transfers between devices: none -> 18 us  [the longest x3 5.89 us: body(): total = total + lax.ppermute(part, 'zp', around(k)).astype(F32)]
    all_to_all x2, blocking collectives: 69.9 us -> 60.1 us  [the longest x1 32.9 us: body(): own = lax.all_to_all(sent.reshape(128, 16, 128), EP, 0, 0, tiled=True)]
    dot_general x4 -> x0, matrix products: 9.47 us -> none  [the longest x1 5.2 us: body(): jnp.dot(hidden, expert_down[0], preferred_element_type=jnp.float32)]
  transfers between devices with their start and end apart: 3 -> 10, of which waited for: 3 -> 9; matrix products, arithmetic and copies ran while one was open for 9% -> 0% of each run, Pallas kernels for 0% -> 3%
where the time goes in v1:
time: 146 us
  blocking collectives  60.1 us (41%)
  waiting for transfers between devices  39.8 us (27%)
  starting transfers between devices  22 us (15%)
  Pallas kernels  18.5 us (13%)
  local copies, waits for them, and re-layouts  4.68 us (3%)
    all_to_all x1, blocking collectives, body(): own = lax.all_to_all(sent.reshape(128, 16, 128), EP, 0, 0, tiled=True)  32.9 us
    all_to_all x1, blocking collectives, body(): items = lax.all_to_all(send.reshape(32, 24, 1024), REGION, 0, 0, tiled=True)  27.2 us
    all_to_all x1, waiting for transfers between devices, body(): lax.all_to_all(expert_out.reshape(32, 24, 1024), REGION, 0, 0, tiled=True)  17.9 us
    pallas_call x8, Pallas kernels, call(): pl.pallas_call(kernel, out_shape=[jax.ShapeDtypeStruct(shape, dtype) for...  14.2 us
    ppermute x3, waiting for transfers between devices, body(): total = total + lax.ppermute(part, 'zp', around(k)).astype(F32)  11.8 us
    ppermute x3, waiting for transfers between devices, body(): lax.ppermute(talker_ids, 'zp', around(k))  7.82 us
    ppermute x3, starting transfers between devices, body(): total = total + lax.ppermute(part, 'zp', around(k)).astype(F32)  5.89 us
    unnamed x22, local copies, waits for them, and re-layouts  4.68 us
  transfers between devices with their start and end apart: 10, of which 9 were waited for; matrix products, arithmetic and copies ran while one was open for 0% of the time, Pallas kernels for 3%

profile of v1, /device:TPU:1, one launch (start us, length us, event | category | flops | bytes accessed | tf_op | source)
XLA Modules:
  0.0 146.0 jit_solution(7385391090208352738)
XLA Ops:
  0.0 0.1 pad_add_fusion.place_ref.refs_0_
  0.1 1.6 %copy-done = bf16[1024,1024]{1,0:T(8,128)(2,1)S(1)} copy-done((bf16[1024,1024]{1,0:T(8,128)(2,1)S(1)}, bf16[1024,1024]{1,0:T(8,128)(2,1)}, u32[]{:S(2)}) %copy-start) | copy-done | bytes 2097176
  1.7 0.9 copy-done.4
  2.6 4.3 %shard_map.82 = (f32[128,512]{1,0:T(8,128)S(1)}, f32[128,512]{1,0:T(8,128)S(1)}) custom-call(s32[2]{0:T(128)S(1)} %pad_add_fusion.place_ref.refs_0_, bf16[128,1024]{1,0:T(8,128)(2,1)S(1)} %copy-done.4, bf16[1024,1024]{1,0:T(8,128)(2,1)S(1)} %copy-done), custom_call_target="tpu_custom_call" | custom-call | tf_op jit(solution)/shard_map/pallas_call | solution.py:197
  6.9 0.0 copy-start.8
  6.9 3.3 %collective-permute-start = (f32[128,512]{1,0:T(8,128)S(1)}, f32[128,512]{1,0:T(8,128)S(1)}, u32[]{:S(2)}, u32[]{:S(2)}) collective-permute-start(f32[128,512]{1,0:T(8,128)S(1)} %get-tuple-element.17), channel_id=1, source_target_pairs={{0,128},{128,0},{1,129},{129,1},{2,130},{130,2},{3,131},{131,3},{4... | collective-permute-start | bytes 786440 | tf_op jit(solution)/shard_map/ppermute | solution.py:231
  10.2 0.0 copy-done.9
  10.2 0.1 copy.9.owner_ref
  10.4 1.0 collective-permute-done.got_ref
  11.4 0.7 shard_map.83
  12.1 32.9 %all_to_all.15 = bf16[128,16,128]{2,1,0:T(8,128)(2,1)S(1)} all-to-all(bf16[128,16,128]{2,1,0:T(8,128)(2,1)S(1)} %bitcast.12), channel_id=1, replica_groups=mesh['group'=2,'x'=4,'y'=4,'zp'=4,'zb'=2] {'x','y','zp','zb'}, dimensions={0} | all-to-all | bytes 1048576 | tf_op jit(solution)/shard_map/all_to_all | solution.py:235
  45.0 2.3 %collective-permute-start.1 = (bf16[128,16,128]{2,1,0:T(8,128)(2,1)S(1)}, bf16[128,16,128]{2,1,0:T(8,128)(2,1)S(1)}, u32[]{:S(2)}, u32[]{:S(2)}) collective-permute-start(bf16[128,16,128]{2,1,0:T(8,128)(2,1)S(1)} %all_to_all.15), channel_id=1, source_target_pairs={{0,128},{128,0},{1,129},{129,1},{2,130},{130,2},{3,131},{131,3},{4... | collective-permute-start | bytes 1572872 | tf_op jit(solution)/shard_map/ppermute | solution.py:240
  47.3 0.0 copy-done.8
  47.3 0.1 copy.13.ids0
  47.4 0.3 collective-permute-start.4
  47.7 2.7 %collective-permute-start.3 = (s32[128,8]{1,0:T(8,128)S(1)}, s32[128,8]{1,0:T(8,128)S(1)}, u32[]{:S(2)}, u32[]{:S(2)}) collective-permute-start(s32[128,8]{1,0:T(8,128)S(1)} %copy.13.ids0), channel_id=1, source_target_pairs={{0,4},{2,6},{4,0},{6,2},{1,5},{3,7},{5,1},{7,3},{8,12},{10,14},{12... | collective-permute-start | bytes 12296 | tf_op jit(solution)/shard_map/ppermute | solution.py:236
  50.5 0.0 collective-permute-start.2
  50.5 5.4 %collective-permute-done.4.ids3 = s32[128,8]{1,0:T(8,128)S(1)} collective-permute-done((s32[128,8]{1,0:T(8,128)S(1)}, s32[128,8]{1,0:T(8,128)S(1)}, u32[]{:S(2)}, u32[]{:S(2)}) %collective-permute-start.4) | collective-permute-done | bytes 4128 | tf_op jit(solution)/shard_map/ppermute | solution.py:236
  55.9 1.4 collective-permute-done.3.ids2
  57.3 1.0 collective-permute-done.2.ids1
  58.3 1.8 %shard_map.84 = (f32[512,128]{1,0:T(8,128)S(1)}, bf16[768,512]{1,0:T(8,128)(2,1)S(1)}) custom-call(s32[2]{0:T(128)S(1)} %pad_add_fusion.place_ref.refs_0_, s32[128,8]{1,0:T(8,128)S(1)} %copy.13.ids0, s32[128,8]{1,0:T(8,128)S(1)} %collective-permute-done.2.ids1, s32[128,8]{1,0:T(8,128)S(1)} %collective-permute-done.3.ids2, ...), custom_call_target="tpu_custom_call" | custom-call | tf_op jit(solution)/shard_map/pallas_call | solution.py:197
  60.1 0.0 collective-permute-done.1
  60.1 2.5 %shard_map.85 = (bf16[768,1024]{1,0:T(8,128)(2,1)S(1)}, bf16[512,1024]{1,0:T(8,128)(2,1)S(1)}, bf16[128,512]{1,0:T(8,128)(2,1)S(1)}) custom-call(s32[2]{0:T(128)S(1)} %pad_add_fusion.place_ref.refs_0_, bf16[2048,128]{1,0:T(8,128)(2,1)S(1)} %bitcast.13, bf16[2048,128]{1,0:T(8,128)(2,1)S(1)} %bitcast.15, bf16[768,512]{1,0:T(8,128)(2,1)S(1)} %get-tuple-element.18.pick_ref), custom_call_target="tpu_custom_call" | custom-call | tf_op jit(solution)/shard_map/pallas_call | solution.py:197
  62.7 0.0 copy-done.6
  62.7 0.0 copy-start.1
  62.7 0.0 copy-start.2
  62.7 0.0 copy-start.3
  62.7 27.2 %all_to_all.16 = bf16[32,24,1024]{2,1,0:T(8,128)(2,1)S(1)} all-to-all(bf16[32,24,1024]{2,1,0:T(8,128)(2,1)S(1)} %bitcast.14), channel_id=1, replica_groups=mesh['group'=2,'x'=4,'y'=4,'zp'=4,'zb'=2] {'x','y','zb'}, dimensions={0} | all-to-all | bytes 3145728 | tf_op jit(solution)/shard_map/all_to_all | solution.py:247
  89.9 0.0 copy-done.3
  89.9 4.3 %shard_map.87 = bf16[768,1024]{1,0:T(8,128)(2,1)} custom-call(bf16[768,1024]{1,0:T(8,128)(2,1)S(1)} %bitcast.11, bf16[1,1024,384]{2,1,0:T(8,128)(2,1)S(1)} %copy-done.1, bf16[1,1024,384]{2,1,0:T(8,128)(2,1)S(1)} %copy-done.2, bf16[1,384,1024]{2,1,0:T(8,128)(2,1)S(1)} %copy-done.3), custom_call_target="tpu_custom_call" | custom-call | tf_op jit(solution)/shard_map/pallas_call | solution.py:249
  94.2 4.0 %all-to-all-start.2 = ((bf16[32,24,1024]{2,1,0:T(8,128)(2,1)}), bf16[32,24,1024]{2,1,0:T(8,128)(2,1)S(1)}, u32[]{:S(2)}, u32[]{:S(2)}) async-start(bf16[32,24,1024]{2,1,0:T(8,128)(2,1)} %bitcast.7), calls=%async_computation.2 | async-start | bytes 3145728 | tf_op jit(solution)/shard_map/all_to_all | solution.py:262
  98.2 0.0 copy-start.5
  98.2 0.9 copy-done.5
  99.1 0.9 copy-done.7
  100.1 2.1 %shard_map.86.refs_1_ = bf16[512,768]{1,0:T(8,128)(2,1)S(1)} custom-call(s32[2]{0:T(128)S(1)} %pad_add_fusion.place_ref.refs_0_, bf16[512,1024]{1,0:T(8,128)(2,1)S(1)} %get-tuple-element.20.normed_ref, bf16[1024,128]{1,0:T(8,128)(2,1)S(1)} %copy-done.5, f32[512,128]{1,0:T(8,128)S(1)} %copy-done.7), custom_call_target="tpu_custom_call" | custom-call | tf_op jit(solution)/shard_map/pallas_call | solution.py:197
  102.2 17.9 %all-to-all-done.2 = bf16[32,24,1024]{2,1,0:T(8,128)(2,1)S(1)} async-done(((bf16[32,24,1024]{2,1,0:T(8,128)(2,1)}), bf16[32,24,1024]{2,1,0:T(8,128)(2,1)S(1)}, u32[]{:S(2)}, u32[]{:S(2)}) %all-to-all-start.2) | async-done | bytes 1572896 | tf_op jit(solution)/shard_map/all_to_all | solution.py:262
  120.1 1.1 shard_map.89
  121.2 3.4 %collective-permute-start.5 = (f32[512,512]{1,0:T(8,128)S(1)}, f32[512,512]{1,0:T(8,128)S(1)}, u32[]{:S(2)}, u32[]{:S(2)}) collective-permute-start(f32[512,512]{1,0:T(8,128)S(1)} %shard_map.89), channel_id=1, source_target_pairs={{0,128},{128,0},{1,129},{129,1},{2,130},{130,2},{3,131},{131,3},{4... | collective-permute-start | bytes 3145736 | tf_op jit(solution)/shard_map/ppermute | solution.py:270
  124.5 1.1 shard_map.88.keep_ref
  125.7 1.2 collective-permute-done.5.got_ref
  126.8 0.6 shard_map.90
  127.5 0.1 collective-permute-start.6
  127.6 3.4 %collective-permute-start.7 = (bf16[128,512]{1,0:T(8,128)(2,1)S(1)}, bf16[128,512]{1,0:T(8,128)(2,1)S(1)}, u32[]{:S(2)}, u32[]{:S(2)}) collective-permute-start(bf16[128,512]{1,0:T(8,128)(2,1)S(1)} %get-tuple-element.25), channel_id=1, source_target_pairs={{0,4},{2,6},{4,0},{6,2},{1,5},{3,7},{5,1},{7,3},{8,12},{10,14},{12... | collective-permute-start | bytes 393224 | tf_op jit(solution)/shard_map/ppermute | solution.py:277
  131.0 2.4 %collective-permute-start.8 = (bf16[128,512]{1,0:T(8,128)(2,1)S(1)}, bf16[128,512]{1,0:T(8,128)(2,1)S(1)}, u32[]{:S(2)}, u32[]{:S(2)}) collective-permute-start(bf16[128,512]{1,0:T(8,128)(2,1)S(1)} %get-tuple-element.26), channel_id=1, source_target_pairs={{0,6},{2,0},{4,2},{6,4},{1,7},{3,1},{5,3},{7,5},{8,14},{10,8},{12,... | collective-permute-start | bytes 393224 | tf_op jit(solution)/shard_map/ppermute | solution.py:277
  133.4 2.3 %collective-permute-done.6 = bf16[128,512]{1,0:T(8,128)(2,1)S(1)} collective-permute-done((bf16[128,512]{1,0:T(8,128)(2,1)S(1)}, bf16[128,512]{1,0:T(8,128)(2,1)S(1)}, u32[]{:S(2)}, u32[]{:S(2)}) %collective-permute-start.6) | collective-permute-done | bytes 131104 | tf_op jit(solution)/shard_map/ppermute | solution.py:277
  135.7 4.8 %collective-permute-done.7 = bf16[128,512]{1,0:T(8,128)(2,1)S(1)} collective-permute-done((bf16[128,512]{1,0:T(8,128)(2,1)S(1)}, bf16[128,512]{1,0:T(8,128)(2,1)S(1)}, u32[]{:S(2)}, u32[]{:S(2)}) %collective-permute-start.7) | collective-permute-done | bytes 131104 | tf_op jit(solution)/shard_map/ppermute | solution.py:277
  140.5 4.7 %collective-permute-done.8 = bf16[128,512]{1,0:T(8,128)(2,1)S(1)} collective-permute-done((bf16[128,512]{1,0:T(8,128)(2,1)S(1)}, bf16[128,512]{1,0:T(8,128)(2,1)S(1)}, u32[]{:S(2)}, u32[]{:S(2)}) %collective-permute-start.8) | collective-permute-done | bytes 131104 | tf_op jit(solution)/shard_map/ppermute | solution.py:277
  145.2 0.7 add_convert_fusion
  (7 shorter events, 0.0 us)
Async XLA Ops:
  0.0 10.2 %copy-start.9 = (s32[128,1]{0,1:T(1,128)S(1)}, s32[128,1]{0,1:T(1,128)}, u32[]{:S(2)}) copy-start(s32[128,1]{0,1:T(1,128)} %param.9) | copy-start | bytes 1540
  0.1 1.6 %copy-start = (bf16[1024,1024]{1,0:T(8,128)(2,1)S(1)}, bf16[1024,1024]{1,0:T(8,128)(2,1)}, u32[]{:S(2)}) copy-start(bf16[1024,1024]{1,0:T(8,128)(2,1)} %w_hbm.1) | copy-start | bytes 6291460
  1.7 0.9 copy-start.4
  6.9 40.4 %copy-start.8 = (s32[128,8]{0,1:T(8,128)S(1)}, s32[128,8]{0,1:T(8,128)}, u32[]{:S(2)}) copy-start(s32[128,8]{0,1:T(8,128)} %param.10) | copy-start | bytes 12292
  6.9 4.5 %collective-permute-start = (f32[128,512]{1,0:T(8,128)S(1)}, f32[128,512]{1,0:T(8,128)S(1)}, u32[]{:S(2)}, u32[]{:S(2)}) collective-permute-start(f32[128,512]{1,0:T(8,128)S(1)} %get-tuple-element.17), channel_id=1, source_target_pairs={{0,128},{128,0},{1,129},{129,1},{2,130},{130,2},{3,131},{131,3},{4... | collective-permute-start | bytes 786440 | tf_op jit(solution)/shard_map/ppermute | solution.py:231
  45.0 15.1 %collective-permute-start.1 = (bf16[128,16,128]{2,1,0:T(8,128)(2,1)S(1)}, bf16[128,16,128]{2,1,0:T(8,128)(2,1)S(1)}, u32[]{:S(2)}, u32[]{:S(2)}) collective-permute-start(bf16[128,16,128]{2,1,0:T(8,128)(2,1)S(1)} %all_to_all.15), channel_id=1, source_target_pairs={{0,128},{128,0},{1,129},{129,1},{2,130},{130,2},{3,131},{131,3},{4... | collective-permute-start | bytes 1572872 | tf_op jit(solution)/shard_map/ppermute | solution.py:240
  47.4 8.5 %collective-permute-start.4 = (s32[128,8]{1,0:T(8,128)S(1)}, s32[128,8]{1,0:T(8,128)S(1)}, u32[]{:S(2)}, u32[]{:S(2)}) collective-permute-start(s32[128,8]{1,0:T(8,128)S(1)} %copy.13.ids0), channel_id=1, source_target_pairs={{0,6},{2,0},{4,2},{6,4},{1,7},{3,1},{5,3},{7,5},{8,14},{10,8},{12,... | collective-permute-start | bytes 12296 | tf_op jit(solution)/shard_map/ppermute | solution.py:236
  47.7 9.6 %collective-permute-start.3 = (s32[128,8]{1,0:T(8,128)S(1)}, s32[128,8]{1,0:T(8,128)S(1)}, u32[]{:S(2)}, u32[]{:S(2)}) collective-permute-start(s32[128,8]{1,0:T(8,128)S(1)} %copy.13.ids0), channel_id=1, source_target_pairs={{0,4},{2,6},{4,0},{6,2},{1,5},{3,7},{5,1},{7,3},{8,12},{10,14},{12... | collective-permute-start | bytes 12296 | tf_op jit(solution)/shard_map/ppermute | solution.py:236
  50.5 7.8 %collective-permute-start.2 = (s32[128,8]{1,0:T(8,128)S(1)}, s32[128,8]{1,0:T(8,128)S(1)}, u32[]{:S(2)}, u32[]{:S(2)}) collective-permute-start(s32[128,8]{1,0:T(8,128)S(1)} %copy.13.ids0), channel_id=1, source_target_pairs={{0,2},{2,4},{4,6},{6,0},{1,3},{3,5},{5,7},{7,1},{8,10},{10,12},{12... | collective-permute-start | bytes 12296 | tf_op jit(solution)/shard_map/ppermute | solution.py:236
  60.1 2.6 %copy-start.6 = (f32[512,128]{1,0:T(8,128)}, f32[512,128]{1,0:T(8,128)S(1)}, u32[]{:S(2)}) copy-start(f32[512,128]{1,0:T(8,128)S(1)} %get-tuple-element.21.code_ref) | copy-start | bytes 786436
  62.7 27.3 %copy-start.1 = (bf16[1,1024,384]{2,1,0:T(8,128)(2,1)S(1)}, bf16[1,1024,384]{2,1,0:T(8,128)(2,1)}, u32[]{:S(2)}) copy-start(bf16[1,1024,384]{2,1,0:T(8,128)(2,1)} %gate_ref.1) | copy-start | bytes 2359300
  62.7 27.3 %copy-start.2 = (bf16[1,1024,384]{2,1,0:T(8,128)(2,1)S(1)}, bf16[1,1024,384]{2,1,0:T(8,128)(2,1)}, u32[]{:S(2)}) copy-start(bf16[1,1024,384]{2,1,0:T(8,128)(2,1)} %up_ref.1) | copy-start | bytes 2359300
  62.7 27.2 %copy-start.3 = (bf16[1,384,1024]{2,1,0:T(8,128)(2,1)S(1)}, bf16[1,384,1024]{2,1,0:T(8,128)(2,1)}, u32[]{:S(2)}) copy-start(bf16[1,384,1024]{2,1,0:T(8,128)(2,1)} %down_ref.1) | copy-start | bytes 2359300
  94.2 25.8 %all-to-all-start.2 = ((bf16[32,24,1024]{2,1,0:T(8,128)(2,1)}), bf16[32,24,1024]{2,1,0:T(8,128)(2,1)S(1)}, u32[]{:S(2)}, u32[]{:S(2)}) async-start(bf16[32,24,1024]{2,1,0:T(8,128)(2,1)} %bitcast.7), calls=%async_computation.2 | async-start | bytes 3145728 | tf_op jit(solution)/shard_map/all_to_all | solution.py:262
  98.2 1.0 copy-start.5
  99.1 0.9 copy-start.7
  121.2 5.7 %collective-permute-start.5 = (f32[512,512]{1,0:T(8,128)S(1)}, f32[512,512]{1,0:T(8,128)S(1)}, u32[]{:S(2)}, u32[]{:S(2)}) collective-permute-start(f32[512,512]{1,0:T(8,128)S(1)} %shard_map.89), channel_id=1, source_target_pairs={{0,128},{128,0},{1,129},{129,1},{2,130},{130,2},{3,131},{131,3},{4... | collective-permute-start | bytes 3145736 | tf_op jit(solution)/shard_map/ppermute | solution.py:270
  127.5 8.2 %collective-permute-start.6 = (bf16[128,512]{1,0:T(8,128)(2,1)S(1)}, bf16[128,512]{1,0:T(8,128)(2,1)S(1)}, u32[]{:S(2)}, u32[]{:S(2)}) collective-permute-start(bf16[128,512]{1,0:T(8,128)(2,1)S(1)} %get-tuple-element.24), channel_id=1, source_target_pairs={{0,2},{2,4},{4,6},{6,0},{1,3},{3,5},{5,7},{7,1},{8,10},{10,12},{12... | collective-permute-start | bytes 393224 | tf_op jit(solution)/shard_map/ppermute | solution.py:277
  127.6 12.9 %collective-permute-start.7 = (bf16[128,512]{1,0:T(8,128)(2,1)S(1)}, bf16[128,512]{1,0:T(8,128)(2,1)S(1)}, u32[]{:S(2)}, u32[]{:S(2)}) collective-permute-start(bf16[128,512]{1,0:T(8,128)(2,1)S(1)} %get-tuple-element.25), channel_id=1, source_target_pairs={{0,4},{2,6},{4,0},{6,2},{1,5},{3,7},{5,1},{7,3},{8,12},{10,14},{12... | collective-permute-start | bytes 393224 | tf_op jit(solution)/shard_map/ppermute | solution.py:277
  131.0 14.3 %collective-permute-start.8 = (bf16[128,512]{1,0:T(8,128)(2,1)S(1)}, bf16[128,512]{1,0:T(8,128)(2,1)S(1)}, u32[]{:S(2)}, u32[]{:S(2)}) collective-permute-start(bf16[128,512]{1,0:T(8,128)(2,1)S(1)} %get-tuple-element.26), channel_id=1, source_target_pairs={{0,6},{2,0},{4,2},{6,4},{1,7},{3,1},{5,3},{7,5},{8,14},{10,8},{12,... | collective-permute-start | bytes 393224 | tf_op jit(solution)/shard_map/ppermute | solution.py:277

commit v2 on v1

v2 whole, which is shorter than its diff:
```python
import jax
import jax.numpy as jnp
from jax import lax
from jax.experimental import pallas as pl
from jax.experimental.pallas import tpu as pltpu
from jax.sharding import Mesh
from jax.sharding import PartitionSpec as P

F32 = jnp.float32
BF16 = jnp.bfloat16
I32 = jnp.int32
EP = ("x", "y", "zp", "zb")
REGION = ("x", "y", "zb")
SWAP = [(0, 1), (1, 0)]
SMEM = pl.BlockSpec(memory_space=pltpu.SMEM)
VMEM = pl.BlockSpec(memory_space=pltpu.VMEM)
HBM = pl.BlockSpec(memory_space=pltpu.HBM)
PARAMS = pltpu.CompilerParams(vmem_limit_bytes=40 * 1024 * 1024)


def iota(shape, dim):
    return lax.broadcasted_iota(I32, shape, dim)


def dot(a, b):
    return jnp.dot(a, b, preferred_element_type=F32)


def dot_nt(a, b):
    return lax.dot_general(a, b, (((1,), (1,)), ((), ())), preferred_element_type=F32)


def dot_tn(a, b):
    return lax.dot_general(a, b, (((0,), (0,)), ((), ())), preferred_element_type=F32)


def quantize(x):
    magnitude = jnp.abs(x)
    lane = iota(x.shape, 1)
    largest = magnitude
    for step in (1, 2, 4, 8, 16):
        before = pltpu.roll(largest, step, 1)
        after = pltpu.roll(largest, 128 - step, 1)
        largest = jnp.maximum(largest, jnp.where((lane & step) != 0, before, after))
    power = jnp.full(x.shape, 2.0**-31, F32)
    inverse = jnp.full(x.shape, 2.0**31, F32)
    for step in (32, 16, 8, 4, 2, 1):
        larger = power * 2.0**step
        below = larger * 448.0 < largest
        power = jnp.where(below, larger, power)
        inverse = jnp.where(below, inverse * 2.0**-step, inverse)
    scale = jnp.minimum(power * 2.0, 16.0)
    inverse = jnp.maximum(inverse * 0.5, 0.0625)
    level = scale * 2.0**-6
    inverse = inverse * 2.0**6
    for step in (8, 4, 2, 1):
        larger = level * 2.0**step
        reached = larger <= magnitude
        level = jnp.where(reached, larger, level)
        inverse = jnp.where(reached, inverse * 2.0**-step, inverse)
    return (jnp.floor(x * (inverse * 8.0) + 0.5) * (level * 0.125)).astype(BF16)


def project_kernel(place_ref, x_ref, w_hbm, keep_ref, give_ref, restored, weight, sem):
    core = place_ref[0]
    copy = pltpu.make_async_copy(w_hbm, weight, sem)
    copy.start()
    for block in range(8):
        lanes = pl.ds(block * 128, 128)
        restored[:, lanes] = quantize(x_ref[:, lanes].astype(F32))
    copy.wait()
    rows = restored[...]
    mine = pl.ds(pl.multiple_of(core * 512, 512), 512)
    other = pl.ds(pl.multiple_of((1 - core) * 512, 512), 512)
    give_ref[...] = dot(rows, weight[:, other])
    keep_ref[...] = dot(rows, weight[:, mine])


def by24(n):
    return (n * 2731) >> 16


def spread_kernel(owner_ref, keep_ref, got_ref, ids_ref, out_ref):
    projected = (keep_ref[...] + got_ref[...]).astype(BF16)
    n = iota((128, 512), 1)
    e = n >> 2
    wanted = ((((e >> 3) << 2) + (n & 3)) << 1) + (e & 1)
    chosen = (owner_ref[...] == wanted).astype(BF16)
    rows = dot_tn(chosen, projected).astype(BF16)
    pad = (iota((16, 8), 0) == iota((16, 8), 1)).astype(BF16)
    ids = dot_nt(pad, ids_ref[...].astype(F32).astype(BF16)).astype(BF16)
    a = iota((192, 144), 0)
    e = by24(a)
    i = a - e * 24
    source = jnp.where(i < 16, ((i >> 2) << 5) + (e << 2) + (i & 3), 112 + i)
    order = (iota((192, 144), 1) == source).astype(BF16)
    for g in range(16):
        part = rows[g * 32 : (g + 1) * 32]
        stack = jnp.concatenate([part[:, f * 128 : (f + 1) * 128] for f in range(4)] + [ids], axis=0)
        out_ref[pl.ds(g * 192, 192), :] = dot(order, stack).astype(BF16)


def expand_matrix(zp):
    e = by24(iota((768, 128), 0))
    return (iota((768, 128), 1) == ((e >> 1) << 3) + zp * 2 + (e & 1)).astype(BF16)


def item_code(n, half):
    r = n - by24(n) * 24
    member = (r * 43) >> 8
    return (r - member * 6 + half * 6 + member * 16).astype(F32)


def index_kernel(place_ref, own_ref, code_ref, pick_ref):
    core, zp, xy, zb = (place_ref[i] for i in range(4))
    expert = iota((128, 128), 0)
    earlier = (expert < iota((128, 128), 1)).astype(BF16)
    expert = expert.astype(F32)
    expand = expand_matrix(zp)
    wanted = item_code(iota((768, 128), 0), core)
    a = iota((16, 48), 0)
    choose = ((iota((16, 48), 1) == zb * 24 + 16 + a) & (a < 8)).astype(F32).astype(BF16)
    for member in range(4):
        pair = pl.ds(pl.multiple_of((xy * 4 + member) * 48, 48), 48)
        ids = dot(choose, own_ref[pair, :])
        named = expert == ids[0:1, :]
        for t in range(1, 8):
            named = named | (expert == ids[t : t + 1, :])
        rank = dot(named.astype(F32).astype(BF16), earlier)
        code = jnp.where(named, rank + 16.0 * member, -1.0)
        code_ref[pl.ds(member * 128, 128), :] = code.T
        found = dot(expand, code.astype(BF16))
        pick_ref[:, pl.ds(member * 128, 128)] = (found == wanted).astype(F32).astype(BF16)


def dispatch_kernel(place_ref, own_ref, other_ref, pick_ref, send_ref, normed_ref, rest_ref, rows):
    core = place_ref[0]
    zp = place_ref[1]
    a = iota((256, 384), 0)
    b = iota((256, 384), 1)
    order = (b == (a & 15) * 24 + (a >> 4)).astype(BF16)
    for ref, half in ((own_ref, core), (other_ref, 1 - core)):
        for g in range(8):
            part = dot(order, ref[pl.ds(g * 384, 384), :]).astype(BF16)
            for f in range(4):
                lanes = pl.ds(pl.multiple_of(half * 512 + f * 128, 128), 128)
                for member in range(4):
                    at = (f * 4 + member) * 16
                    rows[pl.ds(member * 128 + g * 16, 16), lanes] = part[at : at + 16]
    for member in range(4):
        at = pl.ds(member * 128, 128)
        value = rows[at, :].astype(F32)
        inverse = lax.rsqrt(jnp.mean(value * value, axis=1, keepdims=True) + 1e-06)
        normed_ref[at, :] = (value * inverse).astype(BF16)
    for part in range(4):
        at = pl.ds(part * 192, 192)
        send_ref[at, :] = dot(pick_ref[at, :], normed_ref[...]).astype(BF16)
    rest_ref[...] = rows[
        pl.ds(pl.multiple_of(zp * 128, 128), 128), pl.ds(pl.multiple_of(core * 512, 512), 512)
    ]


def gate_kernel(place_ref, normed_ref, router_ref, code_ref, mix0_ref, mix1_ref):
    expand = expand_matrix(place_ref[1])
    wanted = [item_code(iota((128, 768), 1), half) for half in (0, 1)]
    for member in range(4):
        at = pl.ds(member * 128, 128)
        code = code_ref[at, :]
        logits = dot(normed_ref[at, :], router_ref[...])
        weights = jnp.where(code >= 0.0, jnp.exp(logits), 0.0)
        gates = weights / jnp.sum(weights, axis=1, keepdims=True)
        found = dot_nt(code.astype(BF16), expand)
        spread = dot_nt(gates.astype(BF16), expand)
        mix0_ref[at, :] = jnp.where(found == wanted[0], spread, 0.0).astype(BF16)
        mix1_ref[at, :] = jnp.where(found == wanted[1], spread, 0.0).astype(BF16)


def hidden_kernel(x_ref, gate_ref, up_ref, out_ref):
    x = x_ref[...]
    gate = dot(x, gate_ref[0])
    up = dot(x, up_ref[0])
    out_ref[...] = (gate / (1.0 + jnp.exp(-gate)) * up).astype(BF16)


def down_kernel(place_ref, own_ref, other_ref, down_ref, out_ref):
    core = place_ref[0]
    mine = pl.ds(pl.multiple_of(core * 512, 512), 512)
    other = pl.ds(pl.multiple_of((1 - core) * 512, 512), 512)
    weight = down_ref[0, :, mine]
    out_ref[:, mine] = dot(own_ref[...], weight).astype(BF16)
    out_ref[:, other] = dot(other_ref[...], weight).astype(BF16)


def mix_kernel(place_ref, mix0_ref, mix1_ref, back_ref, rest_ref, own_ref, one_ref, two_ref, three_ref):
    zp = place_ref[1]
    for k, ref in ((2, two_ref), (1, one_ref), (3, three_ref), (0, own_ref)):
        at = pl.ds(pl.multiple_of(((zp + k) & 3) * 128, 128), 128)
        total = dot(mix0_ref[at, :], back_ref[:, 0:512]) + dot(mix1_ref[at, :], back_ref[:, 512:1024])
        if k == 0:
            total = total + rest_ref[...].astype(F32)
        ref[...] = total.astype(ref.dtype)


def call(kernel, outs, ins, scratch=(), specs=None):
    return pl.pallas_call(
        kernel,
        out_shape=[jax.ShapeDtypeStruct(shape, dtype) for shape, dtype in outs],
        in_specs=specs or [SMEM] + [VMEM] * (len(ins) - 1),
        out_specs=[VMEM] * len(outs),
        scratch_shapes=list(scratch),
        compiler_params=PARAMS,
    )(*ins)


def around(k):
    return [(i, (i + k) % 4) for i in range(4)]


def body(
    thinker_rows,
    owner_map,
    talker_ids,
    project_weight,
    router_weight,
    expert_gate,
    expert_up,
    expert_down,
):
    core = lax.axis_index("group")
    zp = lax.axis_index("zp")
    place = jnp.stack([core, zp, lax.axis_index(("x", "y")), lax.axis_index("zb")]).astype(I32)
    keep, give = call(
        project_kernel,
        [((128, 512), F32)] * 2,
        (place, thinker_rows, project_weight),
        [pltpu.VMEM((128, 1024), BF16), pltpu.VMEM((1024, 1024), BF16), pltpu.SemaphoreType.DMA],
        [SMEM, VMEM, HBM],
    )
    got = lax.ppermute(give, "group", SWAP)
    (sent,) = call(
        spread_kernel,
        [((3072, 128), BF16)],
        (owner_map, keep, got, talker_ids),
        specs=[VMEM] * 4,
    )
    own = lax.all_to_all(sent.reshape(128, 24, 128), EP, 0, 0, tiled=True)
    other = lax.ppermute(own, "group", SWAP)
    code, pick = call(
        index_kernel,
        [((512, 128), F32), ((768, 512), BF16)],
        (place, own.reshape(3072, 128)),
    )
    send, normed, rest = call(
        dispatch_kernel,
        [((768, 1024), BF16), ((512, 1024), BF16), ((128, 512), BF16)],
        (place, own.reshape(3072, 128), other.reshape(3072, 128), pick),
        [pltpu.VMEM((512, 1024), BF16)],
    )
    items = lax.all_to_all(send.reshape(32, 24, 1024), REGION, 0, 0, tiled=True)
    mix0, mix1 = call(
        gate_kernel, [((512, 768), BF16)] * 2, (place, normed, router_weight, code)
    )
    hidden = pl.pallas_call(
        hidden_kernel,
        grid=(4,),
        out_shape=jax.ShapeDtypeStruct((768, 384), BF16),
        in_specs=[
            pl.BlockSpec((192, 1024), lambda i: (i, 0)),
            pl.BlockSpec((1, 1024, 384), lambda i: (0, 0, 0)),
            pl.BlockSpec((1, 1024, 384), lambda i: (0, 0, 0)),
        ],
        out_specs=pl.BlockSpec((192, 384), lambda i: (i, 0)),
        compiler_params=PARAMS,
    )(items.reshape(768, 1024), expert_gate, expert_up)
    other_hidden = lax.ppermute(hidden, "group", SWAP)
    (expert_out,) = call(
        down_kernel, [((768, 1024), BF16)], (place, hidden, other_hidden, expert_down)
    )
    back = lax.all_to_all(expert_out.reshape(32, 24, 1024), REGION, 0, 0, tiled=True)
    total, one, two, three = call(
        mix_kernel,
        [((128, 512), F32)] + [((128, 512), BF16)] * 3,
        (place, mix0, mix1, back.reshape(768, 1024), rest),
    )
    for k, part in ((2, two), (1, one), (3, three)):
        total = total + lax.ppermute(part, "zp", around(k)).astype(F32)
    return total.astype(BF16)


def solution(mesh):
    ep = ("x", "y", "zp", "zb")
    split = Mesh(mesh.devices.reshape(2, 4, 4, 4, 2), ("group",) + ep)
    return jax.shard_map(
        body,
        mesh=split,
        in_specs=(
            P(ep, "group"),
            P(ep, None),
            P(ep, None),
            P("group", None),
            P(),
            P(ep, None, None),
            P(ep, None, None),
            P(ep, None, None),
        ),
        out_specs=P(ep, "group"),
        check_vma=False,
    )
```

time: 146 us -> 140 us (0.959)
  waiting for transfers between devices: 39.8 us -> 32.4 us
  starting transfers between devices: 22 us -> 16.2 us
  blocking collectives: 60.1 us -> 64.7 us
  local copies, waits for them, and re-layouts: 4.68 us -> 6.69 us
    ppermute x4 -> x1, waiting for transfers between devices: 8.98 us -> 1.63 us  [body(): other_hidden = lax.ppermute(hidden, 'group', SWAP)]
    all_to_all x1, blocking collectives: 32.9 us -> 38.6 us  [body(): own = lax.all_to_all(sent.reshape(128, 24, 128), EP, 0, 0, tiled=True)]
    ppermute x4 -> x1, starting transfers between devices: 6.44 us -> 1.61 us  [body(): other_hidden = lax.ppermute(hidden, 'group', SWAP)]
    ppermute x3, waiting for transfers between devices: 11.8 us -> 9.54 us  [body(): total = total + lax.ppermute(part, 'zp', around(k)).astype(F32)]
    all_to_all x1, waiting for transfers between devices: 17.9 us -> 20 us  [body(): lax.all_to_all(expert_out.reshape(32, 24, 1024), REGION, 0, 0, tiled=True)]
    unnamed x22 -> x26, local copies, waits for them, and re-layouts: 4.68 us -> 6.69 us
    pallas_call x1, Pallas kernels: 4.26 us -> 2.33 us  [body(): pl.pallas_call(hidden_kernel, grid=(4,), out_shape=jax.ShapeDtypeStruct((...]
    pallas_call x8 -> x7, Pallas kernels: 14.2 us -> 16 us  [call(): pl.pallas_call(kernel, out_shape=[jax.ShapeDtypeStruct(shape, dtype) for...]
  transfers between devices with their start and end apart: 10 -> 7, of which waited for: 9 -> 7; matrix products, arithmetic and copies ran while one was open for 0% -> 0% of each run, Pallas kernels for 3% -> 3%
where the time goes in v2:
time: 140 us; the launch traced here: 139 us
  blocking collectives  64.7 us (46%)
  waiting for transfers between devices  32.4 us (23%)
  Pallas kernels  18.4 us (13%)
  starting transfers between devices  16.2 us (12%)
  local copies, waits for them, and re-layouts  6.69 us (5%)
    all_to_all x1, blocking collectives, body(): own = lax.all_to_all(sent.reshape(128, 24, 128), EP, 0, 0, tiled=True)  38.6 us
    all_to_all x1, blocking collectives, body(): items = lax.all_to_all(send.reshape(32, 24, 1024), REGION, 0, 0, tiled=True)  26.1 us
    all_to_all x1, waiting for transfers between devices, body(): lax.all_to_all(expert_out.reshape(32, 24, 1024), REGION, 0, 0, tiled=True)  20 us
    pallas_call x7, Pallas kernels, call(): pl.pallas_call(kernel, out_shape=[jax.ShapeDtypeStruct(shape, dtype) for...  16 us
    ppermute x3, waiting for transfers between devices, body(): total = total + lax.ppermute(part, 'zp', around(k)).astype(F32)  9.54 us
    unnamed x26, local copies, waits for them, and re-layouts  6.69 us
    ppermute x3, starting transfers between devices, body(): total = total + lax.ppermute(part, 'zp', around(k)).astype(F32)  4.92 us
    all_to_all x1, starting transfers between devices, body(): lax.all_to_all(expert_out.reshape(32, 24, 1024), REGION, 0, 0, tiled=True)  4.15 us
  transfers between devices with their start and end apart: 7, of which 7 were waited for; matrix products, arithmetic and copies ran while one was open for 0% of the time, Pallas kernels for 3%

profile of v2, /device:TPU:1, one launch (start us, length us, event | category | flops | bytes accessed | tf_op | source)
XLA Modules:
  0.0 139.3 jit_solution(6399385072130551583)
XLA Ops:
  0.0 0.0 copy-start.11
  0.0 0.0 copy-start.10
  0.0 0.1 pad_add_fusion.place_ref
  0.1 0.0 copy-start
  0.1 1.6 %copy-done = bf16[1024,1024]{1,0:T(8,128)(2,1)S(1)} copy-done((bf16[1024,1024]{1,0:T(8,128)(2,1)S(1)}, bf16[1024,1024]{1,0:T(8,128)(2,1)}, u32[]{:S(2)}) %copy-start) | copy-done | bytes 2097176
  1.7 0.9 copy-done.6
  2.6 4.3 %shard_map.82 = (f32[128,512]{1,0:T(8,128)S(1)}, f32[128,512]{1,0:T(8,128)S(1)}) custom-call(s32[4]{0:T(128)S(1)} %pad_add_fusion.place_ref, bf16[128,1024]{1,0:T(8,128)(2,1)S(1)} %copy-done.6, bf16[1024,1024]{1,0:T(8,128)(2,1)S(1)} %copy-done), custom_call_target="tpu_custom_call" | custom-call | tf_op jit(solution)/shard_map/pallas_call | solution.py:205
  6.9 3.3 %collective-permute-start = (f32[128,512]{1,0:T(8,128)S(1)}, f32[128,512]{1,0:T(8,128)S(1)}, u32[]{:S(2)}, u32[]{:S(2)}) collective-permute-start(f32[128,512]{1,0:T(8,128)S(1)} %get-tuple-element.19), channel_id=1, source_target_pairs={{0,128},{128,0},{1,129},{129,1},{2,130},{130,2},{3,131},{131,3},{4... | collective-permute-start | bytes 786440 | tf_op jit(solution)/shard_map/ppermute | solution.py:239
  10.2 0.0 copy-done.11
  10.2 0.1 copy.9.owner_ref
  10.3 0.0 copy-done.10
  10.3 0.1 copy.10.ids_ref
  10.5 0.9 collective-permute-done.got_ref
  11.4 1.0 shard_map.83
  12.3 38.6 %all_to_all.15 = bf16[128,24,128]{2,1,0:T(8,128)(2,1)S(1)} all-to-all(bf16[128,24,128]{2,1,0:T(8,128)(2,1)S(1)} %bitcast.15), channel_id=1, replica_groups=mesh['group'=2,'x'=4,'y'=4,'zp'=4,'zb'=2] {'x','y','zp','zb'}, dimensions={0} | all-to-all | bytes 1572864 | tf_op jit(solution)/shard_map/all_to_all | solution.py:246
  51.0 2.2 %collective-permute-start.1 = (bf16[128,24,128]{2,1,0:T(8,128)(2,1)S(1)}, bf16[128,24,128]{2,1,0:T(8,128)(2,1)S(1)}, u32[]{:S(2)}, u32[]{:S(2)}) collective-permute-start(bf16[128,24,128]{2,1,0:T(8,128)(2,1)S(1)} %all_to_all.15), channel_id=1, source_target_pairs={{0,128},{128,0},{1,129},{129,1},{2,130},{130,2},{3,131},{131,3},{4... | collective-permute-start | bytes 2359304 | tf_op jit(solution)/shard_map/ppermute | solution.py:247
  53.2 1.7 %shard_map.84 = (f32[512,128]{1,0:T(8,128)S(1)}, bf16[768,512]{1,0:T(8,128)(2,1)S(1)}) custom-call(s32[4]{0:T(128)S(1)} %pad_add_fusion.place_ref, bf16[3072,128]{1,0:T(8,128)(2,1)S(1)} %bitcast.11), custom_call_target="tpu_custom_call" | custom-call | tf_op jit(solution)/shard_map/pallas_call | solution.py:205
  54.9 0.0 copy-start.8
  54.9 0.2 collective-permute-done.1
  55.1 2.8 %shard_map.85 = (bf16[768,1024]{1,0:T(8,128)(2,1)S(1)}, bf16[512,1024]{1,0:T(8,128)(2,1)S(1)}, bf16[128,512]{1,0:T(8,128)(2,1)S(1)}) custom-call(s32[4]{0:T(128)S(1)} %pad_add_fusion.place_ref, bf16[3072,128]{1,0:T(8,128)(2,1)S(1)} %bitcast.12, bf16[3072,128]{1,0:T(8,128)(2,1)S(1)} %bitcast.17, bf16[768,512]{1,0:T(8,128)(2,1)S(1)} %get-tuple-element.20.pick_ref), custom_call_target="tpu_custom_call" | custom-call | tf_op jit(solution)/shard_map/pallas_call | solution.py:205
  57.9 0.0 copy-done.8
  57.9 0.0 copy-start.1
  57.9 0.0 copy-start.2
  57.9 26.1 %all_to_all.16 = bf16[32,24,1024]{2,1,0:T(8,128)(2,1)S(1)} all-to-all(bf16[32,24,1024]{2,1,0:T(8,128)(2,1)S(1)} %bitcast.16), channel_id=1, replica_groups=mesh['group'=2,'x'=4,'y'=4,'zp'=4,'zb'=2] {'x','y','zb'}, dimensions={0} | all-to-all | bytes 3145728 | tf_op jit(solution)/shard_map/all_to_all | solution.py:259
  84.0 0.0 copy-done.1
  84.0 0.0 copy-done.2
  84.0 2.3 %shard_map.87.own_ref = bf16[768,384]{1,0:T(8,128)(2,1)S(1)} custom-call(bf16[768,1024]{1,0:T(8,128)(2,1)S(1)} %bitcast.13, bf16[1,1024,384]{2,1,0:T(8,128)(2,1)S(1)} %copy-done.1, bf16[1,1024,384]{2,1,0:T(8,128)(2,1)S(1)} %copy-done.2), custom_call_target="tpu_custom_call" | custom-call | tf_op jit(solution)/shard_map/pallas_call | solution.py:263
  86.4 1.6 %collective-permute-start.2 = (bf16[768,384]{1,0:T(8,128)(2,1)S(1)}, bf16[768,384]{1,0:T(8,128)(2,1)S(1)}, u32[]{:S(2)}, u32[]{:S(2)}) collective-permute-start(bf16[768,384]{1,0:T(8,128)(2,1)S(1)} %shard_map.87.own_ref), channel_id=1, source_target_pairs={{0,128},{128,0},{1,129},{129,1},{2,130},{130,2},{3,131},{131,3},{4... | collective-permute-start | bytes 1769480 | tf_op jit(solution)/shard_map/ppermute | solution.py:275
  88.0 1.6 %collective-permute-done.2.other_ref = bf16[768,384]{1,0:T(8,128)(2,1)S(1)} collective-permute-done((bf16[768,384]{1,0:T(8,128)(2,1)S(1)}, bf16[768,384]{1,0:T(8,128)(2,1)S(1)}, u32[]{:S(2)}, u32[]{:S(2)}) %collective-permute-start.2) | collective-permute-done | bytes 589856 | tf_op jit(solution)/shard_map/ppermute | solution.py:275
  89.6 0.0 copy-done.5
  89.6 2.7 %shard_map.88 = bf16[768,1024]{1,0:T(8,128)(2,1)} custom-call(s32[4]{0:T(128)S(1)} %pad_add_fusion.place_ref, bf16[768,384]{1,0:T(8,128)(2,1)S(1)} %shard_map.87.own_ref, bf16[768,384]{1,0:T(8,128)(2,1)S(1)} %collective-permute-done.2.other_ref, bf16[1,384,1024]{2,1,0:T(8,128)(2,1)S(1)} %copy-done.5), custom_call_target="tpu_custom_call" | custom-call | tf_op jit(solution)/shard_map/pallas_call | solution.py:205
  92.3 4.2 %all-to-all-start.2 = ((bf16[32,24,1024]{2,1,0:T(8,128)(2,1)}), bf16[32,24,1024]{2,1,0:T(8,128)(2,1)S(1)}, u32[]{:S(2)}, u32[]{:S(2)}) async-start(bf16[32,24,1024]{2,1,0:T(8,128)(2,1)} %bitcast.9), calls=%async_computation.2 | async-start | bytes 3145728 | tf_op jit(solution)/shard_map/all_to_all | solution.py:279
  96.5 0.0 copy-start.7
  96.5 0.9 copy-done.7
  97.4 0.9 copy-done.9
  98.4 2.1 %shard_map.86 = (bf16[512,768]{1,0:T(8,128)(2,1)S(1)}, bf16[512,768]{1,0:T(8,128)(2,1)S(1)}) custom-call(s32[4]{0:T(128)S(1)} %pad_add_fusion.place_ref, bf16[512,1024]{1,0:T(8,128)(2,1)S(1)} %get-tuple-element.21.normed_ref, bf16[1024,128]{1,0:T(8,128)(2,1)S(1)} %copy-done.7, f32[512,128]{1,0:T(8,128)S(1)} %copy-done.9), custom_call_target="tpu_custom_call" | custom-call | tf_op jit(solution)/shard_map/pallas_call | solution.py:205
  100.5 0.0 copy-start.3
  100.5 0.9 copy-done.3
  101.3 20.0 %all-to-all-done.2 = bf16[32,24,1024]{2,1,0:T(8,128)(2,1)S(1)} async-done(((bf16[32,24,1024]{2,1,0:T(8,128)(2,1)}), bf16[32,24,1024]{2,1,0:T(8,128)(2,1)S(1)}, u32[]{:S(2)}, u32[]{:S(2)}) %all-to-all-start.2) | async-done | bytes 1572896 | tf_op jit(solution)/shard_map/all_to_all | solution.py:279
  121.4 1.1 copy-done.4
  122.5 1.5 %shard_map.89 = (f32[128,512]{1,0:T(8,128)S(1)}, bf16[128,512]{1,0:T(8,128)(2,1)S(1)}, bf16[128,512]{1,0:T(8,128)(2,1)S(1)}, bf16[128,512]{1,0:T(8,128)(2,1)S(1)}) custom-call(s32[4]{0:T(128)S(1)} %pad_add_fusion.place_ref, bf16[512,768]{1,0:T(8,128)(2,1)S(1)} %get-tuple-element.23.mix0_ref, bf16[512,768]{1,0:T(8,128)(2,1)S(1)} %copy-done.4, ...), custom_call_target="tpu_custom_call" | custom-call | tf_op jit(solution)/shard_map/pallas_call | solution.py:205
  124.1 1.3 collective-permute-start.3
  125.4 1.4 %collective-permute-start.4 = (bf16[128,512]{1,0:T(8,128)(2,1)S(1)}, bf16[128,512]{1,0:T(8,128)(2,1)S(1)}, u32[]{:S(2)}, u32[]{:S(2)}) collective-permute-start(bf16[128,512]{1,0:T(8,128)(2,1)S(1)} %get-tuple-element.29), channel_id=1, source_target_pairs={{0,2},{2,4},{4,6},{6,0},{1,3},{3,5},{5,7},{7,1},{8,10},{10,12},{12... | collective-permute-start | bytes 393224 | tf_op jit(solution)/shard_map/ppermute | solution.py:286
  126.8 2.2 %collective-permute-start.5 = (bf16[128,512]{1,0:T(8,128)(2,1)S(1)}, bf16[128,512]{1,0:T(8,128)(2,1)S(1)}, u32[]{:S(2)}, u32[]{:S(2)}) collective-permute-start(bf16[128,512]{1,0:T(8,128)(2,1)S(1)} %get-tuple-element.30), channel_id=1, source_target_pairs={{0,6},{2,0},{4,2},{6,4},{1,7},{3,1},{5,3},{7,5},{8,14},{10,8},{12,... | collective-permute-start | bytes 393224 | tf_op jit(solution)/shard_map/ppermute | solution.py:286
  129.0 6.6 %collective-permute-done.3 = bf16[128,512]{1,0:T(8,128)(2,1)S(1)} collective-permute-done((bf16[128,512]{1,0:T(8,128)(2,1)S(1)}, bf16[128,512]{1,0:T(8,128)(2,1)S(1)}, u32[]{:S(2)}, u32[]{:S(2)}) %collective-permute-start.3) | collective-permute-done | bytes 131104 | tf_op jit(solution)/shard_map/ppermute | solution.py:286
  135.6 1.9 %collective-permute-done.4 = bf16[128,512]{1,0:T(8,128)(2,1)S(1)} collective-permute-done((bf16[128,512]{1,0:T(8,128)(2,1)S(1)}, bf16[128,512]{1,0:T(8,128)(2,1)S(1)}, u32[]{:S(2)}, u32[]{:S(2)}) %collective-permute-start.4) | collective-permute-done | bytes 131104 | tf_op jit(solution)/shard_map/ppermute | solution.py:286
  137.4 1.1 collective-permute-done.5
  138.5 0.7 add_convert_fusion
  (4 shorter events, 0.0 us)
Async XLA Ops:
  0.0 10.2 %copy-start.11 = (s32[128,1]{0,1:T(1,128)S(1)}, s32[128,1]{0,1:T(1,128)}, u32[]{:S(2)}) copy-start(s32[128,1]{0,1:T(1,128)} %param.9) | copy-start | bytes 1540
  0.0 10.3 %copy-start.10 = (s32[128,8]{0,1:T(8,128)S(1)}, s32[128,8]{0,1:T(8,128)}, u32[]{:S(2)}) copy-start(s32[128,8]{0,1:T(8,128)} %param.10) | copy-start | bytes 12292
  0.1 1.6 %copy-start = (bf16[1024,1024]{1,0:T(8,128)(2,1)S(1)}, bf16[1024,1024]{1,0:T(8,128)(2,1)}, u32[]{:S(2)}) copy-start(bf16[1024,1024]{1,0:T(8,128)(2,1)} %w_hbm.1) | copy-start | bytes 6291460
  1.7 0.9 copy-start.6
  6.9 4.5 %collective-permute-start = (f32[128,512]{1,0:T(8,128)S(1)}, f32[128,512]{1,0:T(8,128)S(1)}, u32[]{:S(2)}, u32[]{:S(2)}) collective-permute-start(f32[128,512]{1,0:T(8,128)S(1)} %get-tuple-element.19), channel_id=1, source_target_pairs={{0,128},{128,0},{1,129},{129,1},{2,130},{130,2},{3,131},{131,3},{4... | collective-permute-start | bytes 786440 | tf_op jit(solution)/shard_map/ppermute | solution.py:239
  51.0 4.1 %collective-permute-start.1 = (bf16[128,24,128]{2,1,0:T(8,128)(2,1)S(1)}, bf16[128,24,128]{2,1,0:T(8,128)(2,1)S(1)}, u32[]{:S(2)}, u32[]{:S(2)}) collective-permute-start(bf16[128,24,128]{2,1,0:T(8,128)(2,1)S(1)} %all_to_all.15), channel_id=1, source_target_pairs={{0,128},{128,0},{1,129},{129,1},{2,130},{130,2},{3,131},{131,3},{4... | collective-permute-start | bytes 2359304 | tf_op jit(solution)/shard_map/ppermute | solution.py:247
  54.9 3.0 %copy-start.8 = (f32[512,128]{1,0:T(8,128)}, f32[512,128]{1,0:T(8,128)S(1)}, u32[]{:S(2)}) copy-start(f32[512,128]{1,0:T(8,128)S(1)} %get-tuple-element.22.code_ref) | copy-start | bytes 786436
  57.9 26.1 %copy-start.1 = (bf16[1,1024,384]{2,1,0:T(8,128)(2,1)S(1)}, bf16[1,1024,384]{2,1,0:T(8,128)(2,1)}, u32[]{:S(2)}) copy-start(bf16[1,1024,384]{2,1,0:T(8,128)(2,1)} %gate_ref.1) | copy-start | bytes 2359300
  57.9 26.1 %copy-start.2 = (bf16[1,1024,384]{2,1,0:T(8,128)(2,1)S(1)}, bf16[1,1024,384]{2,1,0:T(8,128)(2,1)}, u32[]{:S(2)}) copy-start(bf16[1,1024,384]{2,1,0:T(8,128)(2,1)} %up_ref.1) | copy-start | bytes 2359300
  84.0 5.6 %copy-start.5 = (bf16[1,384,1024]{2,1,0:T(8,128)(2,1)S(1)}, bf16[1,384,1024]{2,1,0:T(8,128)(2,1)}, u32[]{:S(2)}) copy-start(bf16[1,384,1024]{2,1,0:T(8,128)(2,1)} %down_ref.1) | copy-start | bytes 2359300
  86.4 3.2 %collective-permute-start.2 = (bf16[768,384]{1,0:T(8,128)(2,1)S(1)}, bf16[768,384]{1,0:T(8,128)(2,1)S(1)}, u32[]{:S(2)}, u32[]{:S(2)}) collective-permute-start(bf16[768,384]{1,0:T(8,128)(2,1)S(1)} %shard_map.87.own_ref), channel_id=1, source_target_pairs={{0,128},{128,0},{1,129},{129,1},{2,130},{130,2},{3,131},{131,3},{4... | collective-permute-start | bytes 1769480 | tf_op jit(solution)/shard_map/ppermute | solution.py:275
  92.3 29.1 %all-to-all-start.2 = ((bf16[32,24,1024]{2,1,0:T(8,128)(2,1)}), bf16[32,24,1024]{2,1,0:T(8,128)(2,1)S(1)}, u32[]{:S(2)}, u32[]{:S(2)}) async-start(bf16[32,24,1024]{2,1,0:T(8,128)(2,1)} %bitcast.9), calls=%async_computation.2 | async-start | bytes 3145728 | tf_op jit(solution)/shard_map/all_to_all | solution.py:279
  96.5 1.0 copy-start.7
  97.4 0.9 copy-start.9
  100.5 0.9 copy-start.3
  121.4 1.1 copy-start.4
  124.1 11.5 %collective-permute-start.3 = (bf16[128,512]{1,0:T(8,128)(2,1)S(1)}, bf16[128,512]{1,0:T(8,128)(2,1)S(1)}, u32[]{:S(2)}, u32[]{:S(2)}) collective-permute-start(bf16[128,512]{1,0:T(8,128)(2,1)S(1)} %get-tuple-element.28), channel_id=1, source_target_pairs={{0,4},{2,6},{4,0},{6,2},{1,5},{3,7},{5,1},{7,3},{8,12},{10,14},{12... | collective-permute-start | bytes 393224 | tf_op jit(solution)/shard_map/ppermute | solution.py:286
  125.4 12.0 %collective-permute-start.4 = (bf16[128,512]{1,0:T(8,128)(2,1)S(1)}, bf16[128,512]{1,0:T(8,128)(2,1)S(1)}, u32[]{:S(2)}, u32[]{:S(2)}) collective-permute-start(bf16[128,512]{1,0:T(8,128)(2,1)S(1)} %get-tuple-element.29), channel_id=1, source_target_pairs={{0,2},{2,4},{4,6},{6,0},{1,3},{3,5},{5,7},{7,1},{8,10},{10,12},{12... | collective-permute-start | bytes 393224 | tf_op jit(solution)/shard_map/ppermute | solution.py:286
  126.8 11.7 %collective-permute-start.5 = (bf16[128,512]{1,0:T(8,128)(2,1)S(1)}, bf16[128,512]{1,0:T(8,128)(2,1)S(1)}, u32[]{:S(2)}, u32[]{:S(2)}) collective-permute-start(bf16[128,512]{1,0:T(8,128)(2,1)S(1)} %get-tuple-element.30), channel_id=1, source_target_pairs={{0,6},{2,0},{4,2},{6,4},{1,7},{3,1},{5,3},{7,5},{8,14},{10,8},{12,... | collective-permute-start | bytes 393224 | tf_op jit(solution)/shard_map/ppermute | solution.py:286

commit v3 on v2

v3 whole, which is shorter than its diff:
```python
import functools

import jax
import jax.numpy as jnp
from jax import lax
from jax.experimental import pallas as pl
from jax.experimental.pallas import tpu as pltpu
from jax.sharding import Mesh
from jax.sharding import PartitionSpec as P

F32 = jnp.float32
BF16 = jnp.bfloat16
I32 = jnp.int32
EP = ("x", "y", "zp", "zb")
REGION = ("x", "y", "zb")
SWAP = [(0, 1), (1, 0)]
VMEM = pl.BlockSpec(memory_space=pltpu.VMEM)
HBM = pl.BlockSpec(memory_space=pltpu.HBM)
PARAMS = pltpu.CompilerParams(vmem_limit_bytes=16 * 1024 * 1024)


def iota(shape, dim):
    return lax.broadcasted_iota(I32, shape, dim)


def dot(a, b):
    return jnp.dot(a, b, preferred_element_type=F32)


def dot_nt(a, b):
    return lax.dot_general(a, b, (((1,), (1,)), ((), ())), preferred_element_type=F32)


def dot_tn(a, b):
    return lax.dot_general(a, b, (((0,), (0,)), ((), ())), preferred_element_type=F32)


def quantize(x_ref, out_ref):
    rows = x_ref.shape[0]
    r = iota((128, 128), 0)
    lane = iota((128, 128), 1)
    compact = jnp.zeros((rows, 128), F32)
    for b in range(8):
        largest = jnp.abs(x_ref[:, pl.ds(b * 128, 128)].astype(F32))
        for step in (16, 8, 4, 2, 1):
            largest = jnp.maximum(largest, pltpu.roll(largest, 128 - step, 1))
        first = (lane == r + b) & ((r & 31) == 0)
        compact = compact + dot(largest.astype(BF16), first.astype(F32).astype(BF16))
    power = jnp.full(compact.shape, 2.0**-31, F32)
    inverse = jnp.full(compact.shape, 2.0**31, F32)
    for step in (32, 16, 8, 4, 2, 1):
        larger = power * 2.0**step
        below = larger * 448.0 < compact
        power = jnp.where(below, larger, power)
        inverse = jnp.where(below, inverse * 2.0**-step, inverse)
    spacing = (jnp.minimum(power * 2.0, 16.0) * 2.0**-9).astype(BF16)
    inverse = (jnp.maximum(inverse * 0.5, 0.0625) * 2.0**9).astype(BF16)
    for b in range(8):
        lanes = pl.ds(b * 128, 128)
        spread = (r == (lane & 96) + b).astype(F32).astype(BF16)
        x = x_ref[:, lanes].astype(F32)
        size = jnp.abs(x) * 0.125
        level = dot(spacing, spread)
        over = dot(inverse, spread)
        for step in (8, 4, 2, 1):
            larger = level * 2.0**step
            reached = larger <= size
            level = jnp.where(reached, larger, level)
            over = jnp.where(reached, over * 2.0**-step, over)
        out_ref[:, lanes] = (jnp.floor(x * over + 0.5) * level).astype(BF16)


def halves():
    core = lax.axis_index("group")
    mine = pl.ds(pl.multiple_of(core * 512, 512), 512)
    other = pl.ds(pl.multiple_of((1 - core) * 512, 512), 512)
    return mine, other


def project_kernel(x_ref, w_hbm, give_ref, keep_ref, restored, weight, sem):
    copy = pltpu.make_async_copy(w_hbm, weight, sem)
    copy.start()
    quantize(x_ref, restored)
    copy.wait()
    mine, other = halves()
    give_ref[...] = dot(restored[...], weight[:, other])
    keep_ref[...] = dot(restored[...], weight[:, mine])


def by24(n):
    return (n * 2731) >> 16


def spread_kernel(owner_ref, keep_ref, got_ref, ids_ref, out_ref):
    projected = (keep_ref[...] + got_ref[...]).astype(BF16)
    n = iota((128, 512), 1)
    e = n >> 2
    wanted = ((((e >> 3) << 2) + (n & 3)) << 1) + (e & 1)
    chosen = (owner_ref[...] == wanted).astype(BF16)
    rows = dot_tn(chosen, projected).astype(BF16)
    pad = (iota((16, 8), 0) == iota((16, 8), 1)).astype(BF16)
    ids = dot_nt(pad, ids_ref[...].astype(F32).astype(BF16)).astype(BF16)
    a = iota((192, 144), 0)
    e = by24(a)
    i = a - e * 24
    source = jnp.where(i < 16, ((i >> 2) << 5) + (e << 2) + (i & 3), 112 + i)
    order = (iota((192, 144), 1) == source).astype(BF16)
    for g in range(16):
        part = rows[g * 32 : (g + 1) * 32]
        stack = jnp.concatenate([part[:, f * 128 : (f + 1) * 128] for f in range(4)] + [ids], axis=0)
        out_ref[pl.ds(g * 192, 192), :] = dot(order, stack).astype(BF16)


def expand_matrix(zp):
    e = by24(iota((768, 128), 0))
    return (iota((768, 128), 1) == ((e >> 1) << 3) + zp * 2 + (e & 1)).astype(BF16)


def item_code(n, half):
    r = n - by24(n) * 24
    member = (r * 43) >> 8
    return (r - member * 6 + half * 6 + member * 16).astype(F32)


def index_kernel(own_ref, code_ref, pick_ref):
    core, zp, xy, zb = (lax.axis_index(name) for name in ("group", "zp", ("x", "y"), "zb"))
    expert = iota((128, 128), 0)
    earlier = (expert < iota((128, 128), 1)).astype(BF16)
    expert = expert.astype(F32)
    expand = expand_matrix(zp)
    wanted = item_code(iota((768, 128), 0), core)
    a = iota((16, 48), 0)
    choose = ((iota((16, 48), 1) == zb * 24 + 16 + a) & (a < 8)).astype(F32).astype(BF16)
    for member in range(4):
        pair = pl.ds(pl.multiple_of((xy * 4 + member) * 48, 48), 48)
        ids = dot(choose, own_ref[pair, :])
        named = expert == ids[0:1, :]
        for t in range(1, 8):
            named = named | (expert == ids[t : t + 1, :])
        rank = dot(named.astype(F32).astype(BF16), earlier)
        code = jnp.where(named, rank + 16.0 * member, -1.0)
        code_ref[pl.ds(member * 128, 128), :] = code.T
        found = dot(expand, code.astype(BF16))
        pick_ref[:, pl.ds(member * 128, 128)] = (found == wanted).astype(F32).astype(BF16)


def dispatch_kernel(own_ref, other_ref, pick_ref, send_ref, normed_ref, rest_ref, rows):
    core = lax.axis_index("group")
    zp = lax.axis_index("zp")
    a = iota((256, 384), 0)
    b = iota((256, 384), 1)
    order = (b == (a & 15) * 24 + (a >> 4)).astype(BF16)
    for ref, half in ((own_ref, core), (other_ref, 1 - core)):
        for g in range(8):
            part = dot(order, ref[pl.ds(g * 384, 384), :]).astype(BF16)
            for f in range(4):
                lanes = pl.ds(pl.multiple_of(half * 512 + f * 128, 128), 128)
                for member in range(4):
                    at = (f * 4 + member) * 16
                    rows[pl.ds(member * 128 + g * 16, 16), lanes] = part[at : at + 16]
    for member in range(4):
        at = pl.ds(member * 128, 128)
        value = rows[at, :].astype(F32)
        inverse = lax.rsqrt(jnp.mean(value * value, axis=1, keepdims=True) + 1e-06)
        normed_ref[at, :] = (value * inverse).astype(BF16)
    for part in range(4):
        at = pl.ds(part * 192, 192)
        send_ref[at, :] = dot(pick_ref[at, :], normed_ref[...]).astype(BF16)
    rest_ref[...] = rows[
        pl.ds(pl.multiple_of(zp * 128, 128), 128), pl.ds(pl.multiple_of(core * 512, 512), 512)
    ]


def gate_kernel(normed_ref, router_ref, code_ref, mix0_ref, mix1_ref):
    expand = expand_matrix(lax.axis_index("zp"))
    wanted = [item_code(iota((128, 768), 1), half) for half in (0, 1)]
    for member in range(4):
        at = pl.ds(member * 128, 128)
        code = code_ref[at, :]
        logits = dot(normed_ref[at, :], router_ref[...])
        weights = jnp.where(code >= 0.0, jnp.exp(logits), 0.0)
        gates = weights / jnp.sum(weights, axis=1, keepdims=True)
        found = dot_nt(code.astype(BF16), expand)
        spread = dot_nt(gates.astype(BF16), expand)
        mix0_ref[at, :] = jnp.where(found == wanted[0], spread, 0.0).astype(BF16)
        mix1_ref[at, :] = jnp.where(found == wanted[1], spread, 0.0).astype(BF16)


def hidden_kernel(x_ref, gate_ref, up_ref, out_ref):
    for i in range(3):
        at = pl.ds(i * 256, 256)
        x = x_ref[at, :]
        gate = dot(x, gate_ref[0])
        up = dot(x, up_ref[0])
        out_ref[at, :] = (gate / (1.0 + jnp.exp(-gate)) * up).astype(BF16)


def down_kernel(whose, hidden_ref, down_ref, *refs):
    out_hbm, stage, sems = refs[-3:]
    pair = halves()
    copies = []
    for i in range(3):
        at = pl.ds(i * 256, 256)
        stage[at, :] = dot(hidden_ref[at, :], down_ref[0, :, pair[0]]).astype(BF16)
        copies.append(
            pltpu.make_async_copy(stage.at[at, :], out_hbm.at[at, pair[whose]], sems.at[i])
        )
        copies[-1].start()
    for copy in copies:
        copy.wait()


def mix_kernel(
    mix0_ref, mix1_hbm, back_ref, rest_ref, two_ref, one_ref, three_ref, own_ref, mix1, total, sem
):
    zp = lax.axis_index("zp")
    copy = pltpu.make_async_copy(mix1_hbm, mix1, sem)
    copy.start()
    total[...] = dot(mix0_ref[...], back_ref[:, 0:512])
    copy.wait()
    for k, ref in ((2, two_ref), (1, one_ref), (3, three_ref), (0, own_ref)):
        at = pl.ds(pl.multiple_of(((zp + k) & 3) * 128, 128), 128)
        value = total[at, :] + dot(mix1[at, :], back_ref[:, 512:1024])
        if k == 0:
            value = value + rest_ref[...].astype(F32)
        ref[...] = value.astype(ref.dtype)


def call(kernel, outs, ins, scratch=(), specs=None, out_spec=VMEM, aliases=None):
    return pl.pallas_call(
        kernel,
        out_shape=[jax.ShapeDtypeStruct(shape, dtype) for shape, dtype in outs],
        in_specs=specs or [VMEM] * len(ins),
        out_specs=[out_spec] * len(outs),
        scratch_shapes=list(scratch),
        input_output_aliases=aliases or {},
        compiler_params=PARAMS,
    )(*ins)


def pinned(x):
    return pltpu.with_memory_space_constraint(x, pltpu.HBM)


def around(k):
    return [(i, (i + k) % 4) for i in range(4)]


def body(
    thinker_rows,
    owner_map,
    talker_ids,
    project_weight,
    router_weight,
    expert_gate,
    expert_up,
    expert_down,
):
    give, keep = call(
        project_kernel,
        [((128, 512), F32)] * 2,
        (pinned(thinker_rows), pinned(project_weight)),
        [pltpu.VMEM((128, 1024), BF16), pltpu.VMEM((1024, 1024), BF16), pltpu.SemaphoreType.DMA],
        [VMEM, HBM],
    )
    got = lax.ppermute(give, "group", SWAP)
    (sent,) = call(spread_kernel, [((3072, 128), BF16)], (owner_map, keep, got, talker_ids))
    own = lax.all_to_all(sent.reshape(128, 24, 128), EP, 0, 0, tiled=True)
    other = lax.ppermute(own, "group", SWAP)
    code, pick = call(
        index_kernel, [((512, 128), F32), ((768, 512), BF16)], (own.reshape(3072, 128),)
    )
    send, normed, rest = call(
        dispatch_kernel,
        [((768, 1024), BF16), ((512, 1024), BF16), ((128, 512), BF16)],
        (own.reshape(3072, 128), other.reshape(3072, 128), pick),
        [pltpu.VMEM((512, 1024), BF16)],
    )
    items = lax.all_to_all(send.reshape(32, 24, 1024), REGION, 0, 0, tiled=True)
    mix0, mix1 = call(gate_kernel, [((512, 768), BF16)] * 2, (normed, router_weight, code))
    (hidden,) = call(
        hidden_kernel,
        [((768, 384), BF16)],
        (items.reshape(768, 1024), expert_gate, expert_up),
    )
    other_hidden = lax.ppermute(hidden, "group", SWAP)
    down = functools.partial(
        call,
        outs=[((768, 1024), BF16)],
        scratch=[pltpu.VMEM((768, 512), BF16), pltpu.SemaphoreType.DMA((3,))],
        out_spec=HBM,
    )
    (expert_out,) = down(functools.partial(down_kernel, 0), ins=(hidden, expert_down))
    (expert_out,) = down(
        functools.partial(down_kernel, 1),
        ins=(other_hidden, expert_down, expert_out),
        specs=[VMEM, VMEM, HBM],
        aliases={2: 0},
    )
    back = lax.all_to_all(expert_out.reshape(32, 24, 1024), REGION, 0, 0, tiled=True)
    two, one, three, total = call(
        mix_kernel,
        [((128, 512), BF16)] * 3 + [((128, 512), F32)],
        (mix0, pinned(mix1), back.reshape(768, 1024), rest),
        [pltpu.VMEM((512, 768), BF16), pltpu.VMEM((512, 512), F32), pltpu.SemaphoreType.DMA],
        [VMEM, HBM, VMEM, VMEM],
    )
    for k, part in ((2, two), (1, one), (3, three)):
        total = total + lax.ppermute(part, "zp", around(k)).astype(F32)
    return total.astype(BF16)


def solution(mesh):
    ep = ("x", "y", "zp", "zb")
    split = Mesh(mesh.devices.reshape(2, 4, 4, 4, 2), ("group",) + ep)
    return jax.shard_map(
        body,
        mesh=split,
        in_specs=(
            P(ep, "group"),
            P(ep, None),
            P(ep, None),
            P("group", None),
            P(),
            P(ep, None, None),
            P(ep, None, None),
            P(ep, None, None),
        ),
        out_specs=P(ep, "group"),
        check_vma=False,
    )
```

time: 140 us -> 133 us (0.950)
  local copies, waits for them, and re-layouts: 6.69 us -> 3 us
  Pallas kernels: 18.4 us -> 15.2 us
    unnamed x26 -> x20, local copies, waits for them, and re-layouts: 6.69 us -> 3 us
    pallas_call x1 -> x0, Pallas kernels: 2.33 us -> none  [body(): pl.pallas_call(hidden_kernel, grid=(4,), out_shape=jax.ShapeDtypeStruct((...]
    pallas_call x7 -> x9, Pallas kernels: 16 us -> 15.2 us  [call(): pl.pallas_call(kernel, out_shape=[jax.ShapeDtypeStruct(shape, dtype) for...]
where the time goes in v3:
time: 133 us; the launch traced here: 132 us
  blocking collectives  64.8 us (49%)
  waiting for transfers between devices  32.1 us (24%)
  starting transfers between devices  16.2 us (12%)
  Pallas kernels  15.2 us (11%)
  local copies, waits for them, and re-layouts  3 us (2%)
    all_to_all x1, blocking collectives, body(): own = lax.all_to_all(sent.reshape(128, 24, 128), EP, 0, 0, tiled=True)  38.6 us
    all_to_all x1, blocking collectives, body(): items = lax.all_to_all(send.reshape(32, 24, 1024), REGION, 0, 0, tiled=True)  26.2 us
    all_to_all x1, waiting for transfers between devices, body(): lax.all_to_all(expert_out.reshape(32, 24, 1024), REGION, 0, 0, tiled=True)  20.6 us
    pallas_call x9, Pallas kernels, call(): pl.pallas_call(kernel, out_shape=[jax.ShapeDtypeStruct(shape, dtype) for...  15.2 us
    ppermute x3, waiting for transfers between devices, body(): total = total + lax.ppermute(part, 'zp', around(k)).astype(F32)  9.56 us
    ppermute x3, starting transfers between devices, body(): total = total + lax.ppermute(part, 'zp', around(k)).astype(F32)  4.88 us
    all_to_all x1, starting transfers between devices, body(): lax.all_to_all(expert_out.reshape(32, 24, 1024), REGION, 0, 0, tiled=True)  3.98 us
    ppermute x1, starting transfers between devices, body(): got = lax.ppermute(give, 'group', SWAP)  3.32 us
  transfers between devices with their start and end apart: 7, of which 7 were waited for; matrix products, arithmetic and copies ran while one was open for 0% of the time, Pallas kernels for 3%

profile of v3, /device:TPU:1, one launch (start us, length us, event | category | flops | bytes accessed | tf_op | source)
XLA Modules:
  0.0 132.1 jit_solution(15767235012335575899)
XLA Ops:
  0.0 0.0 copy-start.8
  0.0 0.0 copy-start.7
  0.0 3.0 %shard_map.82 = (f32[128,512]{1,0:T(8,128)S(1)}, f32[128,512]{1,0:T(8,128)S(1)}) custom-call(bf16[128,1024]{1,0:T(8,128)(2,1)} %x_ref.1, bf16[1024,1024]{1,0:T(8,128)(2,1)} %w_hbm.1), custom_call_target="tpu_custom_call" | custom-call | tf_op jit(solution)/shard_map/pallas_call | solution.py:230
  3.1 3.3 %collective-permute-start = (f32[128,512]{1,0:T(8,128)S(1)}, f32[128,512]{1,0:T(8,128)S(1)}, u32[]{:S(2)}, u32[]{:S(2)}) collective-permute-start(f32[128,512]{1,0:T(8,128)S(1)} %get-tuple-element.19), channel_id=1, source_target_pairs={{0,128},{128,0},{1,129},{129,1},{2,130},{130,2},{3,131},{131,3},{4... | collective-permute-start | bytes 786440 | tf_op jit(solution)/shard_map/ppermute | solution.py:266
  6.4 0.0 copy-done.8
  6.4 0.1 copy.10.owner_ref
  6.5 0.0 copy-done.7
  6.5 0.1 copy.11.ids_ref
  6.6 0.9 collective-permute-done.got_ref
  7.5 1.0 shard_map.83
  8.5 38.6 %all_to_all.15 = bf16[128,24,128]{2,1,0:T(8,128)(2,1)S(1)} all-to-all(bf16[128,24,128]{2,1,0:T(8,128)(2,1)S(1)} %bitcast.11), channel_id=1, replica_groups=mesh['group'=2,'x'=4,'y'=4,'zp'=4,'zb'=2] {'x','y','zp','zb'}, dimensions={0} | all-to-all | bytes 1572864 | tf_op jit(solution)/shard_map/all_to_all | solution.py:268
  47.1 2.2 %collective-permute-start.1 = (bf16[128,24,128]{2,1,0:T(8,128)(2,1)S(1)}, bf16[128,24,128]{2,1,0:T(8,128)(2,1)S(1)}, u32[]{:S(2)}, u32[]{:S(2)}) collective-permute-start(bf16[128,24,128]{2,1,0:T(8,128)(2,1)S(1)} %all_to_all.15), channel_id=1, source_target_pairs={{0,128},{128,0},{1,129},{129,1},{2,130},{130,2},{3,131},{131,3},{4... | collective-permute-start | bytes 2359304 | tf_op jit(solution)/shard_map/ppermute | solution.py:269
  49.3 1.2 shard_map.84
  50.5 0.0 copy-start.5
  50.5 0.7 collective-permute-done.1
  51.2 2.3 %shard_map.85 = (bf16[768,1024]{1,0:T(8,128)(2,1)S(1)}, bf16[512,1024]{1,0:T(8,128)(2,1)S(1)}, bf16[128,512]{1,0:T(8,128)(2,1)S(1)}) custom-call(bf16[3072,128]{1,0:T(8,128)(2,1)S(1)} %bitcast.8, bf16[3072,128]{1,0:T(8,128)(2,1)S(1)} %bitcast.13, bf16[768,512]{1,0:T(8,128)(2,1)S(1)} %get-tuple-element.20.pick_ref), custom_call_target="tpu_custom_call" | custom-call | tf_op jit(solution)/shard_map/pallas_call | solution.py:230
  53.5 0.0 copy-done.5
  53.5 0.0 copy-start.1
  53.5 0.0 copy-start.2
  53.6 26.2 %all_to_all.16 = bf16[32,24,1024]{2,1,0:T(8,128)(2,1)S(1)} all-to-all(bf16[32,24,1024]{2,1,0:T(8,128)(2,1)S(1)} %bitcast.12), channel_id=1, replica_groups=mesh['group'=2,'x'=4,'y'=4,'zp'=4,'zb'=2] {'x','y','zb'}, dimensions={0} | all-to-all | bytes 3145728 | tf_op jit(solution)/shard_map/all_to_all | solution.py:279
  79.7 0.0 copy-done.1
  79.7 0.0 copy-done.2
  79.7 0.0 copy-start
  79.7 1.8 %shard_map.87.hidden_ref = bf16[768,384]{1,0:T(8,128)(2,1)S(1)} custom-call(bf16[768,1024]{1,0:T(8,128)(2,1)S(1)} %bitcast.10, bf16[1,1024,384]{2,1,0:T(8,128)(2,1)S(1)} %copy-done.1, bf16[1,1024,384]{2,1,0:T(8,128)(2,1)S(1)} %copy-done.2), custom_call_target="tpu_custom_call" | custom-call | tf_op jit(solution)/shard_map/pallas_call | solution.py:230
  81.5 1.8 %collective-permute-start.2 = (bf16[768,384]{1,0:T(8,128)(2,1)S(1)}, bf16[768,384]{1,0:T(8,128)(2,1)S(1)}, u32[]{:S(2)}, u32[]{:S(2)}) collective-permute-start(bf16[768,384]{1,0:T(8,128)(2,1)S(1)} %shard_map.87.hidden_ref), channel_id=1, source_target_pairs={{0,128},{128,0},{1,129},{129,1},{2,130},{130,2},{3,131},{131,3},{4... | collective-permute-start | bytes 1769480 | tf_op jit(solution)/shard_map/ppermute | solution.py:286
  83.3 0.0 copy-done
  83.3 1.3 %shard_map.88.refs_0_ = bf16[768,1024]{1,0:T(8,128)(2,1)} custom-call(bf16[768,384]{1,0:T(8,128)(2,1)S(1)} %shard_map.87.hidden_ref, bf16[1,384,1024]{2,1,0:T(8,128)(2,1)S(1)} %copy-done), custom_call_target="tpu_custom_call" | custom-call | tf_op jit(solution)/shard_map/pallas_call | solution.py:230
  84.7 0.3 collective-permute-done.2.hidden_ref
  84.9 1.3 %shard_map.89 = bf16[768,1024]{1,0:T(8,128)(2,1)} custom-call(bf16[768,384]{1,0:T(8,128)(2,1)S(1)} %collective-permute-done.2.hidden_ref, bf16[1,384,1024]{2,1,0:T(8,128)(2,1)S(1)} %copy-done, bf16[768,1024]{1,0:T(8,128)(2,1)} %shard_map.88.refs_0_), custom_call_target="tpu_custom_call", output_to_operand_aliasing={{}: (2, {})} | custom-call | tf_op jit(solution)/shard_map/pallas_call | solution.py:230
  86.3 4.0 %all-to-all-start.2 = ((bf16[32,24,1024]{2,1,0:T(8,128)(2,1)}), bf16[32,24,1024]{2,1,0:T(8,128)(2,1)S(1)}, u32[]{:S(2)}, u32[]{:S(2)}) async-start(bf16[32,24,1024]{2,1,0:T(8,128)(2,1)} %bitcast.5), calls=%async_computation.2 | async-start | bytes 3145728 | tf_op jit(solution)/shard_map/all_to_all | solution.py:300
  90.3 0.0 copy-start.4
  90.3 0.9 copy-done.4
  91.2 0.0 copy-start.6
  91.2 0.9 copy-done.6
  92.2 1.6 %shard_map.86 = (bf16[512,768]{1,0:T(8,128)(2,1)S(1)}, bf16[512,768]{1,0:T(8,128)(2,1)S(1)}) custom-call(bf16[512,1024]{1,0:T(8,128)(2,1)S(1)} %get-tuple-element.21.normed_ref, bf16[1024,128]{1,0:T(8,128)(2,1)S(1)} %copy-done.4, f32[512,128]{1,0:T(8,128)S(1)} %copy-done.6), custom_call_target="tpu_custom_call" | custom-call | tf_op jit(solution)/shard_map/pallas_call | solution.py:230
  93.7 0.0 copy-start.3
  93.7 0.9 copy-done.3
  94.6 20.6 %all-to-all-done.2 = bf16[32,24,1024]{2,1,0:T(8,128)(2,1)S(1)} async-done(((bf16[32,24,1024]{2,1,0:T(8,128)(2,1)}), bf16[32,24,1024]{2,1,0:T(8,128)(2,1)S(1)}, u32[]{:S(2)}, u32[]{:S(2)}) %all-to-all-start.2) | async-done | bytes 1572896 | tf_op jit(solution)/shard_map/all_to_all | solution.py:300
  115.2 1.7 %shard_map.90 = (bf16[128,512]{1,0:T(8,128)(2,1)S(1)}, bf16[128,512]{1,0:T(8,128)(2,1)S(1)}, bf16[128,512]{1,0:T(8,128)(2,1)S(1)}, f32[128,512]{1,0:T(8,128)S(1)}) custom-call(bf16[512,768]{1,0:T(8,128)(2,1)S(1)} %get-tuple-element.23.mix0_ref, bf16[512,768]{1,0:T(8,128)(2,1)} %copy-done.3, bf16[768,1024]{1,0:T(8,128)(2,1)S(1)} %bitcast.9, ...), custom_call_target="tpu_custom_call" | custom-call | tf_op jit(solution)/shard_map/pallas_call | solution.py:230
  116.9 1.3 collective-permute-start.3
  118.2 1.4 %collective-permute-start.4 = (bf16[128,512]{1,0:T(8,128)(2,1)S(1)}, bf16[128,512]{1,0:T(8,128)(2,1)S(1)}, u32[]{:S(2)}, u32[]{:S(2)}) collective-permute-start(bf16[128,512]{1,0:T(8,128)(2,1)S(1)} %get-tuple-element.29), channel_id=1, source_target_pairs={{0,2},{2,4},{4,6},{6,0},{1,3},{3,5},{5,7},{7,1},{8,10},{10,12},{12... | collective-permute-start | bytes 393224 | tf_op jit(solution)/shard_map/ppermute | solution.py:309
  119.7 2.2 %collective-permute-start.5 = (bf16[128,512]{1,0:T(8,128)(2,1)S(1)}, bf16[128,512]{1,0:T(8,128)(2,1)S(1)}, u32[]{:S(2)}, u32[]{:S(2)}) collective-permute-start(bf16[128,512]{1,0:T(8,128)(2,1)S(1)} %get-tuple-element.30), channel_id=1, source_target_pairs={{0,6},{2,0},{4,2},{6,4},{1,7},{3,1},{5,3},{7,5},{8,14},{10,8},{12,... | collective-permute-start | bytes 393224 | tf_op jit(solution)/shard_map/ppermute | solution.py:309
  121.8 6.5 %collective-permute-done.3 = bf16[128,512]{1,0:T(8,128)(2,1)S(1)} collective-permute-done((bf16[128,512]{1,0:T(8,128)(2,1)S(1)}, bf16[128,512]{1,0:T(8,128)(2,1)S(1)}, u32[]{:S(2)}, u32[]{:S(2)}) %collective-permute-start.3) | collective-permute-done | bytes 131104 | tf_op jit(solution)/shard_map/ppermute | solution.py:309
  128.4 1.9 %collective-permute-done.4 = bf16[128,512]{1,0:T(8,128)(2,1)S(1)} collective-permute-done((bf16[128,512]{1,0:T(8,128)(2,1)S(1)}, bf16[128,512]{1,0:T(8,128)(2,1)S(1)}, u32[]{:S(2)}, u32[]{:S(2)}) %collective-permute-start.4) | collective-permute-done | bytes 131104 | tf_op jit(solution)/shard_map/ppermute | solution.py:309
  130.3 1.1 collective-permute-done.5
  131.4 0.7 add_convert_fusion
Async XLA Ops:
  0.0 6.4 %copy-start.8 = (s32[128,1]{0,1:T(1,128)S(1)}, s32[128,1]{0,1:T(1,128)}, u32[]{:S(2)}) copy-start(s32[128,1]{0,1:T(1,128)} %param.9) | copy-start | bytes 1540
  0.0 6.5 %copy-start.7 = (s32[128,8]{0,1:T(8,128)S(1)}, s32[128,8]{0,1:T(8,128)}, u32[]{:S(2)}) copy-start(s32[128,8]{0,1:T(8,128)} %param.10) | copy-start | bytes 12292
  3.1 4.5 %collective-permute-start = (f32[128,512]{1,0:T(8,128)S(1)}, f32[128,512]{1,0:T(8,128)S(1)}, u32[]{:S(2)}, u32[]{:S(2)}) collective-permute-start(f32[128,512]{1,0:T(8,128)S(1)} %get-tuple-element.19), channel_id=1, source_target_pairs={{0,128},{128,0},{1,129},{129,1},{2,130},{130,2},{3,131},{131,3},{4... | collective-permute-start | bytes 786440 | tf_op jit(solution)/shard_map/ppermute | solution.py:266
  47.1 4.1 %collective-permute-start.1 = (bf16[128,24,128]{2,1,0:T(8,128)(2,1)S(1)}, bf16[128,24,128]{2,1,0:T(8,128)(2,1)S(1)}, u32[]{:S(2)}, u32[]{:S(2)}) collective-permute-start(bf16[128,24,128]{2,1,0:T(8,128)(2,1)S(1)} %all_to_all.15), channel_id=1, source_target_pairs={{0,128},{128,0},{1,129},{129,1},{2,130},{130,2},{3,131},{131,3},{4... | collective-permute-start | bytes 2359304 | tf_op jit(solution)/shard_map/ppermute | solution.py:269
  50.5 3.0 %copy-start.5 = (f32[512,128]{1,0:T(8,128)}, f32[512,128]{1,0:T(8,128)S(1)}, u32[]{:S(2)}) copy-start(f32[512,128]{1,0:T(8,128)S(1)} %get-tuple-element.22.code_ref) | copy-start | bytes 786436
  53.5 26.2 %copy-start.1 = (bf16[1,1024,384]{2,1,0:T(8,128)(2,1)S(1)}, bf16[1,1024,384]{2,1,0:T(8,128)(2,1)}, u32[]{:S(2)}) copy-start(bf16[1,1024,384]{2,1,0:T(8,128)(2,1)} %gate_ref.1) | copy-start | bytes 2359300
  53.5 26.2 %copy-start.2 = (bf16[1,1024,384]{2,1,0:T(8,128)(2,1)S(1)}, bf16[1,1024,384]{2,1,0:T(8,128)(2,1)}, u32[]{:S(2)}) copy-start(bf16[1,1024,384]{2,1,0:T(8,128)(2,1)} %up_ref.1) | copy-start | bytes 2359300
  79.7 3.6 %copy-start = (bf16[1,384,1024]{2,1,0:T(8,128)(2,1)S(1)}, bf16[1,384,1024]{2,1,0:T(8,128)(2,1)}, u32[]{:S(2)}) copy-start(bf16[1,384,1024]{2,1,0:T(8,128)(2,1)} %down_ref.3) | copy-start | bytes 2359300
  81.5 3.4 %collective-permute-start.2 = (bf16[768,384]{1,0:T(8,128)(2,1)S(1)}, bf16[768,384]{1,0:T(8,128)(2,1)S(1)}, u32[]{:S(2)}, u32[]{:S(2)}) collective-permute-start(bf16[768,384]{1,0:T(8,128)(2,1)S(1)} %shard_map.87.hidden_ref), channel_id=1, source_target_pairs={{0,128},{128,0},{1,129},{129,1},{2,130},{130,2},{3,131},{131,3},{4... | collective-permute-start | bytes 1769480 | tf_op jit(solution)/shard_map/ppermute | solution.py:286
  86.3 28.9 %all-to-all-start.2 = ((bf16[32,24,1024]{2,1,0:T(8,128)(2,1)}), bf16[32,24,1024]{2,1,0:T(8,128)(2,1)S(1)}, u32[]{:S(2)}, u32[]{:S(2)}) async-start(bf16[32,24,1024]{2,1,0:T(8,128)(2,1)} %bitcast.5), calls=%async_computation.2 | async-start | bytes 3145728 | tf_op jit(solution)/shard_map/all_to_all | solution.py:300
  90.3 1.0 copy-start.4
  91.2 0.9 copy-start.6
  93.7 0.9 copy-start.3
  116.9 11.4 %collective-permute-start.3 = (bf16[128,512]{1,0:T(8,128)(2,1)S(1)}, bf16[128,512]{1,0:T(8,128)(2,1)S(1)}, u32[]{:S(2)}, u32[]{:S(2)}) collective-permute-start(bf16[128,512]{1,0:T(8,128)(2,1)S(1)} %get-tuple-element.28), channel_id=1, source_target_pairs={{0,4},{2,6},{4,0},{6,2},{1,5},{3,7},{5,1},{7,3},{8,12},{10,14},{12... | collective-permute-start | bytes 393224 | tf_op jit(solution)/shard_map/ppermute | solution.py:309
  118.2 12.0 %collective-permute-start.4 = (bf16[128,512]{1,0:T(8,128)(2,1)S(1)}, bf16[128,512]{1,0:T(8,128)(2,1)S(1)}, u32[]{:S(2)}, u32[]{:S(2)}) collective-permute-start(bf16[128,512]{1,0:T(8,128)(2,1)S(1)} %get-tuple-element.29), channel_id=1, source_target_pairs={{0,2},{2,4},{4,6},{6,0},{1,3},{3,5},{5,7},{7,1},{8,10},{10,12},{12... | collective-permute-start | bytes 393224 | tf_op jit(solution)/shard_map/ppermute | solution.py:309
  119.7 11.7 %collective-permute-start.5 = (bf16[128,512]{1,0:T(8,128)(2,1)S(1)}, bf16[128,512]{1,0:T(8,128)(2,1)S(1)}, u32[]{:S(2)}, u32[]{:S(2)}) collective-permute-start(bf16[128,512]{1,0:T(8,128)(2,1)S(1)} %get-tuple-element.30), channel_id=1, source_target_pairs={{0,6},{2,0},{4,2},{6,4},{1,7},{3,1},{5,3},{7,5},{8,14},{10,8},{12,... | collective-permute-start | bytes 393224 | tf_op jit(solution)/shard_map/ppermute | solution.py:309

commit v4 on v3

v4 whole, which is shorter than its diff:
```python
import functools

import jax
import jax.numpy as jnp
from jax import lax
from jax.experimental import pallas as pl
from jax.experimental.pallas import tpu as pltpu
from jax.sharding import Mesh
from jax.sharding import PartitionSpec as P

F32 = jnp.float32
BF16 = jnp.bfloat16
I32 = jnp.int32
EP = ("x", "y", "zp", "zb")
REGION = ("x", "y", "zb")
SWAP = [(0, 1), (1, 0)]
VMEM = pl.BlockSpec(memory_space=pltpu.VMEM)
HBM = pl.BlockSpec(memory_space=pltpu.HBM)
PARAMS = pltpu.CompilerParams(vmem_limit_bytes=16 * 1024 * 1024)


def iota(shape, dim):
    return lax.broadcasted_iota(I32, shape, dim)


def dot(a, b):
    return jnp.dot(a, b, preferred_element_type=F32)


def dot_nt(a, b):
    return lax.dot_general(a, b, (((1,), (1,)), ((), ())), preferred_element_type=F32)


def dot_tn(a, b):
    return lax.dot_general(a, b, (((0,), (0,)), ((), ())), preferred_element_type=F32)


def quantize(x_ref, out_ref):
    rows = x_ref.shape[0]
    r = iota((128, 128), 0)
    lane = iota((128, 128), 1)
    compact = jnp.zeros((rows, 128), F32)
    for b in range(8):
        largest = jnp.abs(x_ref[:, pl.ds(b * 128, 128)].astype(F32))
        for step in (16, 8, 4, 2, 1):
            largest = jnp.maximum(largest, pltpu.roll(largest, 128 - step, 1))
        first = (lane == r + b) & ((r & 31) == 0)
        compact = compact + dot(largest.astype(BF16), first.astype(F32).astype(BF16))
    power = jnp.full(compact.shape, 2.0**-31, F32)
    inverse = jnp.full(compact.shape, 2.0**31, F32)
    for step in (32, 16, 8, 4, 2, 1):
        larger = power * 2.0**step
        below = larger * 448.0 < compact
        power = jnp.where(below, larger, power)
        inverse = jnp.where(below, inverse * 2.0**-step, inverse)
    spacing = (jnp.minimum(power * 2.0, 16.0) * 2.0**-9).astype(BF16)
    inverse = (jnp.maximum(inverse * 0.5, 0.0625) * 2.0**9).astype(BF16)
    for b in range(8):
        lanes = pl.ds(b * 128, 128)
        spread = (r == (lane & 96) + b).astype(F32).astype(BF16)
        x = x_ref[:, lanes].astype(F32)
        size = jnp.abs(x) * 0.125
        level = dot(spacing, spread)
        over = dot(inverse, spread)
        for step in (8, 4, 2, 1):
            larger = level * 2.0**step
            reached = larger <= size
            level = jnp.where(reached, larger, level)
            over = jnp.where(reached, over * 2.0**-step, over)
        out_ref[:, lanes] = (jnp.floor(x * over + 0.5) * level).astype(BF16)


def halves():
    core = lax.axis_index("group")
    mine = pl.ds(pl.multiple_of(core * 512, 512), 512)
    other = pl.ds(pl.multiple_of((1 - core) * 512, 512), 512)
    return mine, other


def project_kernel(x_ref, w_hbm, give_ref, keep_ref, restored, weight, sem):
    copy = pltpu.make_async_copy(w_hbm, weight, sem)
    copy.start()
    quantize(x_ref, restored)
    copy.wait()
    mine, other = halves()
    give_ref[...] = dot(restored[...], weight[:, other])
    keep_ref[...] = dot(restored[...], weight[:, mine])


def by24(n):
    return (n * 2731) >> 16


def prepare_kernel(owner_ref, ids_ref, chosen_ref, ids_out_ref, order_ref):
    n = iota((128, 512), 1)
    e = n >> 2
    wanted = ((((e >> 3) << 2) + (n & 3)) << 1) + (e & 1)
    chosen_ref[...] = (owner_ref[...] == wanted).astype(F32).T.astype(BF16)
    a = iota((16, 8), 0)
    part = (iota((16, 8), 1) == a + lax.axis_index("group") * 4) & (a < 4)
    ids = dot_nt(part.astype(F32).astype(BF16), ids_ref[...].astype(F32).astype(BF16))
    ids_out_ref[...] = ids.astype(BF16)
    a = iota((160, 144), 0)
    e = (a * 3277) >> 16
    i = a - e * 20
    source = jnp.where(i < 16, ((i >> 2) << 5) + (e << 2) + (i & 3), 112 + i)
    order_ref[...] = (iota((160, 144), 1) == source).astype(F32).astype(BF16)


def spread_kernel(keep_ref, got_ref, chosen_ref, ids_ref, order_ref, out_ref):
    projected = (keep_ref[...] + got_ref[...]).astype(BF16)
    rows = dot(chosen_ref[...], projected).astype(BF16)
    ids = ids_ref[...]
    order = order_ref[...]
    for g in range(16):
        part = rows[g * 32 : (g + 1) * 32]
        stack = jnp.concatenate([part[:, f * 128 : (f + 1) * 128] for f in range(4)] + [ids], axis=0)
        out_ref[pl.ds(g * 160, 160), :] = dot(order, stack).astype(BF16)


def expand_matrix(zp):
    e = by24(iota((768, 128), 0))
    return (iota((768, 128), 1) == ((e >> 1) << 3) + zp * 2 + (e & 1)).astype(BF16)


def item_code(n, half):
    r = n - by24(n) * 24
    member = (r * 43) >> 8
    return (r - member * 6 + half * 6 + member * 16).astype(F32)


def arrange(ref, rows, at, order):
    for g in range(8):
        part = dot(order, ref[pl.ds(g * 320, 320), :]).astype(BF16)
        for f in range(4):
            lanes = pl.ds(pl.multiple_of(at + f * 128, 128), 128)
            for member in range(4):
                first = (f * 4 + member) * 16
                rows[pl.ds(member * 128 + g * 16, 16), lanes] = part[first : first + 16]


def arrange_kernel(own_ref, rows_ref, order_ref, expand_ref):
    a = iota((256, 320), 0)
    order = (iota((256, 320), 1) == (a & 15) * 20 + (a >> 4)).astype(F32).astype(BF16)
    order_ref[...] = order
    expand_ref[:, 0:128] = expand_matrix(lax.axis_index("zp"))
    taken = item_code(iota((768, 128), 0), lax.axis_index("group"))
    expand_ref[:, 128:256] = jnp.where(iota((768, 128), 1) == 0, -taken, 0.0).astype(BF16)
    arrange(own_ref, rows_ref, 0, order)


def find_items(own_ref, other_ref, expand_ref, code_ref, pick):
    xy, zb = lax.axis_index(("x", "y")), lax.axis_index("zb")
    expert = iota((128, 128), 0)
    earlier = (expert < iota((128, 128), 1)).astype(F32).astype(BF16)
    expert = expert.astype(F32)
    a = iota((16, 160), 0)
    line = pl.ds(pl.multiple_of(xy * 160, 160), 160)
    choose = (iota((16, 160), 1) == (a >> 2) * 40 + zb * 20 + 16 + (a & 3)).astype(F32).astype(BF16)
    first = dot(choose, own_ref[line, :])
    second = dot(choose, other_ref[line, :])
    expand = expand_ref[...]
    ones = jnp.ones((128, 128), BF16)
    for member in range(4):
        named = expert == first[member * 4 : member * 4 + 1, :]
        for t in range(1, 4):
            named = named | (expert == first[member * 4 + t : member * 4 + t + 1, :])
        for t in range(4):
            named = named | (expert == second[member * 4 + t : member * 4 + t + 1, :])
        rank = dot(named.astype(F32).astype(BF16), earlier)
        code = jnp.where(named, rank + 16.0 * member, -1.0)
        code_ref[pl.ds(member * 128, 128), 1024:1152] = code.T.astype(BF16)
        found = dot(expand, jnp.concatenate([code.astype(BF16), ones], axis=0))
        pick[:, pl.ds(member * 128, 128)] = (found == 0.0).astype(F32).astype(BF16)


def dispatch_kernel(
    own_ref, other_ref, mine_ref, order_ref, expand_ref, send_ref, normed_ref, rows, pick
):
    zp = lax.axis_index("zp")
    mine, other = halves()
    find_items(own_ref, other_ref, expand_ref, normed_ref, pick)
    rows[:, mine] = mine_ref[...]
    arrange(other_ref, rows, (1 - lax.axis_index("group")) * 512, order_ref[...])
    for member in range(4):
        at = pl.ds(member * 128, 128)
        value = rows[at, :].astype(F32)
        inverse = lax.rsqrt(jnp.mean(value * value, axis=1, keepdims=True) + 1e-06)
        normed_ref[at, 0:1024] = (value * inverse).astype(BF16)
    for part in range(2):
        at = pl.ds(part * 384, 384)
        send_ref[at, :] = dot(pick[at, :], normed_ref[0:512, 0:1024]).astype(BF16)
    normed_ref[512:640, 0:512] = mine_ref[pl.ds(pl.multiple_of(zp * 128, 128), 128), :]


def gate_kernel(normed_ref, router_ref, mix_ref):
    mix_ref[512:640, 0:512] = normed_ref[512:640, 0:512]
    expand = expand_matrix(lax.axis_index("zp"))
    wanted = [item_code(iota((128, 768), 1), half) for half in (0, 1)]
    for member in range(4):
        at = pl.ds(member * 128, 128)
        code = normed_ref[at, 1024:1152]
        logits = dot(normed_ref[at, 0:1024], router_ref[...])
        weights = jnp.where(code.astype(F32) >= 0.0, jnp.exp(logits), 0.0)
        gates = weights / jnp.sum(weights, axis=1, keepdims=True)
        found = dot_nt(code, expand)
        spread = dot_nt(gates.astype(BF16), expand)
        mix_ref[at, 0:768] = jnp.where(found == wanted[0], spread, 0.0).astype(BF16)
        mix_ref[at, 768:1536] = jnp.where(found == wanted[1], spread, 0.0).astype(BF16)


def hidden_kernel(x_ref, gate_ref, up_ref, out_ref):
    x = x_ref[...]

    def act(gate, up):
        return (gate / (1.0 + jnp.exp(-gate)) * up).astype(BF16)

    out_ref[:, 0:256] = act(dot(x, gate_ref[0, :, 0:256]), dot(x, up_ref[0, :, 0:256]))
    last = jnp.concatenate([gate_ref[0, :, 256:384], up_ref[0, :, 256:384]], axis=1)
    both = dot(x, last)
    out_ref[:, 256:384] = act(both[:, 0:128], both[:, 128:256])


def down_kernel(whose, hidden_ref, down_ref, *refs):
    out_hbm, stage, sems = refs[-3:]
    pair = halves()
    copies = []
    for i in range(2):
        at = pl.ds(i * 384, 384)
        stage[at, :] = dot(hidden_ref[at, :], down_ref[0, :, pair[0]]).astype(BF16)
        for j in range(2):
            at = pl.ds(i * 384 + j * 192, 192)
            copies.append(
                pltpu.make_async_copy(
                    stage.at[at, :], out_hbm.at[at, pair[whose]], sems.at[i * 2 + j]
                )
            )
            copies[-1].start()
    for copy in copies:
        copy.wait()


def mix_kernel(mix_ref, back_ref, two_ref, one_ref, three_ref, own_ref, total):
    zp = lax.axis_index("zp")
    items = jnp.concatenate([back_ref[:, 0:512], back_ref[:, 512:1024]], axis=0)
    total[...] = dot(mix_ref[0:512, :], items)
    for k, ref in ((2, two_ref), (1, one_ref), (3, three_ref), (0, own_ref)):
        value = total[pl.ds(pl.multiple_of(((zp + k) & 3) * 128, 128), 128), :]
        if k == 0:
            value = value + mix_ref[512:640, 0:512].astype(F32)
        ref[...] = value.astype(ref.dtype)


def call(kernel, outs, ins, scratch=(), specs=None, out_spec=VMEM, aliases=None):
    return pl.pallas_call(
        kernel,
        out_shape=[jax.ShapeDtypeStruct(shape, dtype) for shape, dtype in outs],
        in_specs=specs or [VMEM] * len(ins),
        out_specs=[out_spec] * len(outs),
        scratch_shapes=list(scratch),
        input_output_aliases=aliases or {},
        compiler_params=PARAMS,
    )(*ins)


def pinned(x):
    return pltpu.with_memory_space_constraint(x, pltpu.HBM)


def around(k):
    return [(i, (i + k) % 4) for i in range(4)]


def body(
    thinker_rows,
    owner_map,
    talker_ids,
    project_weight,
    router_weight,
    expert_gate,
    expert_up,
    expert_down,
):
    give, keep = call(
        project_kernel,
        [((128, 512), F32)] * 2,
        (pinned(thinker_rows), pinned(project_weight)),
        [pltpu.VMEM((128, 1024), BF16), pltpu.VMEM((1024, 1024), BF16), pltpu.SemaphoreType.DMA],
        [VMEM, HBM],
    )
    got = lax.ppermute(give, "group", SWAP)
    chosen, ids, order = call(
        prepare_kernel,
        [((512, 128), BF16), ((16, 128), BF16), ((160, 144), BF16)],
        (owner_map, talker_ids),
    )
    (sent,) = call(spread_kernel, [((2560, 128), BF16)], (keep, got, chosen, ids, order))
    own = lax.all_to_all(sent.reshape(128, 5, 4, 128), EP, 0, 0, tiled=True)
    other = lax.ppermute(own, "group", SWAP).reshape(2560, 128)
    own = own.reshape(2560, 128)
    mine, order, expand = call(
        arrange_kernel,
        [((512, 512), BF16), ((256, 320), BF16), ((768, 256), BF16)],
        (own,),
    )
    send, normed = call(
        dispatch_kernel,
        [((768, 1024), BF16), ((640, 1152), BF16)],
        (own, other, mine, order, expand),
        [pltpu.VMEM((512, 1024), BF16), pltpu.VMEM((768, 512), BF16)],
    )
    items = lax.all_to_all(send.reshape(32, 24, 1024), REGION, 0, 0, tiled=True)
    (mix,) = call(gate_kernel, [((640, 1536), BF16)], (normed, router_weight))
    (hidden,) = call(
        hidden_kernel,
        [((768, 384), BF16)],
        (items.reshape(768, 1024), expert_gate, expert_up),
    )
    other_hidden = lax.ppermute(hidden, "group", SWAP)
    down = functools.partial(
        call,
        outs=[((768, 1024), BF16)],
        scratch=[pltpu.VMEM((768, 512), BF16), pltpu.SemaphoreType.DMA((4,))],
        out_spec=HBM,
    )
    (expert_out,) = down(functools.partial(down_kernel, 0), ins=(hidden, expert_down))
    (expert_out,) = down(
        functools.partial(down_kernel, 1),
        ins=(other_hidden, expert_down, expert_out),
        specs=[VMEM, VMEM, HBM],
        aliases={2: 0},
    )
    back = lax.all_to_all(expert_out.reshape(32, 24, 1024), REGION, 0, 0, tiled=True)
    two, one, three, total = call(
        mix_kernel,
        [((128, 512), BF16)] * 3 + [((128, 512), F32)],
        (mix, back.reshape(768, 1024)),
        [pltpu.VMEM((512, 512), F32)],
    )
    for k, part in ((2, two), (1, one), (3, three)):
        total = total + lax.ppermute(part, "zp", around(k)).astype(F32)
    return total.astype(BF16)


def solution(mesh):
    ep = ("x", "y", "zp", "zb")
    split = Mesh(mesh.devices.reshape(2, 4, 4, 4, 2), ("group",) + ep)
    return jax.shard_map(
        body,
        mesh=split,
        in_specs=(
            P(ep, "group"),
            P(ep, None),
            P(ep, None),
            P("group", None),
            P(),
            P(ep, None, None),
            P(ep, None, None),
            P(ep, None, None),
        ),
        out_specs=P(ep, "group"),
        check_vma=False,
    )
```

time: 133 us -> 129 us (0.970)
  blocking collectives: 64.8 us -> 61.9 us
    all_to_all x1, blocking collectives: 38.6 us -> 35.6 us  [body(): own = lax.all_to_all(sent.reshape(128, 5, 4, 128), EP, 0, 0, tiled=True)]
    pallas_call x9 -> x10, Pallas kernels: 15.2 us -> 14.3 us  [call(): pl.pallas_call(kernel, out_shape=[jax.ShapeDtypeStruct(shape, dtype) for...]
    unnamed x20 -> x18, local copies, waits for them, and re-layouts: 3 us -> 2.56 us
where the time goes in v4:
time: 129 us; the launch traced here: 128 us
  blocking collectives  61.9 us (48%)
  waiting for transfers between devices  32.3 us (25%)
  starting transfers between devices  16.4 us (13%)
  Pallas kernels  14.3 us (11%)
  local copies, waits for them, and re-layouts  2.56 us (2%)
    all_to_all x1, blocking collectives, body(): own = lax.all_to_all(sent.reshape(128, 5, 4, 128), EP, 0, 0, tiled=True)  35.6 us
    all_to_all x1, blocking collectives, body(): items = lax.all_to_all(send.reshape(32, 24, 1024), REGION, 0, 0, tiled=True)  26.3 us
    all_to_all x1, waiting for transfers between devices, body(): lax.all_to_all(expert_out.reshape(32, 24, 1024), REGION, 0, 0, tiled=True)  21.1 us
    pallas_call x10, Pallas kernels, call(): pl.pallas_call(kernel, out_shape=[jax.ShapeDtypeStruct(shape, dtype) for...  14.3 us
    ppermute x3, waiting for transfers between devices, body(): total = total + lax.ppermute(part, 'zp', around(k)).astype(F32)  9.51 us
    ppermute x3, starting transfers between devices, body(): total = total + lax.ppermute(part, 'zp', around(k)).astype(F32)  5 us
    all_to_all x1, starting transfers between devices, body(): lax.all_to_all(expert_out.reshape(32, 24, 1024), REGION, 0, 0, tiled=True)  4.16 us
    ppermute x1, starting transfers between devices, body(): got = lax.ppermute(give, 'group', SWAP)  3.32 us
  transfers between devices with their start and end apart: 7, of which 7 were waited for; matrix products, arithmetic and copies ran while one was open for 0% of the time, Pallas kernels for 3%

profile of v4, /device:TPU:1, one launch (start us, length us, event | category | flops | bytes accessed | tf_op | source)
XLA Modules:
  0.0 128.4 jit_solution(7820515227843378107)
XLA Ops:
  0.0 0.0 copy-start.7
  0.0 0.0 copy-start.6
  0.0 3.0 %shard_map.82 = (f32[128,512]{1,0:T(8,128)S(1)}, f32[128,512]{1,0:T(8,128)S(1)}) custom-call(bf16[128,1024]{1,0:T(8,128)(2,1)} %x_ref.1, bf16[1024,1024]{1,0:T(8,128)(2,1)} %w_hbm.1), custom_call_target="tpu_custom_call" | custom-call | tf_op jit(solution)/shard_map/pallas_call | solution.py:255
  3.1 3.3 %collective-permute-start = (f32[128,512]{1,0:T(8,128)S(1)}, f32[128,512]{1,0:T(8,128)S(1)}, u32[]{:S(2)}, u32[]{:S(2)}) collective-permute-start(f32[128,512]{1,0:T(8,128)S(1)} %get-tuple-element.20), channel_id=1, source_target_pairs={{0,128},{128,0},{1,129},{129,1},{2,130},{130,2},{3,131},{131,3},{4... | collective-permute-start | bytes 786440 | tf_op jit(solution)/shard_map/ppermute | solution.py:291
  6.4 0.0 copy-done.7
  6.4 0.1 copy.10.owner_ref
  6.5 0.0 copy-done.6
  6.5 0.1 copy.11.ids_ref
  6.6 0.2 shard_map.83
  6.8 0.8 collective-permute-done.got_ref
  7.5 0.6 shard_map.84
  8.2 35.6 %all_to_all.15 = bf16[128,5,4,128]{3,2,1,0:T(4,128)(2,1)S(1)} all-to-all(bf16[128,5,4,128]{3,2,1,0:T(4,128)(2,1)S(1)} %bitcast.11), channel_id=1, replica_groups=mesh['group'=2,'x'=4,'y'=4,'zp'=4,'zb'=2] {'x','y','zp','zb'}, dimensions={0} | all-to-all | bytes 1310720 | tf_op jit(solution)/shard_map/all_to_all | solution.py:298
  43.8 2.4 %collective-permute-start.1 = (bf16[128,5,4,128]{3,2,1,0:T(4,128)(2,1)S(1)}, bf16[128,5,4,128]{3,2,1,0:T(4,128)(2,1)S(1)}, u32[]{:S(2)}, u32[]{:S(2)}) collective-permute-start(bf16[128,5,4,128]{3,2,1,0:T(4,128)(2,1)S(1)} %all_to_all.15), channel_id=1, source_target_pairs={{0,128},{128,0},{1,129},{129,1},{2,130},{130,2},{3,131},{131,3},{4... | collective-permute-start | bytes 1966088 | tf_op jit(solution)/shard_map/ppermute | solution.py:299
  46.2 0.9 shard_map.85
  47.2 0.8 collective-permute-done.1
  47.9 2.7 %shard_map.86 = (bf16[768,1024]{1,0:T(8,128)(2,1)S(1)}, bf16[640,1152]{1,0:T(8,128)(2,1)S(1)}) custom-call(bf16[2560,128]{1,0:T(8,128)(2,1)S(1)} %bitcast.10, bf16[2560,128]{1,0:T(8,128)(2,1)S(1)} %bitcast.13, bf16[512,512]{1,0:T(8,128)(2,1)S(1)} %get-tuple-element.24.mine_ref, bf16[256,320]{1,0:T(8,128)(2,1)S(1)} %get-tuple-element.25.order_ref, ...), custom_call_target="tpu_custom_call" | custom-call | tf_op jit(solution)/shard_map/pallas_call | solution.py:255
  50.6 0.0 copy-start.1
  50.6 0.0 copy-start.3
  50.6 0.0 copy-start.4
  50.6 26.3 %all_to_all.16 = bf16[32,24,1024]{2,1,0:T(8,128)(2,1)S(1)} all-to-all(bf16[32,24,1024]{2,1,0:T(8,128)(2,1)S(1)} %bitcast.12), channel_id=1, replica_groups=mesh['group'=2,'x'=4,'y'=4,'zp'=4,'zb'=2] {'x','y','zb'}, dimensions={0} | all-to-all | bytes 3145728 | tf_op jit(solution)/shard_map/all_to_all | solution.py:312
  76.9 0.0 copy-done.1
  76.9 0.0 copy-done.3
  76.9 0.0 copy-done.4
  76.9 0.0 copy-start
  76.9 1.4 %shard_map.88.hidden_ref = bf16[768,384]{1,0:T(8,128)(2,1)S(1)} custom-call(bf16[768,1024]{1,0:T(8,128)(2,1)S(1)} %bitcast.8, bf16[1,1024,384]{2,1,0:T(8,128)(2,1)S(1)} %copy-done.3, bf16[1,1024,384]{2,1,0:T(8,128)(2,1)S(1)} %copy-done.4), custom_call_target="tpu_custom_call" | custom-call | tf_op jit(solution)/shard_map/pallas_call | solution.py:255
  78.3 1.6 %collective-permute-start.2 = (bf16[768,384]{1,0:T(8,128)(2,1)S(1)}, bf16[768,384]{1,0:T(8,128)(2,1)S(1)}, u32[]{:S(2)}, u32[]{:S(2)}) collective-permute-start(bf16[768,384]{1,0:T(8,128)(2,1)S(1)} %shard_map.88.hidden_ref), channel_id=1, source_target_pairs={{0,128},{128,0},{1,129},{129,1},{2,130},{130,2},{3,131},{131,3},{4... | collective-permute-start | bytes 1769480 | tf_op jit(solution)/shard_map/ppermute | solution.py:319
  79.9 0.0 copy-done
  79.9 1.4 %shard_map.89.refs_0_ = bf16[768,1024]{1,0:T(8,128)(2,1)} custom-call(bf16[768,384]{1,0:T(8,128)(2,1)S(1)} %shard_map.88.hidden_ref, bf16[1,384,1024]{2,1,0:T(8,128)(2,1)S(1)} %copy-done), custom_call_target="tpu_custom_call" | custom-call | tf_op jit(solution)/shard_map/pallas_call | solution.py:255
  81.3 0.2 collective-permute-done.2.hidden_ref
  81.5 1.4 %shard_map.90 = bf16[768,1024]{1,0:T(8,128)(2,1)} custom-call(bf16[768,384]{1,0:T(8,128)(2,1)S(1)} %collective-permute-done.2.hidden_ref, bf16[1,384,1024]{2,1,0:T(8,128)(2,1)S(1)} %copy-done, bf16[768,1024]{1,0:T(8,128)(2,1)} %shard_map.89.refs_0_), custom_call_target="tpu_custom_call", output_to_operand_aliasing={{}: (2, {})} | custom-call | tf_op jit(solution)/shard_map/pallas_call | solution.py:255
  83.0 4.2 %all-to-all-start.2 = ((bf16[32,24,1024]{2,1,0:T(8,128)(2,1)}), bf16[32,24,1024]{2,1,0:T(8,128)(2,1)S(1)}, u32[]{:S(2)}, u32[]{:S(2)}) async-start(bf16[32,24,1024]{2,1,0:T(8,128)(2,1)} %bitcast.5), calls=%async_computation.2 | async-start | bytes 3145728 | tf_op jit(solution)/shard_map/all_to_all | solution.py:333
  87.1 0.0 copy-start.2
  87.1 1.4 %copy-done.2 = bf16[640,1152]{1,0:T(8,128)(2,1)S(1)} copy-done((bf16[640,1152]{1,0:T(8,128)(2,1)S(1)}, bf16[640,1152]{1,0:T(8,128)(2,1)}, u32[]{:S(2)}) %copy-start.2) | copy-done | bytes 1474584
  88.5 0.0 copy-start.5
  88.5 0.9 copy-done.5
  89.5 1.5 %shard_map.87.mix_ref = bf16[640,1536]{1,0:T(8,128)(2,1)S(1)} custom-call(bf16[640,1152]{1,0:T(8,128)(2,1)S(1)} %copy-done.2, bf16[1024,128]{1,0:T(8,128)(2,1)S(1)} %copy-done.5), custom_call_target="tpu_custom_call" | custom-call | tf_op jit(solution)/shard_map/pallas_call | solution.py:255
  91.0 21.1 %all-to-all-done.2 = bf16[32,24,1024]{2,1,0:T(8,128)(2,1)S(1)} async-done(((bf16[32,24,1024]{2,1,0:T(8,128)(2,1)}), bf16[32,24,1024]{2,1,0:T(8,128)(2,1)S(1)}, u32[]{:S(2)}, u32[]{:S(2)}) %all-to-all-start.2) | async-done | bytes 1572896 | tf_op jit(solution)/shard_map/all_to_all | solution.py:333
  112.1 1.1 shard_map.91
  113.2 1.4 %collective-permute-start.3 = (bf16[128,512]{1,0:T(8,128)(2,1)S(1)}, bf16[128,512]{1,0:T(8,128)(2,1)S(1)}, u32[]{:S(2)}, u32[]{:S(2)}) collective-permute-start(bf16[128,512]{1,0:T(8,128)(2,1)S(1)} %get-tuple-element.30), channel_id=1, source_target_pairs={{0,4},{2,6},{4,0},{6,2},{1,5},{3,7},{5,1},{7,3},{8,12},{10,14},{12... | collective-permute-start | bytes 393224 | tf_op jit(solution)/shard_map/ppermute | solution.py:341
  114.6 1.4 %collective-permute-start.4 = (bf16[128,512]{1,0:T(8,128)(2,1)S(1)}, bf16[128,512]{1,0:T(8,128)(2,1)S(1)}, u32[]{:S(2)}, u32[]{:S(2)}) collective-permute-start(bf16[128,512]{1,0:T(8,128)(2,1)S(1)} %get-tuple-element.31), channel_id=1, source_target_pairs={{0,2},{2,4},{4,6},{6,0},{1,3},{3,5},{5,7},{7,1},{8,10},{10,12},{12... | collective-permute-start | bytes 393224 | tf_op jit(solution)/shard_map/ppermute | solution.py:341
  115.9 2.2 %collective-permute-start.5 = (bf16[128,512]{1,0:T(8,128)(2,1)S(1)}, bf16[128,512]{1,0:T(8,128)(2,1)S(1)}, u32[]{:S(2)}, u32[]{:S(2)}) collective-permute-start(bf16[128,512]{1,0:T(8,128)(2,1)S(1)} %get-tuple-element.32), channel_id=1, source_target_pairs={{0,6},{2,0},{4,2},{6,4},{1,7},{3,1},{5,3},{7,5},{8,14},{10,8},{12,... | collective-permute-start | bytes 393224 | tf_op jit(solution)/shard_map/ppermute | solution.py:341
  118.2 6.6 %collective-permute-done.3 = bf16[128,512]{1,0:T(8,128)(2,1)S(1)} collective-permute-done((bf16[128,512]{1,0:T(8,128)(2,1)S(1)}, bf16[128,512]{1,0:T(8,128)(2,1)S(1)}, u32[]{:S(2)}, u32[]{:S(2)}) %collective-permute-start.3) | collective-permute-done | bytes 131104 | tf_op jit(solution)/shard_map/ppermute | solution.py:341
  124.8 1.7 %collective-permute-done.4 = bf16[128,512]{1,0:T(8,128)(2,1)S(1)} collective-permute-done((bf16[128,512]{1,0:T(8,128)(2,1)S(1)}, bf16[128,512]{1,0:T(8,128)(2,1)S(1)}, u32[]{:S(2)}, u32[]{:S(2)}) %collective-permute-start.4) | collective-permute-done | bytes 131104 | tf_op jit(solution)/shard_map/ppermute | solution.py:341
  126.5 1.1 collective-permute-done.5
  127.7 0.7 add_convert_fusion
Async XLA Ops:
  0.0 6.4 %copy-start.7 = (s32[128,1]{0,1:T(1,128)S(1)}, s32[128,1]{0,1:T(1,128)}, u32[]{:S(2)}) copy-start(s32[128,1]{0,1:T(1,128)} %param.9) | copy-start | bytes 1540
  0.0 6.5 %copy-start.6 = (s32[128,8]{0,1:T(8,128)S(1)}, s32[128,8]{0,1:T(8,128)}, u32[]{:S(2)}) copy-start(s32[128,8]{0,1:T(8,128)} %param.10) | copy-start | bytes 12292
  3.1 4.5 %collective-permute-start = (f32[128,512]{1,0:T(8,128)S(1)}, f32[128,512]{1,0:T(8,128)S(1)}, u32[]{:S(2)}, u32[]{:S(2)}) collective-permute-start(f32[128,512]{1,0:T(8,128)S(1)} %get-tuple-element.20), channel_id=1, source_target_pairs={{0,128},{128,0},{1,129},{129,1},{2,130},{130,2},{3,131},{131,3},{4... | collective-permute-start | bytes 786440 | tf_op jit(solution)/shard_map/ppermute | solution.py:291
  43.8 4.1 %collective-permute-start.1 = (bf16[128,5,4,128]{3,2,1,0:T(4,128)(2,1)S(1)}, bf16[128,5,4,128]{3,2,1,0:T(4,128)(2,1)S(1)}, u32[]{:S(2)}, u32[]{:S(2)}) collective-permute-start(bf16[128,5,4,128]{3,2,1,0:T(4,128)(2,1)S(1)} %all_to_all.15), channel_id=1, source_target_pairs={{0,128},{128,0},{1,129},{129,1},{2,130},{130,2},{3,131},{131,3},{4... | collective-permute-start | bytes 1966088 | tf_op jit(solution)/shard_map/ppermute | solution.py:299
  50.6 26.3 %copy-start.1 = (bf16[640,1152]{1,0:T(8,128)(2,1)}, bf16[640,1152]{1,0:T(8,128)(2,1)S(1)}, u32[]{:S(2)}) copy-start(bf16[640,1152]{1,0:T(8,128)(2,1)S(1)} %get-tuple-element.27.normed_ref) | copy-start | bytes 4423684
  50.6 26.3 %copy-start.3 = (bf16[1,1024,384]{2,1,0:T(8,128)(2,1)S(1)}, bf16[1,1024,384]{2,1,0:T(8,128)(2,1)}, u32[]{:S(2)}) copy-start(bf16[1,1024,384]{2,1,0:T(8,128)(2,1)} %gate_ref.1) | copy-start | bytes 2359300
  50.6 26.3 %copy-start.4 = (bf16[1,1024,384]{2,1,0:T(8,128)(2,1)S(1)}, bf16[1,1024,384]{2,1,0:T(8,128)(2,1)}, u32[]{:S(2)}) copy-start(bf16[1,1024,384]{2,1,0:T(8,128)(2,1)} %up_ref.1) | copy-start | bytes 2359300
  76.9 3.0 %copy-start = (bf16[1,384,1024]{2,1,0:T(8,128)(2,1)S(1)}, bf16[1,384,1024]{2,1,0:T(8,128)(2,1)}, u32[]{:S(2)}) copy-start(bf16[1,384,1024]{2,1,0:T(8,128)(2,1)} %down_ref.3) | copy-start | bytes 2359300
  78.3 3.2 %collective-permute-start.2 = (bf16[768,384]{1,0:T(8,128)(2,1)S(1)}, bf16[768,384]{1,0:T(8,128)(2,1)S(1)}, u32[]{:S(2)}, u32[]{:S(2)}) collective-permute-start(bf16[768,384]{1,0:T(8,128)(2,1)S(1)} %shard_map.88.hidden_ref), channel_id=1, source_target_pairs={{0,128},{128,0},{1,129},{129,1},{2,130},{130,2},{3,131},{131,3},{4... | collective-permute-start | bytes 1769480 | tf_op jit(solution)/shard_map/ppermute | solution.py:319
  83.0 29.1 %all-to-all-start.2 = ((bf16[32,24,1024]{2,1,0:T(8,128)(2,1)}), bf16[32,24,1024]{2,1,0:T(8,128)(2,1)S(1)}, u32[]{:S(2)}, u32[]{:S(2)}) async-start(bf16[32,24,1024]{2,1,0:T(8,128)(2,1)} %bitcast.5), calls=%async_computation.2 | async-start | bytes 3145728 | tf_op jit(solution)/shard_map/all_to_all | solution.py:333
  87.1 1.4 %copy-start.2 = (bf16[640,1152]{1,0:T(8,128)(2,1)S(1)}, bf16[640,1152]{1,0:T(8,128)(2,1)}, u32[]{:S(2)}) copy-start(bf16[640,1152]{1,0:T(8,128)(2,1)} %copy-done.1) | copy-start | bytes 4423684
  88.5 0.9 copy-start.5
  113.2 11.6 %collective-permute-start.3 = (bf16[128,512]{1,0:T(8,128)(2,1)S(1)}, bf16[128,512]{1,0:T(8,128)(2,1)S(1)}, u32[]{:S(2)}, u32[]{:S(2)}) collective-permute-start(bf16[128,512]{1,0:T(8,128)(2,1)S(1)} %get-tuple-element.30), channel_id=1, source_target_pairs={{0,4},{2,6},{4,0},{6,2},{1,5},{3,7},{5,1},{7,3},{8,12},{10,14},{12... | collective-permute-start | bytes 393224 | tf_op jit(solution)/shard_map/ppermute | solution.py:341
  114.6 11.9 %collective-permute-start.4 = (bf16[128,512]{1,0:T(8,128)(2,1)S(1)}, bf16[128,512]{1,0:T(8,128)(2,1)S(1)}, u32[]{:S(2)}, u32[]{:S(2)}) collective-permute-start(bf16[128,512]{1,0:T(8,128)(2,1)S(1)} %get-tuple-element.31), channel_id=1, source_target_pairs={{0,2},{2,4},{4,6},{6,0},{1,3},{3,5},{5,7},{7,1},{8,10},{10,12},{12... | collective-permute-start | bytes 393224 | tf_op jit(solution)/shard_map/ppermute | solution.py:341
  115.9 11.7 %collective-permute-start.5 = (bf16[128,512]{1,0:T(8,128)(2,1)S(1)}, bf16[128,512]{1,0:T(8,128)(2,1)S(1)}, u32[]{:S(2)}, u32[]{:S(2)}) collective-permute-start(bf16[128,512]{1,0:T(8,128)(2,1)S(1)} %get-tuple-element.32), channel_id=1, source_target_pairs={{0,6},{2,0},{4,2},{6,4},{1,7},{3,1},{5,3},{7,5},{8,14},{10,8},{12,... | collective-permute-start | bytes 393224 | tf_op jit(solution)/shard_map/ppermute | solution.py:341

commit v5 on v4

--- a/solution.py
+++ b/solution.py
@@ -5,18 +5,26 @@
 from jax import lax
 from jax.experimental import pallas as pl
 from jax.experimental.pallas import tpu as pltpu
-from jax.sharding import Mesh
 from jax.sharding import PartitionSpec as P
 
 F32 = jnp.float32
 BF16 = jnp.bfloat16
 I32 = jnp.int32
-EP = ("x", "y", "zp", "zb")
-REGION = ("x", "y", "zb")
+EP_FIRST = 112
+REGION_FIRST = 21
+EP = [[(r + EP_FIRST) % 128 for r in range(128)]]
+REGIONS = [
+    [(i >> 1) * 8 + zp * 2 + (i & 1) for i in ((r + REGION_FIRST) % 32 for r in range(32))]
+    for zp in range(4)
+]
 SWAP = [(0, 1), (1, 0)]
 VMEM = pl.BlockSpec(memory_space=pltpu.VMEM)
 HBM = pl.BlockSpec(memory_space=pltpu.HBM)
 PARAMS = pltpu.CompilerParams(vmem_limit_bytes=16 * 1024 * 1024)
+
+
+def my_zp():
+    return (lax.axis_index("ep") >> 1) & 3
 
 
 def iota(shape, dim):
@@ -93,7 +101,7 @@
 
 def prepare_kernel(owner_ref, ids_ref, chosen_ref, ids_out_ref, order_ref):
     n = iota((128, 512), 1)
-    e = n >> 2
+    e = ((n >> 2) + EP_FIRST) & 127
     wanted = ((((e >> 3) << 2) + (n & 3)) << 1) + (e & 1)
     chosen_ref[...] = (owner_ref[...] == wanted).astype(F32).T.astype(BF16)
     a = iota((16, 8), 0)
@@ -119,7 +127,7 @@
 
 
 def expand_matrix(zp):
-    e = by24(iota((768, 128), 0))
+    e = (by24(iota((768, 128), 0)) + REGION_FIRST) & 31
     return (iota((768, 128), 1) == ((e >> 1) << 3) + zp * 2 + (e & 1)).astype(BF16)
 
 
@@ -131,31 +139,33 @@
 
 def arrange(ref, rows, at, order):
     for g in range(8):
+        slots = (g * 16 + EP_FIRST) % 128
         part = dot(order, ref[pl.ds(g * 320, 320), :]).astype(BF16)
         for f in range(4):
             lanes = pl.ds(pl.multiple_of(at + f * 128, 128), 128)
             for member in range(4):
                 first = (f * 4 + member) * 16
-                rows[pl.ds(member * 128 + g * 16, 16), lanes] = part[first : first + 16]
+                rows[pl.ds(member * 128 + slots, 16), lanes] = part[first : first + 16]
 
 
 def arrange_kernel(own_ref, rows_ref, order_ref, expand_ref):
     a = iota((256, 320), 0)
     order = (iota((256, 320), 1) == (a & 15) * 20 + (a >> 4)).astype(F32).astype(BF16)
     order_ref[...] = order
-    expand_ref[:, 0:128] = expand_matrix(lax.axis_index("zp"))
+    expand_ref[:, 0:128] = expand_matrix(my_zp())
     taken = item_code(iota((768, 128), 0), lax.axis_index("group"))
     expand_ref[:, 128:256] = jnp.where(iota((768, 128), 1) == 0, -taken, 0.0).astype(BF16)
     arrange(own_ref, rows_ref, 0, order)
 
 
 def find_items(own_ref, other_ref, expand_ref, code_ref, pick):
-    xy, zb = lax.axis_index(("x", "y")), lax.axis_index("zb")
+    ep = lax.axis_index("ep")
+    zb = ep & 1
     expert = iota((128, 128), 0)
     earlier = (expert < iota((128, 128), 1)).astype(F32).astype(BF16)
     expert = expert.astype(F32)
     a = iota((16, 160), 0)
-    line = pl.ds(pl.multiple_of(xy * 160, 160), 160)
+    line = pl.ds(pl.multiple_of((((ep + 128 - EP_FIRST) & 127) >> 3) * 160, 160), 160)
     choose = (iota((16, 160), 1) == (a >> 2) * 40 + zb * 20 + 16 + (a & 3)).astype(F32).astype(BF16)
     first = dot(choose, own_ref[line, :])
     second = dot(choose, other_ref[line, :])
@@ -177,7 +187,7 @@
 def dispatch_kernel(
     own_ref, other_ref, mine_ref, order_ref, expand_ref, send_ref, normed_ref, rows, pick
 ):
-    zp = lax.axis_index("zp")
+    zp = my_zp()
     mine, other = halves()
     find_items(own_ref, other_ref, expand_ref, normed_ref, pick)
     rows[:, mine] = mine_ref[...]
@@ -195,7 +205,7 @@
 
 def gate_kernel(normed_ref, router_ref, mix_ref):
     mix_ref[512:640, 0:512] = normed_ref[512:640, 0:512]
-    expand = expand_matrix(lax.axis_index("zp"))
+    expand = expand_matrix(my_zp())
     wanted = [item_code(iota((128, 768), 1), half) for half in (0, 1)]
     for member in range(4):
         at = pl.ds(member * 128, 128)
@@ -241,7 +251,7 @@
 
 
 def mix_kernel(mix_ref, back_ref, two_ref, one_ref, three_ref, own_ref, total):
-    zp = lax.axis_index("zp")
+    zp = my_zp()
     items = jnp.concatenate([back_ref[:, 0:512], back_ref[:, 512:1024]], axis=0)
     total[...] = dot(mix_ref[0:512, :], items)
     for k, ref in ((2, two_ref), (1, one_ref), (3, three_ref), (0, own_ref)):
@@ -268,7 +278,11 @@
 
 
 def around(k):
-    return [(i, (i + k) % 4) for i in range(4)]
+    return [(i, (i & ~7) + ((i + 2 * k) & 7)) for i in range(128)]
+
+
+def exchange(x, groups):
+    return lax.all_to_all(x, "ep", 0, 0, axis_index_groups=groups, tiled=True)
 
 
 def body(
@@ -295,7 +309,7 @@
         (owner_map, talker_ids),
     )
     (sent,) = call(spread_kernel, [((2560, 128), BF16)], (keep, got, chosen, ids, order))
-    own = lax.all_to_all(sent.reshape(128, 5, 4, 128), EP, 0, 0, tiled=True)
+    own = exchange(sent.reshape(128, 5, 4, 128), EP)
     other = lax.ppermute(own, "group", SWAP).reshape(2560, 128)
     own = own.reshape(2560, 128)
     mine, order, expand = call(
@@ -309,7 +323,7 @@
         (own, other, mine, order, expand),
         [pltpu.VMEM((512, 1024), BF16), pltpu.VMEM((768, 512), BF16)],
     )
-    items = lax.all_to_all(send.reshape(32, 24, 1024), REGION, 0, 0, tiled=True)
+    items = exchange(send.reshape(32, 24, 1024), REGIONS)
     (mix,) = call(gate_kernel, [((640, 1536), BF16)], (normed, router_weight))
     (hidden,) = call(
         hidden_kernel,
@@ -330,7 +344,7 @@
         specs=[VMEM, VMEM, HBM],
         aliases={2: 0},
     )
-    back = lax.all_to_all(expert_out.reshape(32, 24, 1024), REGION, 0, 0, tiled=True)
+    back = exchange(expert_out.reshape(32, 24, 1024), REGIONS)
     two, one, three, total = call(
         mix_kernel,
         [((128, 512), BF16)] * 3 + [((128, 512), F32)],
@@ -338,26 +352,24 @@
         [pltpu.VMEM((512, 512), F32)],
     )
     for k, part in ((2, two), (1, one), (3, three)):
-        total = total + lax.ppermute(part, "zp", around(k)).astype(F32)
+        total = total + lax.ppermute(part, "ep", around(k)).astype(F32)
     return total.astype(BF16)
 
 
 def solution(mesh):
-    ep = ("x", "y", "zp", "zb")
-    split = Mesh(mesh.devices.reshape(2, 4, 4, 4, 2), ("group",) + ep)
     return jax.shard_map(
         body,
-        mesh=split,
+        mesh=mesh,
         in_specs=(
-            P(ep, "group"),
-            P(ep, None),
-            P(ep, None),
+            P("ep", "group"),
+            P("ep", None),
+            P("ep", None),
             P("group", None),
             P(),
-            P(ep, None, None),
-            P(ep, None, None),
-            P(ep, None, None),
+            P("ep", None, None),
+            P("ep", None, None),
+            P("ep", None, None),
         ),
-        out_specs=P(ep, "group"),
+        out_specs=P("ep", "group"),
         check_vma=False,
     )

time: 129 us -> 125 us (0.969)
  starting transfers between devices: 16.4 us -> 21.6 us
  waiting for transfers between devices: 32.3 us -> 27.5 us
  blocking collectives: 61.9 us -> 58 us
    all_to_all x1, waiting for transfers between devices: 21.1 us -> 14.1 us  [exchange(): return lax.all_to_all(x, 'ep', 0, 0, axis_index_groups=groups, tiled=True)]
    all_to_all x1, starting transfers between devices: 4.16 us -> 9.53 us  [exchange(): return lax.all_to_all(x, 'ep', 0, 0, axis_index_groups=groups, tiled=True)]
    all_to_all x2, blocking collectives: 61.9 us -> 58 us  [exchange(): return lax.all_to_all(x, 'ep', 0, 0, axis_index_groups=groups, tiled=True)]
    ppermute x3, waiting for transfers between devices: 9.51 us -> 11.7 us  [body(): total = total + lax.ppermute(part, 'ep', around(k)).astype(F32)]
where the time goes in v5:
time: 125 us
  blocking collectives  58 us (46%)
  waiting for transfers between devices  27.5 us (22%)
  starting transfers between devices  21.6 us (17%)
  Pallas kernels  14.4 us (12%)
  local copies, waits for them, and re-layouts  2.56 us (2%)
    all_to_all x2, blocking collectives, exchange(): return lax.all_to_all(x, 'ep', 0, 0, axis_index_groups=groups, tiled=True)  58 us
    pallas_call x10, Pallas kernels, call(): pl.pallas_call(kernel, out_shape=[jax.ShapeDtypeStruct(shape, dtype) for...  14.4 us
    all_to_all x1, waiting for transfers between devices, exchange(): return lax.all_to_all(x, 'ep', 0, 0, axis_index_groups=groups, tiled=True)  14.1 us
    ppermute x3, waiting for transfers between devices, body(): total = total + lax.ppermute(part, 'ep', around(k)).astype(F32)  11.7 us
    all_to_all x1, starting transfers between devices, exchange(): return lax.all_to_all(x, 'ep', 0, 0, axis_index_groups=groups, tiled=True)  9.53 us
    ppermute x3, starting transfers between devices, body(): total = total + lax.ppermute(part, 'ep', around(k)).astype(F32)  5.3 us
    ppermute x1, starting transfers between devices, body(): got = lax.ppermute(give, 'group', SWAP)  3.32 us
    unnamed x18, local copies, waits for them, and re-layouts  2.56 us
  transfers between devices with their start and end apart: 7, of which 7 were waited for; matrix products, arithmetic and copies ran while one was open for 0% of the time, Pallas kernels for 3%

profile of v5, /device:TPU:1, one launch (start us, length us, event | category | flops | bytes accessed | tf_op | source)
XLA Modules:
  0.0 125.0 jit_solution(11569225125211129954)
XLA Ops:
  0.0 0.0 copy-start.7
  0.0 0.0 copy-start.6
  0.0 3.0 %shard_map.82 = (f32[128,512]{1,0:T(8,128)S(1)}, f32[128,512]{1,0:T(8,128)S(1)}) custom-call(bf16[128,1024]{1,0:T(8,128)(2,1)} %x_ref.1, bf16[1024,1024]{1,0:T(8,128)(2,1)} %w_hbm.1), custom_call_target="tpu_custom_call" | custom-call | tf_op jit(solution)/shard_map/pallas_call | solution.py:265
  3.1 3.3 %collective-permute-start = (f32[128,512]{1,0:T(8,128)S(1)}, f32[128,512]{1,0:T(8,128)S(1)}, u32[]{:S(2)}, u32[]{:S(2)}) collective-permute-start(f32[128,512]{1,0:T(8,128)S(1)} %get-tuple-element.20), channel_id=1, source_target_pairs={{0,128},{128,0},{1,129},{129,1},{2,130},{130,2},{3,131},{131,3},{4... | collective-permute-start | bytes 786440 | tf_op jit(solution)/shard_map/ppermute | solution.py:305
  6.4 0.0 copy-done.7
  6.4 0.1 copy.10.owner_ref
  6.5 0.0 copy-done.6
  6.5 0.1 copy.11.ids_ref
  6.6 0.2 shard_map.83
  6.8 0.8 collective-permute-done.got_ref
  7.5 0.6 shard_map.84
  8.2 32.0 %all_to_all.15 = bf16[128,5,4,128]{3,2,1,0:T(4,128)(2,1)S(1)} all-to-all(bf16[128,5,4,128]{3,2,1,0:T(4,128)(2,1)S(1)} %bitcast.11), channel_id=1, replica_groups={{112,113,114,115,116,117,118,119,120,121,122,123,124,125,126,127,0,1,2,..., dimensions={0} | all-to-all | bytes 1310720 | tf_op jit(solution)/shard_map/all_to_all | solution.py:285
  40.2 2.3 %collective-permute-start.1 = (bf16[128,5,4,128]{3,2,1,0:T(4,128)(2,1)S(1)}, bf16[128,5,4,128]{3,2,1,0:T(4,128)(2,1)S(1)}, u32[]{:S(2)}, u32[]{:S(2)}) collective-permute-start(bf16[128,5,4,128]{3,2,1,0:T(4,128)(2,1)S(1)} %all_to_all.15), channel_id=1, source_target_pairs={{0,128},{128,0},{1,129},{129,1},{2,130},{130,2},{3,131},{131,3},{4... | collective-permute-start | bytes 1966088 | tf_op jit(solution)/shard_map/ppermute | solution.py:313
  42.5 1.0 shard_map.85
  43.5 0.7 collective-permute-done.1
  44.2 2.7 %shard_map.86 = (bf16[768,1024]{1,0:T(8,128)(2,1)S(1)}, bf16[640,1152]{1,0:T(8,128)(2,1)S(1)}) custom-call(bf16[2560,128]{1,0:T(8,128)(2,1)S(1)} %bitcast.10, bf16[2560,128]{1,0:T(8,128)(2,1)S(1)} %bitcast.13, bf16[512,512]{1,0:T(8,128)(2,1)S(1)} %get-tuple-element.24.mine_ref, bf16[256,320]{1,0:T(8,128)(2,1)S(1)} %get-tuple-element.25.order_ref, ...), custom_call_target="tpu_custom_call" | custom-call | tf_op jit(solution)/shard_map/pallas_call | solution.py:265
  46.9 0.0 copy-start.1
  47.0 0.0 copy-start.3
  47.0 0.0 copy-start.4
  47.0 25.9 %all_to_all.16 = bf16[32,24,1024]{2,1,0:T(8,128)(2,1)S(1)} all-to-all(bf16[32,24,1024]{2,1,0:T(8,128)(2,1)S(1)} %bitcast.12), channel_id=1, replica_groups={{81,88,89,96,97,104,105,112,113,120,121,0,1,8,9,16,17,24,25,32,33,40,41..., dimensions={0} | all-to-all | bytes 3145728 | tf_op jit(solution)/shard_map/all_to_all | solution.py:285
  72.9 0.0 copy-done.1
  72.9 0.0 copy-done.3
  72.9 0.0 copy-done.4
  72.9 0.0 copy-start
  72.9 1.4 %shard_map.88.hidden_ref = bf16[768,384]{1,0:T(8,128)(2,1)S(1)} custom-call(bf16[768,1024]{1,0:T(8,128)(2,1)S(1)} %bitcast.8, bf16[1,1024,384]{2,1,0:T(8,128)(2,1)S(1)} %copy-done.3, bf16[1,1024,384]{2,1,0:T(8,128)(2,1)S(1)} %copy-done.4), custom_call_target="tpu_custom_call" | custom-call | tf_op jit(solution)/shard_map/pallas_call | solution.py:265
  74.3 1.2 collective-permute-start.2
  75.5 0.0 copy-done
  75.5 1.4 %shard_map.89.refs_0_ = bf16[768,1024]{1,0:T(8,128)(2,1)} custom-call(bf16[768,384]{1,0:T(8,128)(2,1)S(1)} %shard_map.88.hidden_ref, bf16[1,384,1024]{2,1,0:T(8,128)(2,1)S(1)} %copy-done), custom_call_target="tpu_custom_call" | custom-call | tf_op jit(solution)/shard_map/pallas_call | solution.py:265
  77.0 0.2 collective-permute-done.2.hidden_ref
  77.2 1.4 %shard_map.90 = bf16[768,1024]{1,0:T(8,128)(2,1)} custom-call(bf16[768,384]{1,0:T(8,128)(2,1)S(1)} %collective-permute-done.2.hidden_ref, bf16[1,384,1024]{2,1,0:T(8,128)(2,1)S(1)} %copy-done, bf16[768,1024]{1,0:T(8,128)(2,1)} %shard_map.89.refs_0_), custom_call_target="tpu_custom_call", output_to_operand_aliasing={{}: (2, {})} | custom-call | tf_op jit(solution)/shard_map/pallas_call | solution.py:265
  78.6 9.5 %all-to-all-start.2 = ((bf16[32,24,1024]{2,1,0:T(8,128)(2,1)}), bf16[32,24,1024]{2,1,0:T(8,128)(2,1)S(1)}, u32[]{:S(2)}, u32[]{:S(2)}) async-start(bf16[32,24,1024]{2,1,0:T(8,128)(2,1)} %bitcast.5), calls=%async_computation.2 | async-start | bytes 3145728 | tf_op jit(solution)/shard_map/all_to_all | solution.py:285
  88.1 0.0 copy-start.2
  88.1 1.4 %copy-done.2 = bf16[640,1152]{1,0:T(8,128)(2,1)S(1)} copy-done((bf16[640,1152]{1,0:T(8,128)(2,1)S(1)}, bf16[640,1152]{1,0:T(8,128)(2,1)}, u32[]{:S(2)}) %copy-start.2) | copy-done | bytes 1474584
  89.5 0.0 copy-start.5
  89.5 0.9 copy-done.5
  90.4 1.6 %shard_map.87.mix_ref = bf16[640,1536]{1,0:T(8,128)(2,1)S(1)} custom-call(bf16[640,1152]{1,0:T(8,128)(2,1)S(1)} %copy-done.2, bf16[1024,128]{1,0:T(8,128)(2,1)S(1)} %copy-done.5), custom_call_target="tpu_custom_call" | custom-call | tf_op jit(solution)/shard_map/pallas_call | solution.py:265
  92.0 14.1 %all-to-all-done.2 = bf16[32,24,1024]{2,1,0:T(8,128)(2,1)S(1)} async-done(((bf16[32,24,1024]{2,1,0:T(8,128)(2,1)}), bf16[32,24,1024]{2,1,0:T(8,128)(2,1)S(1)}, u32[]{:S(2)}, u32[]{:S(2)}) %all-to-all-start.2) | async-done | bytes 1572896 | tf_op jit(solution)/shard_map/all_to_all | solution.py:285
  106.2 1.1 shard_map.91
  107.2 1.7 %collective-permute-start.3 = (bf16[128,512]{1,0:T(8,128)(2,1)S(1)}, bf16[128,512]{1,0:T(8,128)(2,1)S(1)}, u32[]{:S(2)}, u32[]{:S(2)}) collective-permute-start(bf16[128,512]{1,0:T(8,128)(2,1)S(1)} %get-tuple-element.30), channel_id=1, source_target_pairs={{0,4},{1,5},{2,6},{3,7},{4,0},{5,1},{6,2},{7,3},{8,12},{9,13},{10,... | collective-permute-start | bytes 393224 | tf_op jit(solution)/shard_map/ppermute | solution.py:355
  109.0 2.1 %collective-permute-start.4 = (bf16[128,512]{1,0:T(8,128)(2,1)S(1)}, bf16[128,512]{1,0:T(8,128)(2,1)S(1)}, u32[]{:S(2)}, u32[]{:S(2)}) collective-permute-start(bf16[128,512]{1,0:T(8,128)(2,1)S(1)} %get-tuple-element.31), channel_id=1, source_target_pairs={{0,2},{1,3},{2,4},{3,5},{4,6},{5,7},{6,0},{7,1},{8,10},{9,11},{10,... | collective-permute-start | bytes 393224 | tf_op jit(solution)/shard_map/ppermute | solution.py:355
  111.1 1.4 %collective-permute-start.5 = (bf16[128,512]{1,0:T(8,128)(2,1)S(1)}, bf16[128,512]{1,0:T(8,128)(2,1)S(1)}, u32[]{:S(2)}, u32[]{:S(2)}) collective-permute-start(bf16[128,512]{1,0:T(8,128)(2,1)S(1)} %get-tuple-element.32), channel_id=1, source_target_pairs={{0,6},{1,7},{2,0},{3,1},{4,2},{5,3},{6,4},{7,5},{8,14},{9,15},{10,... | collective-permute-start | bytes 393224 | tf_op jit(solution)/shard_map/ppermute | solution.py:355
  112.5 2.7 %collective-permute-done.3 = bf16[128,512]{1,0:T(8,128)(2,1)S(1)} collective-permute-done((bf16[128,512]{1,0:T(8,128)(2,1)S(1)}, bf16[128,512]{1,0:T(8,128)(2,1)S(1)}, u32[]{:S(2)}, u32[]{:S(2)}) %collective-permute-start.3) | collective-permute-done | bytes 131104 | tf_op jit(solution)/shard_map/ppermute | solution.py:355
  115.3 4.6 %collective-permute-done.4 = bf16[128,512]{1,0:T(8,128)(2,1)S(1)} collective-permute-done((bf16[128,512]{1,0:T(8,128)(2,1)S(1)}, bf16[128,512]{1,0:T(8,128)(2,1)S(1)}, u32[]{:S(2)}, u32[]{:S(2)}) %collective-permute-start.4) | collective-permute-done | bytes 131104 | tf_op jit(solution)/shard_map/ppermute | solution.py:355
  119.9 4.4 %collective-permute-done.5 = bf16[128,512]{1,0:T(8,128)(2,1)S(1)} collective-permute-done((bf16[128,512]{1,0:T(8,128)(2,1)S(1)}, bf16[128,512]{1,0:T(8,128)(2,1)S(1)}, u32[]{:S(2)}, u32[]{:S(2)}) %collective-permute-start.5) | collective-permute-done | bytes 131104 | tf_op jit(solution)/shard_map/ppermute | solution.py:355
  124.2 0.7 add_convert_fusion
Async XLA Ops:
  0.0 6.4 %copy-start.7 = (s32[128,1]{0,1:T(1,128)S(1)}, s32[128,1]{0,1:T(1,128)}, u32[]{:S(2)}) copy-start(s32[128,1]{0,1:T(1,128)} %param.9) | copy-start | bytes 1540
  0.0 6.5 %copy-start.6 = (s32[128,8]{0,1:T(8,128)S(1)}, s32[128,8]{0,1:T(8,128)}, u32[]{:S(2)}) copy-start(s32[128,8]{0,1:T(8,128)} %param.10) | copy-start | bytes 12292
  3.1 4.5 %collective-permute-start = (f32[128,512]{1,0:T(8,128)S(1)}, f32[128,512]{1,0:T(8,128)S(1)}, u32[]{:S(2)}, u32[]{:S(2)}) collective-permute-start(f32[128,512]{1,0:T(8,128)S(1)} %get-tuple-element.20), channel_id=1, source_target_pairs={{0,128},{128,0},{1,129},{129,1},{2,130},{130,2},{3,131},{131,3},{4... | collective-permute-start | bytes 786440 | tf_op jit(solution)/shard_map/ppermute | solution.py:305
  40.2 4.0 %collective-permute-start.1 = (bf16[128,5,4,128]{3,2,1,0:T(4,128)(2,1)S(1)}, bf16[128,5,4,128]{3,2,1,0:T(4,128)(2,1)S(1)}, u32[]{:S(2)}, u32[]{:S(2)}) collective-permute-start(bf16[128,5,4,128]{3,2,1,0:T(4,128)(2,1)S(1)} %all_to_all.15), channel_id=1, source_target_pairs={{0,128},{128,0},{1,129},{129,1},{2,130},{130,2},{3,131},{131,3},{4... | collective-permute-start | bytes 1966088 | tf_op jit(solution)/shard_map/ppermute | solution.py:313
  46.9 26.0 %copy-start.1 = (bf16[640,1152]{1,0:T(8,128)(2,1)}, bf16[640,1152]{1,0:T(8,128)(2,1)S(1)}, u32[]{:S(2)}) copy-start(bf16[640,1152]{1,0:T(8,128)(2,1)S(1)} %get-tuple-element.27.normed_ref) | copy-start | bytes 4423684
  47.0 26.0 %copy-start.3 = (bf16[1,1024,384]{2,1,0:T(8,128)(2,1)S(1)}, bf16[1,1024,384]{2,1,0:T(8,128)(2,1)}, u32[]{:S(2)}) copy-start(bf16[1,1024,384]{2,1,0:T(8,128)(2,1)} %gate_ref.1) | copy-start | bytes 2359300
  47.0 26.0 %copy-start.4 = (bf16[1,1024,384]{2,1,0:T(8,128)(2,1)S(1)}, bf16[1,1024,384]{2,1,0:T(8,128)(2,1)}, u32[]{:S(2)}) copy-start(bf16[1,1024,384]{2,1,0:T(8,128)(2,1)} %up_ref.1) | copy-start | bytes 2359300
  72.9 2.6 %copy-start = (bf16[1,384,1024]{2,1,0:T(8,128)(2,1)S(1)}, bf16[1,384,1024]{2,1,0:T(8,128)(2,1)}, u32[]{:S(2)}) copy-start(bf16[1,384,1024]{2,1,0:T(8,128)(2,1)} %down_ref.3) | copy-start | bytes 2359300
  74.3 2.8 %collective-permute-start.2 = (bf16[768,384]{1,0:T(8,128)(2,1)S(1)}, bf16[768,384]{1,0:T(8,128)(2,1)S(1)}, u32[]{:S(2)}, u32[]{:S(2)}) collective-permute-start(bf16[768,384]{1,0:T(8,128)(2,1)S(1)} %shard_map.88.hidden_ref), channel_id=1, source_target_pairs={{0,128},{128,0},{1,129},{129,1},{2,130},{130,2},{3,131},{131,3},{4... | collective-permute-start | bytes 1769480 | tf_op jit(solution)/shard_map/ppermute | solution.py:333
  78.6 27.6 %all-to-all-start.2 = ((bf16[32,24,1024]{2,1,0:T(8,128)(2,1)}), bf16[32,24,1024]{2,1,0:T(8,128)(2,1)S(1)}, u32[]{:S(2)}, u32[]{:S(2)}) async-start(bf16[32,24,1024]{2,1,0:T(8,128)(2,1)} %bitcast.5), calls=%async_computation.2 | async-start | bytes 3145728 | tf_op jit(solution)/shard_map/all_to_all | solution.py:285
  88.1 1.4 %copy-start.2 = (bf16[640,1152]{1,0:T(8,128)(2,1)S(1)}, bf16[640,1152]{1,0:T(8,128)(2,1)}, u32[]{:S(2)}) copy-start(bf16[640,1152]{1,0:T(8,128)(2,1)} %copy-done.1) | copy-start | bytes 4423684
  89.5 0.9 copy-start.5
  107.2 8.0 %collective-permute-start.3 = (bf16[128,512]{1,0:T(8,128)(2,1)S(1)}, bf16[128,512]{1,0:T(8,128)(2,1)S(1)}, u32[]{:S(2)}, u32[]{:S(2)}) collective-permute-start(bf16[128,512]{1,0:T(8,128)(2,1)S(1)} %get-tuple-element.30), channel_id=1, source_target_pairs={{0,4},{1,5},{2,6},{3,7},{4,0},{5,1},{6,2},{7,3},{8,12},{9,13},{10,... | collective-permute-start | bytes 393224 | tf_op jit(solution)/shard_map/ppermute | solution.py:355
  109.0 10.9 %collective-permute-start.4 = (bf16[128,512]{1,0:T(8,128)(2,1)S(1)}, bf16[128,512]{1,0:T(8,128)(2,1)S(1)}, u32[]{:S(2)}, u32[]{:S(2)}) collective-permute-start(bf16[128,512]{1,0:T(8,128)(2,1)S(1)} %get-tuple-element.31), channel_id=1, source_target_pairs={{0,2},{1,3},{2,4},{3,5},{4,6},{5,7},{6,0},{7,1},{8,10},{9,11},{10,... | collective-permute-start | bytes 393224 | tf_op jit(solution)/shard_map/ppermute | solution.py:355
  111.1 13.1 %collective-permute-start.5 = (bf16[128,512]{1,0:T(8,128)(2,1)S(1)}, bf16[128,512]{1,0:T(8,128)(2,1)S(1)}, u32[]{:S(2)}, u32[]{:S(2)}) collective-permute-start(bf16[128,512]{1,0:T(8,128)(2,1)S(1)} %get-tuple-element.32), channel_id=1, source_target_pairs={{0,6},{1,7},{2,0},{3,1},{4,2},{5,3},{6,4},{7,5},{8,14},{9,15},{10,... | collective-permute-start | bytes 393224 | tf_op jit(solution)/shard_map/ppermute | solution.py:355

commit v6 on v5

v6 whole, which is shorter than its diff:
```python
import jax
import jax.numpy as jnp
from jax import lax
from jax.experimental import pallas as pl
from jax.experimental.pallas import tpu as pltpu
from jax.sharding import PartitionSpec as P

F32 = jnp.float32
BF16 = jnp.bfloat16
I32 = jnp.int32
EP_FIRST = 112
REGION_FIRST = 21
EP = [[(r + EP_FIRST) % 128 for r in range(128)]]
REGIONS = [
    [(i & 15) * 8 + zp * 2 + (i >> 4) for i in ((r + REGION_FIRST) % 32 for r in range(32))]
    for zp in range(4)
]
SWAP = [(0, 1), (1, 0)]
VMEM = pl.BlockSpec(memory_space=pltpu.VMEM)
HBM = pl.BlockSpec(memory_space=pltpu.HBM)
PARAMS = pltpu.CompilerParams(vmem_limit_bytes=16 * 1024 * 1024)


def my_zp():
    return (lax.axis_index("ep") >> 1) & 3


def iota(shape, dim):
    return lax.broadcasted_iota(I32, shape, dim)


def dot(a, b):
    return jnp.dot(a, b, preferred_element_type=F32)


def dot_nt(a, b):
    return lax.dot_general(a, b, (((1,), (1,)), ((), ())), preferred_element_type=F32)


def dot_tn(a, b):
    return lax.dot_general(a, b, (((0,), (0,)), ((), ())), preferred_element_type=F32)


def quantize(x_ref, out_ref):
    rows = x_ref.shape[0]
    r = iota((128, 128), 0)
    lane = iota((128, 128), 1)
    compact = jnp.zeros((rows, 128), F32)
    for b in range(8):
        largest = jnp.abs(x_ref[:, pl.ds(b * 128, 128)].astype(F32))
        for step in (16, 8, 4, 2, 1):
            largest = jnp.maximum(largest, pltpu.roll(largest, 128 - step, 1))
        first = (lane == r + b) & ((r & 31) == 0)
        compact = compact + dot(largest.astype(BF16), first.astype(F32).astype(BF16))
    power = jnp.full(compact.shape, 2.0**-31, F32)
    inverse = jnp.full(compact.shape, 2.0**31, F32)
    for step in (32, 16, 8, 4, 2, 1):
        larger = power * 2.0**step
        below = larger * 448.0 < compact
        power = jnp.where(below, larger, power)
        inverse = jnp.where(below, inverse * 2.0**-step, inverse)
    spacing = (jnp.minimum(power * 2.0, 16.0) * 2.0**-9).astype(BF16)
    inverse = (jnp.maximum(inverse * 0.5, 0.0625) * 2.0**9).astype(BF16)
    for b in range(8):
        lanes = pl.ds(b * 128, 128)
        spread = (r == (lane & 96) + b).astype(F32).astype(BF16)
        x = x_ref[:, lanes].astype(F32)
        size = jnp.abs(x) * 0.125
        level = dot(spacing, spread)
        over = dot(inverse, spread)
        for step in (8, 4, 2, 1):
            larger = level * 2.0**step
            reached = larger <= size
            level = jnp.where(reached, larger, level)
            over = jnp.where(reached, over * 2.0**-step, over)
        out_ref[:, lanes] = (jnp.floor(x * over + 0.5) * level).astype(BF16)


def halves():
    core = lax.axis_index("group")
    mine = pl.ds(pl.multiple_of(core * 512, 512), 512)
    other = pl.ds(pl.multiple_of((1 - core) * 512, 512), 512)
    return mine, other


def project_kernel(x_ref, owner_ref, w_hbm, give_ref, keep_ref, restored, weight, sem):
    copy = pltpu.make_async_copy(w_hbm, weight, sem)
    copy.start()
    quantize(x_ref, restored)
    core = lax.axis_index("group")
    n = iota((128, 128), 0)
    half = jnp.where(n < 64, 1 - core, core)
    owner = ((((n & 63) >> 2) * 4 + half * 2 + (n & 1)) << 1) + ((n >> 1) & 1)
    chosen = (owner_ref[...] == owner).astype(F32).astype(BF16)
    rows = dot(chosen, restored[...]).astype(BF16)
    copy.wait()
    both = dot(rows, weight[...])
    give_ref[...] = both[0:64]
    keep_ref[...] = both[64:128]


def by24(n):
    return (n * 2731) >> 16


def prepare_kernel(chosen_ref, order_ref):
    a = iota((256, 64), 0)
    e = ((a >> 1) + EP_FIRST) & 127
    chosen = iota((256, 64), 1) == (((e >> 3) << 1) + (e & 1)) * 2 + (a & 1)
    chosen_ref[...] = chosen.astype(F32).astype(BF16)
    a = iota((256, 256), 0)
    source = (((a >> 1) & 7) << 5) + ((a >> 4) << 1) + (a & 1)
    order_ref[...] = (iota((256, 256), 1) == source).astype(F32).astype(BF16)


def spread_kernel(keep_ref, got_ref, chosen_ref, order_ref, out_ref):
    projected = (keep_ref[...] + got_ref[...]).astype(BF16)
    rows = dot(chosen_ref[...], projected).astype(BF16)
    order = order_ref[...]
    for g in range(8):
        part = rows[g * 32 : (g + 1) * 32]
        stack = jnp.concatenate([part[:, f * 128 : (f + 1) * 128] for f in range(8)], axis=0)
        out_ref[pl.ds(g * 256, 256), :] = dot(order, stack).astype(BF16)


def expand_matrix(zp):
    e = (by24(iota((768, 128), 0)) + REGION_FIRST) & 31
    return (iota((768, 128), 1) == ((e & 15) << 3) + zp * 2 + (e >> 4)).astype(BF16)


def item_code(n):
    r = n - by24(n) * 24
    return jnp.where(r < 12, r, r + 4).astype(F32)


def setup_kernel(order_ref, expand_ref):
    a = iota((256, 256), 0)
    order_ref[...] = (iota((256, 256), 1) == ((a & 15) << 4) + (a >> 4)).astype(F32).astype(BF16)
    expand_ref[:, 0:128] = expand_matrix(my_zp())
    taken = item_code(iota((768, 128), 0))
    expand_ref[:, 128:256] = jnp.where(iota((768, 128), 1) == 0, -taken, 0.0).astype(BF16)


def dispatch_kernel(
    own_ref, order_ref, expand_ref, ids_ref, ids_got_ref, send_ref, normed_ref, rows, pick
):
    core = lax.axis_index("group")
    zp = my_zp()
    expert = iota((128, 128), 0)
    earlier = (expert < iota((128, 128), 1)).astype(F32).astype(BF16)
    expand = expand_ref[...]
    ones = jnp.ones((128, 128), BF16)
    for member in range(2):
        k = (zp + 4 - core * 2 - member) & 3
        ids = jnp.where(core == 1, ids_ref[k], ids_got_ref[k])
        named = expert == ids[0:1, :]
        for t in range(1, 8):
            named = named | (expert == ids[t : t + 1, :])
        rank = dot(named.astype(F32).astype(BF16), earlier)
        code = jnp.where(named, rank + 16.0 * member, -1.0)
        normed_ref[pl.ds(member * 128, 128), 1024:1152] = code.T.astype(BF16)
        found = dot(expand, jnp.concatenate([code.astype(BF16), ones], axis=0))
        pick[:, pl.ds(member * 128, 128)] = (found == 0.0).astype(F32).astype(BF16)
    order = order_ref[...]
    for g in range(8):
        slots = (g * 16 + EP_FIRST) % 128
        part = dot(order, own_ref[pl.ds(g * 256, 256), :]).astype(BF16)
        for f in range(8):
            for member in range(2):
                first = (f * 2 + member) * 16
                rows[pl.ds(member * 128 + slots, 16), pl.ds(f * 128, 128)] = part[first : first + 16]
    for member in range(2):
        at = pl.ds(member * 128, 128)
        value = rows[at, :].astype(F32)
        inverse = lax.rsqrt(jnp.mean(value * value, axis=1, keepdims=True) + 1e-06)
        normed_ref[at, 0:1024] = (value * inverse).astype(BF16)
    for part in range(2):
        at = pl.ds(part * 384, 384)
        send_ref[at, :] = dot(pick[at, :], normed_ref[0:256, 0:1024]).astype(BF16)
    normed_ref[256:384, 0:1024] = rows[pl.ds(pl.multiple_of((zp & 1) * 128, 128), 128), :]


def gate_kernel(normed_ref, router_ref, mix_ref):
    mix_ref[256:384, :] = normed_ref[256:384, 0:1024]
    expand = expand_matrix(my_zp())
    wanted = item_code(iota((128, 768), 1))
    for member in range(2):
        at = pl.ds(member * 128, 128)
        code = normed_ref[at, 1024:1152]
        logits = dot(normed_ref[at, 0:1024], router_ref[...])
        weights = jnp.where(code.astype(F32) >= 0.0, jnp.exp(logits), 0.0)
        gates = weights / jnp.sum(weights, axis=1, keepdims=True)
        found = dot_nt(code, expand)
        spread = dot_nt(gates.astype(BF16), expand)
        mix_ref[at, 0:768] = jnp.where(found == wanted, spread, 0.0).astype(BF16)


def expert_kernel(x_ref, gate_ref, up_ref, down_ref, out_hbm, hidden, stage, sems):
    x = x_ref[...]

    def act(gate, up):
        return (gate / (1.0 + jnp.exp(-gate)) * up).astype(BF16)

    hidden[:, 0:256] = act(dot(x, gate_ref[0, :, 0:256]), dot(x, up_ref[0, :, 0:256]))
    last = jnp.concatenate([gate_ref[0, :, 256:384], up_ref[0, :, 256:384]], axis=1)
    both = dot(x, last)
    hidden[:, 256:384] = act(both[:, 0:128], both[:, 128:256])
    copies = []
    for i in range(4):
        lanes = pl.ds(i * 256, 256)
        stage[:, lanes] = dot(hidden[...], down_ref[0, :, lanes]).astype(BF16)
        copies.append(pltpu.make_async_copy(stage.at[:, lanes], out_hbm.at[:, lanes], sems.at[i]))
        copies[-1].start()
    for copy in copies:
        copy.wait()


def mix_kernel(mix_ref, back_ref, two_ref, one_ref, three_ref, own_ref, total):
    zp = my_zp()
    total[...] = dot(mix_ref[0:256, 0:768], back_ref[...])
    for k, ref in ((2, two_ref), (1, one_ref), (3, three_ref), (0, own_ref)):
        value = total[pl.ds(pl.multiple_of(((zp + k) & 1) * 128, 128), 128), :]
        if k == 0:
            value = value + mix_ref[256:384, :].astype(F32)
        ref[...] = value.astype(ref.dtype)


def sum_kernel(own_ref, two_ref, one_ref, three_ref, mine_ref, other_ref):
    for ref, lanes in zip((other_ref, mine_ref), halves()[::-1]):
        total = own_ref[:, lanes] + two_ref[:, lanes].astype(F32)
        total = total + one_ref[:, lanes].astype(F32)
        ref[...] = (total + three_ref[:, lanes].astype(F32)).astype(BF16)


def call(kernel, outs, ins, scratch=(), specs=None, out_spec=VMEM):
    return pl.pallas_call(
        kernel,
        out_shape=[jax.ShapeDtypeStruct(shape, dtype) for shape, dtype in outs],
        in_specs=specs or [VMEM] * len(ins),
        out_specs=[out_spec] * len(outs),
        scratch_shapes=list(scratch),
        compiler_params=PARAMS,
    )(*ins)


def pinned(x):
    return pltpu.with_memory_space_constraint(x, pltpu.HBM)


def further(i, k):
    return (i & ~7) + ((i + 2 * k) & 7)


def send_to(x, pairs):
    return lax.ppermute(x, ("group", "ep"), [(a * 128 + i, b * 128 + j) for (a, i), (b, j) in pairs])


def exchange(x, groups):
    return lax.all_to_all(x, "ep", 0, 0, axis_index_groups=groups, tiled=True)


def body(
    thinker_rows,
    owner_map,
    talker_ids,
    project_weight,
    router_weight,
    expert_gate,
    expert_up,
    expert_down,
):
    chips = range(128)
    give, keep = call(
        project_kernel,
        [((64, 1024), F32)] * 2,
        (pinned(thinker_rows), pinned(owner_map.reshape(1, 128)), pinned(project_weight)),
        [pltpu.VMEM((128, 1024), BF16), pltpu.VMEM((1024, 1024), BF16), pltpu.SemaphoreType.DMA],
        [VMEM, VMEM, HBM],
    )
    got = lax.ppermute(give, "group", SWAP)
    chosen, order = call(prepare_kernel, [((256, 64), BF16), ((256, 256), BF16)], ())
    (sent,) = call(spread_kernel, [((2048, 128), BF16)], (keep, got, chosen, order))
    own_ids = talker_ids.T
    ids = [own_ids]
    for k in (1, 2, 3):
        ids.append(send_to(own_ids, [((1, i), (1, further(i, k))) for i in chips]))
    ids = jnp.stack(ids)
    sent, ids = lax.optimization_barrier((sent, ids))
    own = exchange(sent.reshape(128, 16, 128), EP)
    got_ids = send_to(ids, [((1, i), (0, i)) for i in chips])
    own, got_ids = lax.optimization_barrier((own, got_ids))
    order, expand = call(setup_kernel, [((256, 256), BF16), ((768, 256), BF16)], ())
    send, normed = call(
        dispatch_kernel,
        [((768, 1024), BF16), ((384, 1152), BF16)],
        (own.reshape(2048, 128), order, expand, ids, got_ids),
        [pltpu.VMEM((256, 1024), BF16), pltpu.VMEM((768, 256), BF16)],
    )
    items = exchange(send.reshape(32, 24, 1024), REGIONS)
    (mix,) = call(gate_kernel, [((384, 1024), BF16)], (normed, router_weight))
    (expert_out,) = call(
        expert_kernel,
        [((768, 1024), BF16)],
        (items.reshape(768, 1024), expert_gate, expert_up, expert_down),
        [
            pltpu.VMEM((768, 384), BF16),
            pltpu.VMEM((768, 1024), BF16),
            pltpu.SemaphoreType.DMA((4,)),
        ],
        out_spec=HBM,
    )
    back = exchange(expert_out.reshape(32, 24, 1024), REGIONS)
    two, one, three, total = call(
        mix_kernel,
        [((128, 1024), BF16)] * 3 + [((128, 1024), F32)],
        (mix, back.reshape(768, 1024)),
        [pltpu.VMEM((256, 1024), F32)],
    )
    parts = []
    for k, part in ((2, two), (1, one), (3, three)):
        ends = [(i, further(i, k)) for i in chips]
        parts.append(send_to(part, [((j >> 2 & 1, i), (j >> 2 & 1, j)) for i, j in ends]))
    mine, other = call(sum_kernel, [((128, 512), BF16)] * 2, (total, *parts))
    swapped = send_to(other, [((i >> 2 & 1, i), (1 - (i >> 2 & 1), i)) for i in chips])
    return jnp.where(lax.axis_index("group") == my_zp() >> 1, mine, swapped)


def solution(mesh):
    return jax.shard_map(
        body,
        mesh=mesh,
        in_specs=(
            P("ep", "group"),
            P("ep", None),
            P("ep", None),
            P("group", None),
            P(),
            P("ep", None, None),
            P("ep", None, None),
            P("ep", None, None),
        ),
        out_specs=P("ep", "group"),
        check_vma=False,
    )
```

time: 125 us -> 121 us (0.968)
  blocking collectives: 58 us -> 19.8 us
  starting transfers between devices: 21.6 us -> 54.1 us
  waiting for transfers between devices: 27.5 us -> 33.7 us
  local copies, waits for them, and re-layouts: 2.56 us -> 0.03 us
  Pallas kernels: 14.4 us -> 12.1 us
    all_to_all x2 -> x1, blocking collectives: 58 us -> 19.8 us  [exchange(): return lax.all_to_all(x, 'ep', 0, 0, axis_index_groups=groups, tiled=True)]
    ppermute x5 -> x8, starting transfers between devices: 8.78 us -> 31.7 us  [send_to(): lax.ppermute(x, ('group', 'ep'), [(a * 128 + i, b * 128 + j) for (a, i),...]
    all_to_all x1 -> x2, starting transfers between devices: 9.53 us -> 19 us  [exchange(): return lax.all_to_all(x, 'ep', 0, 0, axis_index_groups=groups, tiled=True)]
    all_to_all x1 -> x2, waiting for transfers between devices: 14.1 us -> 21 us  [exchange(): return lax.all_to_all(x, 'ep', 0, 0, axis_index_groups=groups, tiled=True)]
    unnamed x18 -> x10, local copies, waits for them, and re-layouts: 2.56 us -> 0.03 us
    pallas_call x10 -> x9, Pallas kernels: 14.4 us -> 12.1 us  [call(): pl.pallas_call(kernel, out_shape=[jax.ShapeDtypeStruct(shape, dtype) for...]
    ppermute x5 -> x8, waiting for transfers between devices: 12.6 us -> 12.7 us  [send_to(): lax.ppermute(x, ('group', 'ep'), [(a * 128 + i, b * 128 + j) for (a, i),...]
  transfers between devices with their start and end apart: 7 -> 11, of which waited for: 7 -> 8; matrix products, arithmetic and copies ran while one was open for 0% -> 0% of each run, Pallas kernels for 3% -> 1%
where the time goes in v6:
time: 121 us; the launch traced here: 120 us
  starting transfers between devices  54.1 us (45%)
  waiting for transfers between devices  33.7 us (28%)
  blocking collectives  19.8 us (16%)
  Pallas kernels  12.1 us (10%)
    ppermute x8, starting transfers between devices, send_to(): lax.ppermute(x, ('group', 'ep'), [(a * 128 + i, b * 128 + j) for (a, i),...  31.7 us
    all_to_all x2, waiting for transfers between devices, exchange(): return lax.all_to_all(x, 'ep', 0, 0, axis_index_groups=groups, tiled=True)  21 us
    all_to_all x1, blocking collectives, exchange(): return lax.all_to_all(x, 'ep', 0, 0, axis_index_groups=groups, tiled=True)  19.8 us
    all_to_all x2, starting transfers between devices, exchange(): return lax.all_to_all(x, 'ep', 0, 0, axis_index_groups=groups, tiled=True)  19 us
    ppermute x8, waiting for transfers between devices, send_to(): lax.ppermute(x, ('group', 'ep'), [(a * 128 + i, b * 128 + j) for (a, i),...  12.7 us
    pallas_call x9, Pallas kernels, call(): pl.pallas_call(kernel, out_shape=[jax.ShapeDtypeStruct(shape, dtype) for...  12.1 us
    ppermute x1, starting transfers between devices, body(): got = lax.ppermute(give, 'group', SWAP)  3.33 us
  transfers between devices with their start and end apart: 11, of which 8 were waited for; matrix products, arithmetic and copies ran while one was open for 0% of the time, Pallas kernels for 1%

profile of v6, /device:TPU:1, one launch (start us, length us, event | category | flops | bytes accessed | tf_op | source)
XLA Modules:
  0.0 120.5 jit_solution(7063188611088238497)
XLA Ops:
  0.0 0.0 copy-start.4
  0.0 3.1 %shard_map.82 = (f32[64,1024]{1,0:T(8,128)S(1)}, f32[64,1024]{1,0:T(8,128)S(1)}) custom-call(bf16[128,1024]{1,0:T(8,128)(2,1)} %x_ref.1, s32[1,128]{1,0:T(1,128)} %bitcast.24, bf16[1024,1024]{1,0:T(8,128)(2,1)} %w_hbm.1), custom_call_target="tpu_custom_call" | custom-call | tf_op jit(solution)/shard_map/pallas_call | solution.py:236
  3.2 3.3 %collective-permute-start = (f32[64,1024]{1,0:T(8,128)S(1)}, f32[64,1024]{1,0:T(8,128)S(1)}, u32[]{:S(2)}, u32[]{:S(2)}) collective-permute-start(f32[64,1024]{1,0:T(8,128)S(1)} %get-tuple-element.24), channel_id=1, source_target_pairs={{0,128},{128,0},{1,129},{129,1},{2,130},{130,2},{3,131},{131,3},{4... | collective-permute-start | bytes 786440 | tf_op jit(solution)/shard_map/ppermute | solution.py:280
  6.5 0.0 copy-done.4
  6.5 6.2 %collective-permute-start.3 = (s32[8,128]{1,0:T(8,128)S(1)}, s32[8,128]{1,0:T(8,128)S(1)}, u32[]{:S(2)}, u32[]{:S(2)}) collective-permute-start(s32[8,128]{1,0:T(8,128)S(1)} %bitcast.17), channel_id=1, source_target_pairs={{128,134},{129,135},{130,128},{131,129},{132,130},{133,131},{134,1... | collective-permute-start | bytes 12296 | tf_op jit(solution)/shard_map/ppermute | solution.py:255
  12.7 2.8 %collective-permute-start.2 = (s32[8,128]{1,0:T(8,128)S(1)}, s32[8,128]{1,0:T(8,128)S(1)}, u32[]{:S(2)}, u32[]{:S(2)}) collective-permute-start(s32[8,128]{1,0:T(8,128)S(1)} %bitcast.18), channel_id=1, source_target_pairs={{128,132},{129,133},{130,134},{131,135},{132,128},{133,129},{134,1... | collective-permute-start | bytes 12296 | tf_op jit(solution)/shard_map/ppermute | solution.py:255
  15.5 4.3 %collective-permute-start.1 = (s32[8,128]{1,0:T(8,128)S(1)}, s32[8,128]{1,0:T(8,128)S(1)}, u32[]{:S(2)}, u32[]{:S(2)}) collective-permute-start(s32[8,128]{1,0:T(8,128)S(1)} %bitcast.19), channel_id=1, source_target_pairs={{128,130},{129,131},{130,132},{131,133},{132,134},{133,135},{134,1... | collective-permute-start | bytes 12296 | tf_op jit(solution)/shard_map/ppermute | solution.py:255
  19.8 0.1 shard_map.83
  19.9 0.0 collective-permute-done.3
  19.9 1.0 collective-permute-done.2
  20.9 1.0 collective-permute-done.1
  22.0 0.0 collective-permute-done.got_ref
  22.0 1.4 %shard_map.84 = bf16[2048,128]{1,0:T(8,128)(2,1)} custom-call(f32[64,1024]{1,0:T(8,128)S(1)} %get-tuple-element.23.keep_ref, f32[64,1024]{1,0:T(8,128)S(1)} %collective-permute-done.got_ref, bf16[256,64]{1,0:T(8,128)(2,1)S(1)} %get-tuple-element.25.chosen_ref, bf16[256,256]{1,0:T(8,128)(2,1)S(1)} %get-tuple-element.26.order_ref), custom_call_target="tpu_custom_call" | custom-call | tf_op jit(solution)/shard_map/pallas_call | solution.py:236
  23.4 14.1 %all-to-all-start = ((bf16[128,16,128]{2,1,0:T(8,128)(2,1)}), bf16[128,16,128]{2,1,0:T(8,128)(2,1)S(1)}, u32[]{:S(2)}, u32[]{:S(2)}) async-start(bf16[128,16,128]{2,1,0:T(8,128)(2,1)} %bitcast.6), calls=%async_computation | async-start | bytes 1048576 | tf_op jit(solution)/shard_map/all_to_all | solution.py:259
  37.5 1.3 %collective-permute-start.4 = (s32[4,8,128]{2,1,0:T(8,128)S(1)}, s32[4,8,128]{2,1,0:T(8,128)S(1)}, u32[]{:S(2)}, u32[]{:S(2)}) collective-permute-start(s32[4,8,128]{2,1,0:T(8,128)S(1)} %pad_add_fusion.ids_ref), channel_id=1, source_target_pairs={{128,0},{129,1},{130,2},{131,3},{132,4},{133,5},{134,6},{135,7},{1... | collective-permute-start | bytes 49160 | tf_op jit(solution)/shard_map/ppermute | solution.py:255
  38.8 0.4 shard_map.85
  39.1 0.5 collective-permute-done.4.ids_got_ref
  39.6 8.8 %all-to-all-done = bf16[128,16,128]{2,1,0:T(8,128)(2,1)S(1)} async-done(((bf16[128,16,128]{2,1,0:T(8,128)(2,1)}), bf16[128,16,128]{2,1,0:T(8,128)(2,1)S(1)}, u32[]{:S(2)}, u32[]{:S(2)}) %all-to-all-start) | async-done | bytes 524320 | tf_op jit(solution)/shard_map/all_to_all | solution.py:259
  48.4 1.6 %shard_map.86 = (bf16[768,1024]{1,0:T(8,128)(2,1)S(1)}, bf16[384,1152]{1,0:T(8,128)(2,1)S(1)}) custom-call(bf16[2048,128]{1,0:T(8,128)(2,1)S(1)} %bitcast.15, bf16[256,256]{1,0:T(8,128)(2,1)S(1)} %get-tuple-element.30.order_ref, bf16[768,256]{1,0:T(8,128)(2,1)S(1)} %get-tuple-element.31.expand_ref, s32[4,8,128]{2,1,0:T(8,128)S(1)} %pad_add_fusion.ids_ref, ...), custom_call_target="tpu_custom_call" | custom-call | tf_op jit(solution)/shard_map/pallas_call | solution.py:236
  50.0 0.0 copy-start
  50.0 0.0 copy-start.1
  50.1 0.0 copy-start.2
  50.1 19.8 %all_to_all.15 = bf16[32,24,1024]{2,1,0:T(8,128)(2,1)S(1)} all-to-all(bf16[32,24,1024]{2,1,0:T(8,128)(2,1)S(1)} %bitcast.16), channel_id=1, replica_groups={{41,49,57,65,73,81,89,97,105,113,121,0,8,16,24,32,40,48,56,64,72,80,88,..., dimensions={0} | all-to-all | bytes 3145728 | tf_op jit(solution)/shard_map/all_to_all | solution.py:259
  69.8 0.0 copy-done
  69.8 0.0 copy-done.1
  69.9 0.0 copy-done.2
  69.9 3.7 %shard_map.88 = bf16[768,1024]{1,0:T(8,128)(2,1)} custom-call(bf16[768,1024]{1,0:T(8,128)(2,1)S(1)} %bitcast.14, bf16[1,1024,384]{2,1,0:T(8,128)(2,1)S(1)} %copy-done, bf16[1,1024,384]{2,1,0:T(8,128)(2,1)S(1)} %copy-done.1, bf16[1,384,1024]{2,1,0:T(8,128)(2,1)S(1)} %copy-done.2), custom_call_target="tpu_custom_call" | custom-call | tf_op jit(solution)/shard_map/pallas_call | solution.py:236
  73.5 0.0 copy-start.3
  73.6 5.0 %all-to-all-start.2 = ((bf16[32,24,1024]{2,1,0:T(8,128)(2,1)}), bf16[32,24,1024]{2,1,0:T(8,128)(2,1)S(1)}, u32[]{:S(2)}, u32[]{:S(2)}) async-start(bf16[32,24,1024]{2,1,0:T(8,128)(2,1)} %bitcast.10), calls=%async_computation.2 | async-start | bytes 3145728 | tf_op jit(solution)/shard_map/all_to_all | solution.py:259
  78.5 0.0 copy-done.3
  78.6 0.9 shard_map.87.mix_ref
  79.4 12.1 %all-to-all-done.2 = bf16[32,24,1024]{2,1,0:T(8,128)(2,1)S(1)} async-done(((bf16[32,24,1024]{2,1,0:T(8,128)(2,1)}), bf16[32,24,1024]{2,1,0:T(8,128)(2,1)S(1)}, u32[]{:S(2)}, u32[]{:S(2)}) %all-to-all-start.2) | async-done | bytes 1572896 | tf_op jit(solution)/shard_map/all_to_all | solution.py:259
  91.6 0.8 shard_map.89
  92.3 13.9 %collective-permute-start.5 = (bf16[128,1024]{1,0:T(8,128)(2,1)S(1)}, bf16[128,1024]{1,0:T(8,128)(2,1)S(1)}, u32[]{:S(2)}, u32[]{:S(2)}) collective-permute-start(bf16[128,1024]{1,0:T(8,128)(2,1)S(1)} %get-tuple-element.36), channel_id=1, source_target_pairs={{128,132},{129,133},{130,134},{131,135},{4,0},{5,1},{6,2},{7,3},{1... | collective-permute-start | bytes 786440 | tf_op jit(solution)/shard_map/ppermute | solution.py:255
  106.2 0.7 collective-permute-start.6
  106.9 1.3 %collective-permute-start.7 = (bf16[128,1024]{1,0:T(8,128)(2,1)S(1)}, bf16[128,1024]{1,0:T(8,128)(2,1)S(1)}, u32[]{:S(2)}, u32[]{:S(2)}) collective-permute-start(bf16[128,1024]{1,0:T(8,128)(2,1)S(1)} %get-tuple-element.38), channel_id=1, source_target_pairs={{128,134},{129,135},{2,0},{3,1},{4,2},{5,3},{134,132},{135,133},{1... | collective-permute-start | bytes 786440 | tf_op jit(solution)/shard_map/ppermute | solution.py:255
  108.2 3.5 %collective-permute-done.5.two_ref = bf16[128,1024]{1,0:T(8,128)(2,1)S(1)} collective-permute-done((bf16[128,1024]{1,0:T(8,128)(2,1)S(1)}, bf16[128,1024]{1,0:T(8,128)(2,1)S(1)}, u32[]{:S(2)}, u32[]{:S(2)}) %collective-permute-start.5) | collective-permute-done | bytes 262176 | tf_op jit(solution)/shard_map/ppermute | solution.py:255
  111.8 0.0 collective-permute-done.6.one_ref
  111.8 4.7 %collective-permute-done.7.three_ref = bf16[128,1024]{1,0:T(8,128)(2,1)S(1)} collective-permute-done((bf16[128,1024]{1,0:T(8,128)(2,1)S(1)}, bf16[128,1024]{1,0:T(8,128)(2,1)S(1)}, u32[]{:S(2)}, u32[]{:S(2)}) %collective-permute-start.7) | collective-permute-done | bytes 262176 | tf_op jit(solution)/shard_map/ppermute | solution.py:255
  116.5 0.1 shard_map.90
  116.6 1.3 %collective-permute-start.8 = (bf16[128,512]{1,0:T(8,128)(2,1)S(1)}, bf16[128,512]{1,0:T(8,128)(2,1)S(1)}, u32[]{:S(2)}, u32[]{:S(2)}) collective-permute-start(bf16[128,512]{1,0:T(8,128)(2,1)S(1)} %get-tuple-element.40), channel_id=1, source_target_pairs={{0,128},{1,129},{2,130},{3,131},{132,4},{133,5},{134,6},{135,7},{8... | collective-permute-start | bytes 393224 | tf_op jit(solution)/shard_map/ppermute | solution.py:255
  117.9 1.9 %collective-permute-done.8 = bf16[128,512]{1,0:T(8,128)(2,1)S(1)} collective-permute-done((bf16[128,512]{1,0:T(8,128)(2,1)S(1)}, bf16[128,512]{1,0:T(8,128)(2,1)S(1)}, u32[]{:S(2)}, u32[]{:S(2)}) %collective-permute-start.8) | collective-permute-done | bytes 131104 | tf_op jit(solution)/shard_map/ppermute | solution.py:255
  119.8 0.7 broadcast_select_fusion
  (1 shorter events, 0.0 us)
Async XLA Ops:
  0.0 6.5 %copy-start.4 = (s32[128,8]{0,1:T(8,128)S(1)}, s32[128,8]{0,1:T(8,128)}, u32[]{:S(2)}) copy-start(s32[128,8]{0,1:T(8,128)} %param.10) | copy-start | bytes 12292
  3.2 18.8 %collective-permute-start = (f32[64,1024]{1,0:T(8,128)S(1)}, f32[64,1024]{1,0:T(8,128)S(1)}, u32[]{:S(2)}, u32[]{:S(2)}) collective-permute-start(f32[64,1024]{1,0:T(8,128)S(1)} %get-tuple-element.24), channel_id=1, source_target_pairs={{0,128},{128,0},{1,129},{129,1},{2,130},{130,2},{3,131},{131,3},{4... | collective-permute-start | bytes 786440 | tf_op jit(solution)/shard_map/ppermute | solution.py:280
  6.5 13.4 %collective-permute-start.3 = (s32[8,128]{1,0:T(8,128)S(1)}, s32[8,128]{1,0:T(8,128)S(1)}, u32[]{:S(2)}, u32[]{:S(2)}) collective-permute-start(s32[8,128]{1,0:T(8,128)S(1)} %bitcast.17), channel_id=1, source_target_pairs={{128,134},{129,135},{130,128},{131,129},{132,130},{133,131},{134,1... | collective-permute-start | bytes 12296 | tf_op jit(solution)/shard_map/ppermute | solution.py:255
  12.7 8.3 %collective-permute-start.2 = (s32[8,128]{1,0:T(8,128)S(1)}, s32[8,128]{1,0:T(8,128)S(1)}, u32[]{:S(2)}, u32[]{:S(2)}) collective-permute-start(s32[8,128]{1,0:T(8,128)S(1)} %bitcast.18), channel_id=1, source_target_pairs={{128,132},{129,133},{130,134},{131,135},{132,128},{133,129},{134,1... | collective-permute-start | bytes 12296 | tf_op jit(solution)/shard_map/ppermute | solution.py:255
  15.5 6.5 %collective-permute-start.1 = (s32[8,128]{1,0:T(8,128)S(1)}, s32[8,128]{1,0:T(8,128)S(1)}, u32[]{:S(2)}, u32[]{:S(2)}) collective-permute-start(s32[8,128]{1,0:T(8,128)S(1)} %bitcast.19), channel_id=1, source_target_pairs={{128,130},{129,131},{130,132},{131,133},{132,134},{133,135},{134,1... | collective-permute-start | bytes 12296 | tf_op jit(solution)/shard_map/ppermute | solution.py:255
  23.4 25.0 %all-to-all-start = ((bf16[128,16,128]{2,1,0:T(8,128)(2,1)}), bf16[128,16,128]{2,1,0:T(8,128)(2,1)S(1)}, u32[]{:S(2)}, u32[]{:S(2)}) async-start(bf16[128,16,128]{2,1,0:T(8,128)(2,1)} %bitcast.6), calls=%async_computation | async-start | bytes 1048576 | tf_op jit(solution)/shard_map/all_to_all | solution.py:259
  37.5 2.1 %collective-permute-start.4 = (s32[4,8,128]{2,1,0:T(8,128)S(1)}, s32[4,8,128]{2,1,0:T(8,128)S(1)}, u32[]{:S(2)}, u32[]{:S(2)}) collective-permute-start(s32[4,8,128]{2,1,0:T(8,128)S(1)} %pad_add_fusion.ids_ref), channel_id=1, source_target_pairs={{128,0},{129,1},{130,2},{131,3},{132,4},{133,5},{134,6},{135,7},{1... | collective-permute-start | bytes 49160 | tf_op jit(solution)/shard_map/ppermute | solution.py:255
  50.0 19.8 %copy-start = (bf16[1,1024,384]{2,1,0:T(8,128)(2,1)S(1)}, bf16[1,1024,384]{2,1,0:T(8,128)(2,1)}, u32[]{:S(2)}) copy-start(bf16[1,1024,384]{2,1,0:T(8,128)(2,1)} %gate_ref.1) | copy-start | bytes 2359300
  50.0 19.8 %copy-start.1 = (bf16[1,1024,384]{2,1,0:T(8,128)(2,1)S(1)}, bf16[1,1024,384]{2,1,0:T(8,128)(2,1)}, u32[]{:S(2)}) copy-start(bf16[1,1024,384]{2,1,0:T(8,128)(2,1)} %up_ref.1) | copy-start | bytes 2359300
  50.1 19.8 %copy-start.2 = (bf16[1,384,1024]{2,1,0:T(8,128)(2,1)S(1)}, bf16[1,384,1024]{2,1,0:T(8,128)(2,1)}, u32[]{:S(2)}) copy-start(bf16[1,384,1024]{2,1,0:T(8,128)(2,1)} %down_ref.1) | copy-start | bytes 2359300
  73.5 5.0 %copy-start.3 = (bf16[1024,128]{1,0:T(8,128)(2,1)S(1)}, bf16[1024,128]{1,0:T(8,128)(2,1)}, u32[]{:S(2)}) copy-start(bf16[1024,128]{1,0:T(8,128)(2,1)} %router_ref.1) | copy-start | bytes 786436
  73.6 18.0 %all-to-all-start.2 = ((bf16[32,24,1024]{2,1,0:T(8,128)(2,1)}), bf16[32,24,1024]{2,1,0:T(8,128)(2,1)S(1)}, u32[]{:S(2)}, u32[]{:S(2)}) async-start(bf16[32,24,1024]{2,1,0:T(8,128)(2,1)} %bitcast.10), calls=%async_computation.2 | async-start | bytes 3145728 | tf_op jit(solution)/shard_map/all_to_all | solution.py:259
  92.3 19.4 %collective-permute-start.5 = (bf16[128,1024]{1,0:T(8,128)(2,1)S(1)}, bf16[128,1024]{1,0:T(8,128)(2,1)S(1)}, u32[]{:S(2)}, u32[]{:S(2)}) collective-permute-start(bf16[128,1024]{1,0:T(8,128)(2,1)S(1)} %get-tuple-element.36), channel_id=1, source_target_pairs={{128,132},{129,133},{130,134},{131,135},{4,0},{5,1},{6,2},{7,3},{1... | collective-permute-start | bytes 786440 | tf_op jit(solution)/shard_map/ppermute | solution.py:255
  106.2 5.6 %collective-permute-start.6 = (bf16[128,1024]{1,0:T(8,128)(2,1)S(1)}, bf16[128,1024]{1,0:T(8,128)(2,1)S(1)}, u32[]{:S(2)}, u32[]{:S(2)}) collective-permute-start(bf16[128,1024]{1,0:T(8,128)(2,1)S(1)} %get-tuple-element.37), channel_id=1, source_target_pairs={{0,2},{1,3},{130,132},{131,133},{132,134},{133,135},{6,0},{7,1},{8... | collective-permute-start | bytes 786440 | tf_op jit(solution)/shard_map/ppermute | solution.py:255
  106.9 9.6 %collective-permute-start.7 = (bf16[128,1024]{1,0:T(8,128)(2,1)S(1)}, bf16[128,1024]{1,0:T(8,128)(2,1)S(1)}, u32[]{:S(2)}, u32[]{:S(2)}) collective-permute-start(bf16[128,1024]{1,0:T(8,128)(2,1)S(1)} %get-tuple-element.38), channel_id=1, source_target_pairs={{128,134},{129,135},{2,0},{3,1},{4,2},{5,3},{134,132},{135,133},{1... | collective-permute-start | bytes 786440 | tf_op jit(solution)/shard_map/ppermute | solution.py:255
  116.6 3.2 %collective-permute-start.8 = (bf16[128,512]{1,0:T(8,128)(2,1)S(1)}, bf16[128,512]{1,0:T(8,128)(2,1)S(1)}, u32[]{:S(2)}, u32[]{:S(2)}) collective-permute-start(bf16[128,512]{1,0:T(8,128)(2,1)S(1)} %get-tuple-element.40), channel_id=1, source_target_pairs={{0,128},{1,129},{2,130},{3,131},{132,4},{133,5},{134,6},{135,7},{8... | collective-permute-start | bytes 393224 | tf_op jit(solution)/shard_map/ppermute | solution.py:255

commit v7 on v6

--- a/solution.py
+++ b/solution.py
@@ -287,13 +287,14 @@
     ids = jnp.stack(ids)
     sent, ids = lax.optimization_barrier((sent, ids))
     own = exchange(sent.reshape(128, 16, 128), EP)
-    got_ids = send_to(ids, [((1, i), (0, i)) for i in chips])
+    copies = lax.optimization_barrier(jnp.broadcast_to(ids[None], (64, 4, 8, 128)))
+    got_ids = send_to(copies, [((1, i), (0, i)) for i in chips])
     own, got_ids = lax.optimization_barrier((own, got_ids))
     order, expand = call(setup_kernel, [((256, 256), BF16), ((768, 256), BF16)], ())
     send, normed = call(
         dispatch_kernel,
         [((768, 1024), BF16), ((384, 1152), BF16)],
-        (own.reshape(2048, 128), order, expand, ids, got_ids),
+        (own.reshape(2048, 128), order, expand, ids, got_ids[0]),
         [pltpu.VMEM((256, 1024), BF16), pltpu.VMEM((768, 256), BF16)],
     )
     items = exchange(send.reshape(32, 24, 1024), REGIONS)

time: 121 us -> 113 us (0.934)
  starting transfers between devices: 54.1 us -> 44.3 us
  waiting for transfers between devices: 33.7 us -> 35.6 us
    ppermute x8, starting transfers between devices: 31.7 us -> 22.2 us  [send_to(): lax.ppermute(x, ('group', 'ep'), [(a * 128 + i, b * 128 + j) for (a, i),...]
  transfers between devices with their start and end apart: 11 -> 11, of which waited for: 8 -> 7; matrix products, arithmetic and copies ran while one was open for 0% -> 0% of each run, Pallas kernels for 1% -> 1%
where the time goes in v7:
time: 113 us
  starting transfers between devices  44.3 us (39%)
  waiting for transfers between devices  35.6 us (32%)
  blocking collectives  19.8 us (18%)
  Pallas kernels  12.1 us (11%)
    ppermute x8, starting transfers between devices, send_to(): lax.ppermute(x, ('group', 'ep'), [(a * 128 + i, b * 128 + j) for (a, i),...  22.2 us
    all_to_all x2, waiting for transfers between devices, exchange(): return lax.all_to_all(x, 'ep', 0, 0, axis_index_groups=groups, tiled=True)  22.1 us
    all_to_all x1, blocking collectives, exchange(): return lax.all_to_all(x, 'ep', 0, 0, axis_index_groups=groups, tiled=True)  19.8 us
    all_to_all x2, starting transfers between devices, exchange(): return lax.all_to_all(x, 'ep', 0, 0, axis_index_groups=groups, tiled=True)  18.8 us
    ppermute x8, waiting for transfers between devices, send_to(): lax.ppermute(x, ('group', 'ep'), [(a * 128 + i, b * 128 + j) for (a, i),...  13.5 us
    pallas_call x9, Pallas kernels, call(): pl.pallas_call(kernel, out_shape=[jax.ShapeDtypeStruct(shape, dtype) for...  12.1 us
    ppermute x1, starting transfers between devices, body(): got = lax.ppermute(give, 'group', SWAP)  3.33 us
  transfers between devices with their start and end apart: 11, of which 7 were waited for; matrix products, arithmetic and copies ran while one was open for 0% of the time, Pallas kernels for 1%

profile of v7, /device:TPU:1, one launch (start us, length us, event | category | flops | bytes accessed | tf_op | source)
XLA Modules:
  0.0 112.8 jit_solution(729479206415845011)
XLA Ops:
  0.0 0.0 copy-start.4
  0.0 3.1 %shard_map.82 = (f32[64,1024]{1,0:T(8,128)S(1)}, f32[64,1024]{1,0:T(8,128)S(1)}) custom-call(bf16[128,1024]{1,0:T(8,128)(2,1)} %x_ref.1, s32[1,128]{1,0:T(1,128)} %bitcast.26, bf16[1024,1024]{1,0:T(8,128)(2,1)} %w_hbm.1), custom_call_target="tpu_custom_call" | custom-call | tf_op jit(solution)/shard_map/pallas_call | solution.py:236
  3.2 3.3 %collective-permute-start = (f32[64,1024]{1,0:T(8,128)S(1)}, f32[64,1024]{1,0:T(8,128)S(1)}, u32[]{:S(2)}, u32[]{:S(2)}) collective-permute-start(f32[64,1024]{1,0:T(8,128)S(1)} %get-tuple-element.24), channel_id=1, source_target_pairs={{0,128},{128,0},{1,129},{129,1},{2,130},{130,2},{3,131},{131,3},{4... | collective-permute-start | bytes 786440 | tf_op jit(solution)/shard_map/ppermute | solution.py:280
  6.5 0.0 copy-done.4
  6.5 6.2 %collective-permute-start.3 = (s32[8,128]{1,0:T(8,128)S(1)}, s32[8,128]{1,0:T(8,128)S(1)}, u32[]{:S(2)}, u32[]{:S(2)}) collective-permute-start(s32[8,128]{1,0:T(8,128)S(1)} %bitcast.19), channel_id=1, source_target_pairs={{128,134},{129,135},{130,128},{131,129},{132,130},{133,131},{134,1... | collective-permute-start | bytes 12296 | tf_op jit(solution)/shard_map/ppermute | solution.py:255
  12.7 2.8 %collective-permute-start.2 = (s32[8,128]{1,0:T(8,128)S(1)}, s32[8,128]{1,0:T(8,128)S(1)}, u32[]{:S(2)}, u32[]{:S(2)}) collective-permute-start(s32[8,128]{1,0:T(8,128)S(1)} %bitcast.20), channel_id=1, source_target_pairs={{128,132},{129,133},{130,134},{131,135},{132,128},{133,129},{134,1... | collective-permute-start | bytes 12296 | tf_op jit(solution)/shard_map/ppermute | solution.py:255
  15.5 4.3 %collective-permute-start.1 = (s32[8,128]{1,0:T(8,128)S(1)}, s32[8,128]{1,0:T(8,128)S(1)}, u32[]{:S(2)}, u32[]{:S(2)}) collective-permute-start(s32[8,128]{1,0:T(8,128)S(1)} %bitcast.21), channel_id=1, source_target_pairs={{128,130},{129,131},{130,132},{131,133},{132,134},{133,135},{134,1... | collective-permute-start | bytes 12296 | tf_op jit(solution)/shard_map/ppermute | solution.py:255
  19.8 0.1 shard_map.83
  19.9 0.0 collective-permute-done.3
  19.9 1.0 collective-permute-done.2
  20.9 1.0 collective-permute-done.1
  22.0 0.0 collective-permute-done.got_ref
  22.0 1.4 %shard_map.84 = bf16[2048,128]{1,0:T(8,128)(2,1)} custom-call(f32[64,1024]{1,0:T(8,128)S(1)} %get-tuple-element.23.keep_ref, f32[64,1024]{1,0:T(8,128)S(1)} %collective-permute-done.got_ref, bf16[256,64]{1,0:T(8,128)(2,1)S(1)} %get-tuple-element.25.chosen_ref, bf16[256,256]{1,0:T(8,128)(2,1)S(1)} %get-tuple-element.26.order_ref), custom_call_target="tpu_custom_call" | custom-call | tf_op jit(solution)/shard_map/pallas_call | solution.py:236
  23.4 0.1 broadcast_in_dim.2
  23.5 1.4 %collective-permute-start.4 = (s32[64,4,8,128]{3,2,1,0:T(8,128)S(1)}, s32[64,4,8,128]{3,2,1,0:T(8,128)S(1)}, u32[]{:S(2)}, u32[]{:S(2)}) collective-permute-start(s32[64,4,8,128]{3,2,1,0:T(8,128)S(1)} %broadcast_in_dim.2), channel_id=1, source_target_pairs={{128,0},{129,1},{130,2},{131,3},{132,4},{133,5},{134,6},{135,7},{1... | collective-permute-start | bytes 3145736 | tf_op jit(solution)/shard_map/ppermute | solution.py:255
  24.9 13.8 %all-to-all-start = ((bf16[128,16,128]{2,1,0:T(8,128)(2,1)}), bf16[128,16,128]{2,1,0:T(8,128)(2,1)S(1)}, u32[]{:S(2)}, u32[]{:S(2)}) async-start(bf16[128,16,128]{2,1,0:T(8,128)(2,1)} %bitcast.6), calls=%async_computation | async-start | bytes 1048576 | tf_op jit(solution)/shard_map/all_to_all | solution.py:259
  38.7 0.4 shard_map.85
  39.0 10.6 %all-to-all-done = bf16[128,16,128]{2,1,0:T(8,128)(2,1)S(1)} async-done(((bf16[128,16,128]{2,1,0:T(8,128)(2,1)}), bf16[128,16,128]{2,1,0:T(8,128)(2,1)S(1)}, u32[]{:S(2)}, u32[]{:S(2)}) %all-to-all-start) | async-done | bytes 524320 | tf_op jit(solution)/shard_map/all_to_all | solution.py:259
  49.6 0.0 collective-permute-done.4
  49.6 1.6 %shard_map.86 = (bf16[768,1024]{1,0:T(8,128)(2,1)S(1)}, bf16[384,1152]{1,0:T(8,128)(2,1)S(1)}) custom-call(bf16[2048,128]{1,0:T(8,128)(2,1)S(1)} %bitcast.17, bf16[256,256]{1,0:T(8,128)(2,1)S(1)} %get-tuple-element.30.order_ref, bf16[768,256]{1,0:T(8,128)(2,1)S(1)} %get-tuple-element.31.expand_ref, s32[4,8,128]{2,1,0:T(8,128)S(1)} %pad_add_fusion.ids_ref, ...), custom_call_target="tpu_custom_call" | custom-call | tf_op jit(solution)/shard_map/pallas_call | solution.py:236
  51.2 0.0 copy-start
  51.3 0.0 copy-start.1
  51.3 0.0 copy-start.2
  51.3 19.8 %all_to_all.15 = bf16[32,24,1024]{2,1,0:T(8,128)(2,1)S(1)} all-to-all(bf16[32,24,1024]{2,1,0:T(8,128)(2,1)S(1)} %bitcast.18), channel_id=1, replica_groups={{41,49,57,65,73,81,89,97,105,113,121,0,8,16,24,32,40,48,56,64,72,80,88,..., dimensions={0} | all-to-all | bytes 3145728 | tf_op jit(solution)/shard_map/all_to_all | solution.py:259
  71.1 0.0 copy-done
  71.1 0.0 copy-done.1
  71.1 0.0 copy-done.2
  71.1 3.7 %shard_map.88 = bf16[768,1024]{1,0:T(8,128)(2,1)} custom-call(bf16[768,1024]{1,0:T(8,128)(2,1)S(1)} %bitcast.16, bf16[1,1024,384]{2,1,0:T(8,128)(2,1)S(1)} %copy-done, bf16[1,1024,384]{2,1,0:T(8,128)(2,1)S(1)} %copy-done.1, bf16[1,384,1024]{2,1,0:T(8,128)(2,1)S(1)} %copy-done.2), custom_call_target="tpu_custom_call" | custom-call | tf_op jit(solution)/shard_map/pallas_call | solution.py:236
  74.8 0.0 copy-start.3
  74.8 5.0 %all-to-all-start.2 = ((bf16[32,24,1024]{2,1,0:T(8,128)(2,1)}), bf16[32,24,1024]{2,1,0:T(8,128)(2,1)S(1)}, u32[]{:S(2)}, u32[]{:S(2)}) async-start(bf16[32,24,1024]{2,1,0:T(8,128)(2,1)} %bitcast.11), calls=%async_computation.2 | async-start | bytes 3145728 | tf_op jit(solution)/shard_map/all_to_all | solution.py:259
  79.8 0.0 copy-done.3
  79.8 0.9 shard_map.87.mix_ref
  80.6 11.6 %all-to-all-done.2 = bf16[32,24,1024]{2,1,0:T(8,128)(2,1)S(1)} async-done(((bf16[32,24,1024]{2,1,0:T(8,128)(2,1)}), bf16[32,24,1024]{2,1,0:T(8,128)(2,1)S(1)}, u32[]{:S(2)}, u32[]{:S(2)}) %all-to-all-start.2) | async-done | bytes 1572896 | tf_op jit(solution)/shard_map/all_to_all | solution.py:259
  92.2 0.8 shard_map.89
  93.0 3.6 %collective-permute-start.5 = (bf16[128,1024]{1,0:T(8,128)(2,1)S(1)}, bf16[128,1024]{1,0:T(8,128)(2,1)S(1)}, u32[]{:S(2)}, u32[]{:S(2)}) collective-permute-start(bf16[128,1024]{1,0:T(8,128)(2,1)S(1)} %get-tuple-element.36), channel_id=1, source_target_pairs={{128,132},{129,133},{130,134},{131,135},{4,0},{5,1},{6,2},{7,3},{1... | collective-permute-start | bytes 786440 | tf_op jit(solution)/shard_map/ppermute | solution.py:255
  96.6 0.7 collective-permute-start.6
  97.3 2.0 %collective-permute-start.7 = (bf16[128,1024]{1,0:T(8,128)(2,1)S(1)}, bf16[128,1024]{1,0:T(8,128)(2,1)S(1)}, u32[]{:S(2)}, u32[]{:S(2)}) collective-permute-start(bf16[128,1024]{1,0:T(8,128)(2,1)S(1)} %get-tuple-element.38), channel_id=1, source_target_pairs={{128,134},{129,135},{2,0},{3,1},{4,2},{5,3},{134,132},{135,133},{1... | collective-permute-start | bytes 786440 | tf_op jit(solution)/shard_map/ppermute | solution.py:255
  99.3 1.6 %collective-permute-done.5.two_ref = bf16[128,1024]{1,0:T(8,128)(2,1)S(1)} collective-permute-done((bf16[128,1024]{1,0:T(8,128)(2,1)S(1)}, bf16[128,1024]{1,0:T(8,128)(2,1)S(1)}, u32[]{:S(2)}, u32[]{:S(2)}) %collective-permute-start.5) | collective-permute-done | bytes 262176 | tf_op jit(solution)/shard_map/ppermute | solution.py:255
  100.9 0.0 collective-permute-done.6.one_ref
  100.9 7.8 %collective-permute-done.7.three_ref = bf16[128,1024]{1,0:T(8,128)(2,1)S(1)} collective-permute-done((bf16[128,1024]{1,0:T(8,128)(2,1)S(1)}, bf16[128,1024]{1,0:T(8,128)(2,1)S(1)}, u32[]{:S(2)}, u32[]{:S(2)}) %collective-permute-start.7) | collective-permute-done | bytes 262176 | tf_op jit(solution)/shard_map/ppermute | solution.py:255
  108.7 0.1 shard_map.90
  108.9 1.3 %collective-permute-start.8 = (bf16[128,512]{1,0:T(8,128)(2,1)S(1)}, bf16[128,512]{1,0:T(8,128)(2,1)S(1)}, u32[]{:S(2)}, u32[]{:S(2)}) collective-permute-start(bf16[128,512]{1,0:T(8,128)(2,1)S(1)} %get-tuple-element.40), channel_id=1, source_target_pairs={{0,128},{1,129},{2,130},{3,131},{132,4},{133,5},{134,6},{135,7},{8... | collective-permute-start | bytes 393224 | tf_op jit(solution)/shard_map/ppermute | solution.py:255
  110.2 1.9 %collective-permute-done.8 = bf16[128,512]{1,0:T(8,128)(2,1)S(1)} collective-permute-done((bf16[128,512]{1,0:T(8,128)(2,1)S(1)}, bf16[128,512]{1,0:T(8,128)(2,1)S(1)}, u32[]{:S(2)}, u32[]{:S(2)}) %collective-permute-start.8) | collective-permute-done | bytes 131104 | tf_op jit(solution)/shard_map/ppermute | solution.py:255
  112.1 0.7 broadcast_select_fusion
  (2 shorter events, 0.0 us)
Async XLA Ops:
  0.0 6.5 %copy-start.4 = (s32[128,8]{0,1:T(8,128)S(1)}, s32[128,8]{0,1:T(8,128)}, u32[]{:S(2)}) copy-start(s32[128,8]{0,1:T(8,128)} %param.10) | copy-start | bytes 12292
  3.2 18.8 %collective-permute-start = (f32[64,1024]{1,0:T(8,128)S(1)}, f32[64,1024]{1,0:T(8,128)S(1)}, u32[]{:S(2)}, u32[]{:S(2)}) collective-permute-start(f32[64,1024]{1,0:T(8,128)S(1)} %get-tuple-element.24), channel_id=1, source_target_pairs={{0,128},{128,0},{1,129},{129,1},{2,130},{130,2},{3,131},{131,3},{4... | collective-permute-start | bytes 786440 | tf_op jit(solution)/shard_map/ppermute | solution.py:280
  6.5 13.4 %collective-permute-start.3 = (s32[8,128]{1,0:T(8,128)S(1)}, s32[8,128]{1,0:T(8,128)S(1)}, u32[]{:S(2)}, u32[]{:S(2)}) collective-permute-start(s32[8,128]{1,0:T(8,128)S(1)} %bitcast.19), channel_id=1, source_target_pairs={{128,134},{129,135},{130,128},{131,129},{132,130},{133,131},{134,1... | collective-permute-start | bytes 12296 | tf_op jit(solution)/shard_map/ppermute | solution.py:255
  12.7 8.3 %collective-permute-start.2 = (s32[8,128]{1,0:T(8,128)S(1)}, s32[8,128]{1,0:T(8,128)S(1)}, u32[]{:S(2)}, u32[]{:S(2)}) collective-permute-start(s32[8,128]{1,0:T(8,128)S(1)} %bitcast.20), channel_id=1, source_target_pairs={{128,132},{129,133},{130,134},{131,135},{132,128},{133,129},{134,1... | collective-permute-start | bytes 12296 | tf_op jit(solution)/shard_map/ppermute | solution.py:255
  15.5 6.5 %collective-permute-start.1 = (s32[8,128]{1,0:T(8,128)S(1)}, s32[8,128]{1,0:T(8,128)S(1)}, u32[]{:S(2)}, u32[]{:S(2)}) collective-permute-start(s32[8,128]{1,0:T(8,128)S(1)} %bitcast.21), channel_id=1, source_target_pairs={{128,130},{129,131},{130,132},{131,133},{132,134},{133,135},{134,1... | collective-permute-start | bytes 12296 | tf_op jit(solution)/shard_map/ppermute | solution.py:255
  23.5 26.1 %collective-permute-start.4 = (s32[64,4,8,128]{3,2,1,0:T(8,128)S(1)}, s32[64,4,8,128]{3,2,1,0:T(8,128)S(1)}, u32[]{:S(2)}, u32[]{:S(2)}) collective-permute-start(s32[64,4,8,128]{3,2,1,0:T(8,128)S(1)} %broadcast_in_dim.2), channel_id=1, source_target_pairs={{128,0},{129,1},{130,2},{131,3},{132,4},{133,5},{134,6},{135,7},{1... | collective-permute-start | bytes 3145736 | tf_op jit(solution)/shard_map/ppermute | solution.py:255
  24.9 24.7 %all-to-all-start = ((bf16[128,16,128]{2,1,0:T(8,128)(2,1)}), bf16[128,16,128]{2,1,0:T(8,128)(2,1)S(1)}, u32[]{:S(2)}, u32[]{:S(2)}) async-start(bf16[128,16,128]{2,1,0:T(8,128)(2,1)} %bitcast.6), calls=%async_computation | async-start | bytes 1048576 | tf_op jit(solution)/shard_map/all_to_all | solution.py:259
  51.2 19.8 %copy-start = (bf16[1,1024,384]{2,1,0:T(8,128)(2,1)S(1)}, bf16[1,1024,384]{2,1,0:T(8,128)(2,1)}, u32[]{:S(2)}) copy-start(bf16[1,1024,384]{2,1,0:T(8,128)(2,1)} %gate_ref.1) | copy-start | bytes 2359300
  51.3 19.8 %copy-start.1 = (bf16[1,1024,384]{2,1,0:T(8,128)(2,1)S(1)}, bf16[1,1024,384]{2,1,0:T(8,128)(2,1)}, u32[]{:S(2)}) copy-start(bf16[1,1024,384]{2,1,0:T(8,128)(2,1)} %up_ref.1) | copy-start | bytes 2359300
  51.3 19.8 %copy-start.2 = (bf16[1,384,1024]{2,1,0:T(8,128)(2,1)S(1)}, bf16[1,384,1024]{2,1,0:T(8,128)(2,1)}, u32[]{:S(2)}) copy-start(bf16[1,384,1024]{2,1,0:T(8,128)(2,1)} %down_ref.1) | copy-start | bytes 2359300
  74.8 5.0 %copy-start.3 = (bf16[1024,128]{1,0:T(8,128)(2,1)S(1)}, bf16[1024,128]{1,0:T(8,128)(2,1)}, u32[]{:S(2)}) copy-start(bf16[1024,128]{1,0:T(8,128)(2,1)} %router_ref.1) | copy-start | bytes 786436
  74.8 17.4 %all-to-all-start.2 = ((bf16[32,24,1024]{2,1,0:T(8,128)(2,1)}), bf16[32,24,1024]{2,1,0:T(8,128)(2,1)S(1)}, u32[]{:S(2)}, u32[]{:S(2)}) async-start(bf16[32,24,1024]{2,1,0:T(8,128)(2,1)} %bitcast.11), calls=%async_computation.2 | async-start | bytes 3145728 | tf_op jit(solution)/shard_map/all_to_all | solution.py:259
  93.0 7.9 %collective-permute-start.5 = (bf16[128,1024]{1,0:T(8,128)(2,1)S(1)}, bf16[128,1024]{1,0:T(8,128)(2,1)S(1)}, u32[]{:S(2)}, u32[]{:S(2)}) collective-permute-start(bf16[128,1024]{1,0:T(8,128)(2,1)S(1)} %get-tuple-element.36), channel_id=1, source_target_pairs={{128,132},{129,133},{130,134},{131,135},{4,0},{5,1},{6,2},{7,3},{1... | collective-permute-start | bytes 786440 | tf_op jit(solution)/shard_map/ppermute | solution.py:255
  96.6 4.3 %collective-permute-start.6 = (bf16[128,1024]{1,0:T(8,128)(2,1)S(1)}, bf16[128,1024]{1,0:T(8,128)(2,1)S(1)}, u32[]{:S(2)}, u32[]{:S(2)}) collective-permute-start(bf16[128,1024]{1,0:T(8,128)(2,1)S(1)} %get-tuple-element.37), channel_id=1, source_target_pairs={{0,2},{1,3},{130,132},{131,133},{132,134},{133,135},{6,0},{7,1},{8... | collective-permute-start | bytes 786440 | tf_op jit(solution)/shard_map/ppermute | solution.py:255
  97.3 11.5 %collective-permute-start.7 = (bf16[128,1024]{1,0:T(8,128)(2,1)S(1)}, bf16[128,1024]{1,0:T(8,128)(2,1)S(1)}, u32[]{:S(2)}, u32[]{:S(2)}) collective-permute-start(bf16[128,1024]{1,0:T(8,128)(2,1)S(1)} %get-tuple-element.38), channel_id=1, source_target_pairs={{128,134},{129,135},{2,0},{3,1},{4,2},{5,3},{134,132},{135,133},{1... | collective-permute-start | bytes 786440 | tf_op jit(solution)/shard_map/ppermute | solution.py:255
  108.9 3.2 %collective-permute-start.8 = (bf16[128,512]{1,0:T(8,128)(2,1)S(1)}, bf16[128,512]{1,0:T(8,128)(2,1)S(1)}, u32[]{:S(2)}, u32[]{:S(2)}) collective-permute-start(bf16[128,512]{1,0:T(8,128)(2,1)S(1)} %get-tuple-element.40), channel_id=1, source_target_pairs={{0,128},{1,129},{2,130},{3,131},{132,4},{133,5},{134,6},{135,7},{8... | collective-permute-start | bytes 393224 | tf_op jit(solution)/shard_map/ppermute | solution.py:255

commit v8 on v7

--- a/solution.py
+++ b/solution.py
@@ -90,7 +90,7 @@
     core = lax.axis_index("group")
     n = iota((128, 128), 0)
     half = jnp.where(n < 64, 1 - core, core)
-    owner = ((((n & 63) >> 2) * 4 + half * 2 + (n & 1)) << 1) + ((n >> 1) & 1)
+    owner = ((((n & 63) >> 2) * 4 + half + (n & 1) * 2) << 1) + ((n >> 1) & 1)
     chosen = (owner_ref[...] == owner).astype(F32).astype(BF16)
     rows = dot(chosen, restored[...]).astype(BF16)
     copy.wait()
@@ -151,7 +151,7 @@
     expand = expand_ref[...]
     ones = jnp.ones((128, 128), BF16)
     for member in range(2):
-        k = (zp + 4 - core * 2 - member) & 3
+        k = (zp + 4 - core - 2 * member) & 3
         ids = jnp.where(core == 1, ids_ref[k], ids_got_ref[k])
         named = expert == ids[0:1, :]
         for t in range(1, 8):
@@ -177,7 +177,7 @@
     for part in range(2):
         at = pl.ds(part * 384, 384)
         send_ref[at, :] = dot(pick[at, :], normed_ref[0:256, 0:1024]).astype(BF16)
-    normed_ref[256:384, 0:1024] = rows[pl.ds(pl.multiple_of((zp & 1) * 128, 128), 128), :]
+    normed_ref[256:384, 0:1024] = rows[pl.ds(pl.multiple_of((zp >> 1) * 128, 128), 128), :]
 
 
 def gate_kernel(normed_ref, router_ref, mix_ref):
@@ -219,7 +219,7 @@
     zp = my_zp()
     total[...] = dot(mix_ref[0:256, 0:768], back_ref[...])
     for k, ref in ((2, two_ref), (1, one_ref), (3, three_ref), (0, own_ref)):
-        value = total[pl.ds(pl.multiple_of(((zp + k) & 1) * 128, 128), 128), :]
+        value = total[pl.ds(pl.multiple_of((((zp + k) & 3) >> 1) * 128, 128), 128), :]
         if k == 0:
             value = value + mix_ref[256:384, :].astype(F32)
         ref[...] = value.astype(ref.dtype)
@@ -318,12 +318,12 @@
         [pltpu.VMEM((256, 1024), F32)],
     )
     parts = []
-    for k, part in ((2, two), (1, one), (3, three)):
+    for k, part in ((1, one), (3, three), (2, two)):
         ends = [(i, further(i, k)) for i in chips]
-        parts.append(send_to(part, [((j >> 2 & 1, i), (j >> 2 & 1, j)) for i, j in ends]))
+        parts.append(send_to(part, [((j >> 1 & 1, i), (j >> 1 & 1, j)) for i, j in ends]))
     mine, other = call(sum_kernel, [((128, 512), BF16)] * 2, (total, *parts))
-    swapped = send_to(other, [((i >> 2 & 1, i), (1 - (i >> 2 & 1), i)) for i in chips])
-    return jnp.where(lax.axis_index("group") == my_zp() >> 1, mine, swapped)
+    swapped = send_to(other, [((i >> 1 & 1, i), (1 - (i >> 1 & 1), i)) for i in chips])
+    return jnp.where(lax.axis_index("group") == my_zp() & 1, mine, swapped)
 
 
 def solution(mesh):

time: 113 us -> 111 us (0.982)
  waiting for transfers between devices: 35.6 us -> 34.4 us
    ppermute x8, waiting for transfers between devices: 13.5 us -> 12.2 us  [send_to(): lax.ppermute(x, ('group', 'ep'), [(a * 128 + i, b * 128 + j) for (a, i),...]
where the time goes in v8:
time: 111 us
  starting transfers between devices  43.7 us (39%)
  waiting for transfers between devices  34.4 us (31%)
  blocking collectives  19.8 us (18%)
  Pallas kernels  12.1 us (11%)
    all_to_all x2, waiting for transfers between devices, exchange(): return lax.all_to_all(x, 'ep', 0, 0, axis_index_groups=groups, tiled=True)  22.1 us
    ppermute x8, starting transfers between devices, send_to(): lax.ppermute(x, ('group', 'ep'), [(a * 128 + i, b * 128 + j) for (a, i),...  21.6 us
    all_to_all x1, blocking collectives, exchange(): return lax.all_to_all(x, 'ep', 0, 0, axis_index_groups=groups, tiled=True)  19.8 us
    all_to_all x2, starting transfers between devices, exchange(): return lax.all_to_all(x, 'ep', 0, 0, axis_index_groups=groups, tiled=True)  18.8 us
    ppermute x8, waiting for transfers between devices, send_to(): lax.ppermute(x, ('group', 'ep'), [(a * 128 + i, b * 128 + j) for (a, i),...  12.2 us
    pallas_call x9, Pallas kernels, call(): pl.pallas_call(kernel, out_shape=[jax.ShapeDtypeStruct(shape, dtype) for...  12.1 us
    ppermute x1, starting transfers between devices, body(): got = lax.ppermute(give, 'group', SWAP)  3.33 us
  transfers between devices with their start and end apart: 11, of which 7 were waited for; matrix products, arithmetic and copies ran while one was open for 0% of the time, Pallas kernels for 1%

profile of v8, /device:TPU:1, one launch (start us, length us, event | category | flops | bytes accessed | tf_op | source)
XLA Modules:
  0.0 110.9 jit_solution(10506571583673752818)
XLA Ops:
  0.0 0.0 copy-start.4
  0.0 3.1 %shard_map.82 = (f32[64,1024]{1,0:T(8,128)S(1)}, f32[64,1024]{1,0:T(8,128)S(1)}) custom-call(bf16[128,1024]{1,0:T(8,128)(2,1)} %x_ref.1, s32[1,128]{1,0:T(1,128)} %bitcast.26, bf16[1024,1024]{1,0:T(8,128)(2,1)} %w_hbm.1), custom_call_target="tpu_custom_call" | custom-call | tf_op jit(solution)/shard_map/pallas_call | solution.py:236
  3.2 3.3 %collective-permute-start = (f32[64,1024]{1,0:T(8,128)S(1)}, f32[64,1024]{1,0:T(8,128)S(1)}, u32[]{:S(2)}, u32[]{:S(2)}) collective-permute-start(f32[64,1024]{1,0:T(8,128)S(1)} %get-tuple-element.24), channel_id=1, source_target_pairs={{0,128},{128,0},{1,129},{129,1},{2,130},{130,2},{3,131},{131,3},{4... | collective-permute-start | bytes 786440 | tf_op jit(solution)/shard_map/ppermute | solution.py:280
  6.5 0.0 copy-done.4
  6.5 6.2 %collective-permute-start.3 = (s32[8,128]{1,0:T(8,128)S(1)}, s32[8,128]{1,0:T(8,128)S(1)}, u32[]{:S(2)}, u32[]{:S(2)}) collective-permute-start(s32[8,128]{1,0:T(8,128)S(1)} %bitcast.19), channel_id=1, source_target_pairs={{128,134},{129,135},{130,128},{131,129},{132,130},{133,131},{134,1... | collective-permute-start | bytes 12296 | tf_op jit(solution)/shard_map/ppermute | solution.py:255
  12.7 2.8 %collective-permute-start.2 = (s32[8,128]{1,0:T(8,128)S(1)}, s32[8,128]{1,0:T(8,128)S(1)}, u32[]{:S(2)}, u32[]{:S(2)}) collective-permute-start(s32[8,128]{1,0:T(8,128)S(1)} %bitcast.20), channel_id=1, source_target_pairs={{128,132},{129,133},{130,134},{131,135},{132,128},{133,129},{134,1... | collective-permute-start | bytes 12296 | tf_op jit(solution)/shard_map/ppermute | solution.py:255
  15.5 4.3 %collective-permute-start.1 = (s32[8,128]{1,0:T(8,128)S(1)}, s32[8,128]{1,0:T(8,128)S(1)}, u32[]{:S(2)}, u32[]{:S(2)}) collective-permute-start(s32[8,128]{1,0:T(8,128)S(1)} %bitcast.21), channel_id=1, source_target_pairs={{128,130},{129,131},{130,132},{131,133},{132,134},{133,135},{134,1... | collective-permute-start | bytes 12296 | tf_op jit(solution)/shard_map/ppermute | solution.py:255
  19.8 0.1 shard_map.83
  19.9 0.0 collective-permute-done.3
  19.9 1.0 collective-permute-done.2
  20.9 1.0 collective-permute-done.1
  22.0 0.0 collective-permute-done.got_ref
  22.0 1.4 %shard_map.84 = bf16[2048,128]{1,0:T(8,128)(2,1)} custom-call(f32[64,1024]{1,0:T(8,128)S(1)} %get-tuple-element.23.keep_ref, f32[64,1024]{1,0:T(8,128)S(1)} %collective-permute-done.got_ref, bf16[256,64]{1,0:T(8,128)(2,1)S(1)} %get-tuple-element.25.chosen_ref, bf16[256,256]{1,0:T(8,128)(2,1)S(1)} %get-tuple-element.26.order_ref), custom_call_target="tpu_custom_call" | custom-call | tf_op jit(solution)/shard_map/pallas_call | solution.py:236
  23.4 0.1 broadcast_in_dim.2
  23.5 1.4 %collective-permute-start.4 = (s32[64,4,8,128]{3,2,1,0:T(8,128)S(1)}, s32[64,4,8,128]{3,2,1,0:T(8,128)S(1)}, u32[]{:S(2)}, u32[]{:S(2)}) collective-permute-start(s32[64,4,8,128]{3,2,1,0:T(8,128)S(1)} %broadcast_in_dim.2), channel_id=1, source_target_pairs={{128,0},{129,1},{130,2},{131,3},{132,4},{133,5},{134,6},{135,7},{1... | collective-permute-start | bytes 3145736 | tf_op jit(solution)/shard_map/ppermute | solution.py:255
  24.9 13.8 %all-to-all-start = ((bf16[128,16,128]{2,1,0:T(8,128)(2,1)}), bf16[128,16,128]{2,1,0:T(8,128)(2,1)S(1)}, u32[]{:S(2)}, u32[]{:S(2)}) async-start(bf16[128,16,128]{2,1,0:T(8,128)(2,1)} %bitcast.6), calls=%async_computation | async-start | bytes 1048576 | tf_op jit(solution)/shard_map/all_to_all | solution.py:259
  38.7 0.4 shard_map.85
  39.0 10.6 %all-to-all-done = bf16[128,16,128]{2,1,0:T(8,128)(2,1)S(1)} async-done(((bf16[128,16,128]{2,1,0:T(8,128)(2,1)}), bf16[128,16,128]{2,1,0:T(8,128)(2,1)S(1)}, u32[]{:S(2)}, u32[]{:S(2)}) %all-to-all-start) | async-done | bytes 524320 | tf_op jit(solution)/shard_map/all_to_all | solution.py:259
  49.6 0.0 collective-permute-done.4
  49.6 1.6 %shard_map.86 = (bf16[768,1024]{1,0:T(8,128)(2,1)S(1)}, bf16[384,1152]{1,0:T(8,128)(2,1)S(1)}) custom-call(bf16[2048,128]{1,0:T(8,128)(2,1)S(1)} %bitcast.17, bf16[256,256]{1,0:T(8,128)(2,1)S(1)} %get-tuple-element.30.order_ref, bf16[768,256]{1,0:T(8,128)(2,1)S(1)} %get-tuple-element.31.expand_ref, s32[4,8,128]{2,1,0:T(8,128)S(1)} %pad_add_fusion.ids_ref, ...), custom_call_target="tpu_custom_call" | custom-call | tf_op jit(solution)/shard_map/pallas_call | solution.py:236
  51.3 0.0 copy-start
  51.3 0.0 copy-start.1
  51.3 0.0 copy-start.2
  51.3 19.8 %all_to_all.15 = bf16[32,24,1024]{2,1,0:T(8,128)(2,1)S(1)} all-to-all(bf16[32,24,1024]{2,1,0:T(8,128)(2,1)S(1)} %bitcast.18), channel_id=1, replica_groups={{41,49,57,65,73,81,89,97,105,113,121,0,8,16,24,32,40,48,56,64,72,80,88,..., dimensions={0} | all-to-all | bytes 3145728 | tf_op jit(solution)/shard_map/all_to_all | solution.py:259
  71.1 0.0 copy-done
  71.1 0.0 copy-done.1
  71.1 0.0 copy-done.2
  71.1 3.7 %shard_map.88 = bf16[768,1024]{1,0:T(8,128)(2,1)} custom-call(bf16[768,1024]{1,0:T(8,128)(2,1)S(1)} %bitcast.16, bf16[1,1024,384]{2,1,0:T(8,128)(2,1)S(1)} %copy-done, bf16[1,1024,384]{2,1,0:T(8,128)(2,1)S(1)} %copy-done.1, bf16[1,384,1024]{2,1,0:T(8,128)(2,1)S(1)} %copy-done.2), custom_call_target="tpu_custom_call" | custom-call | tf_op jit(solution)/shard_map/pallas_call | solution.py:236
  74.8 0.0 copy-start.3
  74.8 5.0 %all-to-all-start.2 = ((bf16[32,24,1024]{2,1,0:T(8,128)(2,1)}), bf16[32,24,1024]{2,1,0:T(8,128)(2,1)S(1)}, u32[]{:S(2)}, u32[]{:S(2)}) async-start(bf16[32,24,1024]{2,1,0:T(8,128)(2,1)} %bitcast.11), calls=%async_computation.2 | async-start | bytes 3145728 | tf_op jit(solution)/shard_map/all_to_all | solution.py:259
  79.8 0.0 copy-done.3
  79.8 0.9 shard_map.87.mix_ref
  80.7 11.6 %all-to-all-done.2 = bf16[32,24,1024]{2,1,0:T(8,128)(2,1)S(1)} async-done(((bf16[32,24,1024]{2,1,0:T(8,128)(2,1)}), bf16[32,24,1024]{2,1,0:T(8,128)(2,1)S(1)}, u32[]{:S(2)}, u32[]{:S(2)}) %all-to-all-start.2) | async-done | bytes 1572896 | tf_op jit(solution)/shard_map/all_to_all | solution.py:259
  92.2 0.8 shard_map.89
  93.0 3.2 %collective-permute-start.5 = (bf16[128,1024]{1,0:T(8,128)(2,1)S(1)}, bf16[128,1024]{1,0:T(8,128)(2,1)S(1)}, u32[]{:S(2)}, u32[]{:S(2)}) collective-permute-start(bf16[128,1024]{1,0:T(8,128)(2,1)S(1)} %get-tuple-element.36), channel_id=1, source_target_pairs={{128,130},{129,131},{2,4},{3,5},{132,134},{133,135},{6,0},{7,1},{1... | collective-permute-start | bytes 786440 | tf_op jit(solution)/shard_map/ppermute | solution.py:255
  96.2 1.8 %collective-permute-start.6 = (bf16[128,1024]{1,0:T(8,128)(2,1)S(1)}, bf16[128,1024]{1,0:T(8,128)(2,1)S(1)}, u32[]{:S(2)}, u32[]{:S(2)}) collective-permute-start(bf16[128,1024]{1,0:T(8,128)(2,1)S(1)} %get-tuple-element.37), channel_id=1, source_target_pairs={{128,134},{129,135},{2,0},{3,1},{132,130},{133,131},{6,4},{7,5},{1... | collective-permute-start | bytes 786440 | tf_op jit(solution)/shard_map/ppermute | solution.py:255
  98.0 0.7 collective-permute-start.7
  98.7 1.1 collective-permute-done.5.two_ref
  99.8 7.1 %collective-permute-done.6.one_ref = bf16[128,1024]{1,0:T(8,128)(2,1)S(1)} collective-permute-done((bf16[128,1024]{1,0:T(8,128)(2,1)S(1)}, bf16[128,1024]{1,0:T(8,128)(2,1)S(1)}, u32[]{:S(2)}, u32[]{:S(2)}) %collective-permute-start.6) | collective-permute-done | bytes 262176 | tf_op jit(solution)/shard_map/ppermute | solution.py:255
  106.9 0.0 collective-permute-done.7.three_ref
  106.9 0.1 shard_map.90
  107.0 1.3 %collective-permute-start.8 = (bf16[128,512]{1,0:T(8,128)(2,1)S(1)}, bf16[128,512]{1,0:T(8,128)(2,1)S(1)}, u32[]{:S(2)}, u32[]{:S(2)}) collective-permute-start(bf16[128,512]{1,0:T(8,128)(2,1)S(1)} %get-tuple-element.40), channel_id=1, source_target_pairs={{0,128},{1,129},{130,2},{131,3},{4,132},{5,133},{134,6},{135,7},{8... | collective-permute-start | bytes 393224 | tf_op jit(solution)/shard_map/ppermute | solution.py:255
  108.3 1.9 %collective-permute-done.8 = bf16[128,512]{1,0:T(8,128)(2,1)S(1)} collective-permute-done((bf16[128,512]{1,0:T(8,128)(2,1)S(1)}, bf16[128,512]{1,0:T(8,128)(2,1)S(1)}, u32[]{:S(2)}, u32[]{:S(2)}) %collective-permute-start.8) | collective-permute-done | bytes 131104 | tf_op jit(solution)/shard_map/ppermute | solution.py:255
  110.3 0.7 broadcast_select_fusion
  (2 shorter events, 0.0 us)
Async XLA Ops:
  0.0 6.5 %copy-start.4 = (s32[128,8]{0,1:T(8,128)S(1)}, s32[128,8]{0,1:T(8,128)}, u32[]{:S(2)}) copy-start(s32[128,8]{0,1:T(8,128)} %param.10) | copy-start | bytes 12292
  3.2 18.8 %collective-permute-start = (f32[64,1024]{1,0:T(8,128)S(1)}, f32[64,1024]{1,0:T(8,128)S(1)}, u32[]{:S(2)}, u32[]{:S(2)}) collective-permute-start(f32[64,1024]{1,0:T(8,128)S(1)} %get-tuple-element.24), channel_id=1, source_target_pairs={{0,128},{128,0},{1,129},{129,1},{2,130},{130,2},{3,131},{131,3},{4... | collective-permute-start | bytes 786440 | tf_op jit(solution)/shard_map/ppermute | solution.py:280
  6.5 13.4 %collective-permute-start.3 = (s32[8,128]{1,0:T(8,128)S(1)}, s32[8,128]{1,0:T(8,128)S(1)}, u32[]{:S(2)}, u32[]{:S(2)}) collective-permute-start(s32[8,128]{1,0:T(8,128)S(1)} %bitcast.19), channel_id=1, source_target_pairs={{128,134},{129,135},{130,128},{131,129},{132,130},{133,131},{134,1... | collective-permute-start | bytes 12296 | tf_op jit(solution)/shard_map/ppermute | solution.py:255
  12.7 8.3 %collective-permute-start.2 = (s32[8,128]{1,0:T(8,128)S(1)}, s32[8,128]{1,0:T(8,128)S(1)}, u32[]{:S(2)}, u32[]{:S(2)}) collective-permute-start(s32[8,128]{1,0:T(8,128)S(1)} %bitcast.20), channel_id=1, source_target_pairs={{128,132},{129,133},{130,134},{131,135},{132,128},{133,129},{134,1... | collective-permute-start | bytes 12296 | tf_op jit(solution)/shard_map/ppermute | solution.py:255
  15.5 6.5 %collective-permute-start.1 = (s32[8,128]{1,0:T(8,128)S(1)}, s32[8,128]{1,0:T(8,128)S(1)}, u32[]{:S(2)}, u32[]{:S(2)}) collective-permute-start(s32[8,128]{1,0:T(8,128)S(1)} %bitcast.21), channel_id=1, source_target_pairs={{128,130},{129,131},{130,132},{131,133},{132,134},{133,135},{134,1... | collective-permute-start | bytes 12296 | tf_op jit(solution)/shard_map/ppermute | solution.py:255
  23.5 26.1 %collective-permute-start.4 = (s32[64,4,8,128]{3,2,1,0:T(8,128)S(1)}, s32[64,4,8,128]{3,2,1,0:T(8,128)S(1)}, u32[]{:S(2)}, u32[]{:S(2)}) collective-permute-start(s32[64,4,8,128]{3,2,1,0:T(8,128)S(1)} %broadcast_in_dim.2), channel_id=1, source_target_pairs={{128,0},{129,1},{130,2},{131,3},{132,4},{133,5},{134,6},{135,7},{1... | collective-permute-start | bytes 3145736 | tf_op jit(solution)/shard_map/ppermute | solution.py:255
  24.9 24.7 %all-to-all-start = ((bf16[128,16,128]{2,1,0:T(8,128)(2,1)}), bf16[128,16,128]{2,1,0:T(8,128)(2,1)S(1)}, u32[]{:S(2)}, u32[]{:S(2)}) async-start(bf16[128,16,128]{2,1,0:T(8,128)(2,1)} %bitcast.6), calls=%async_computation | async-start | bytes 1048576 | tf_op jit(solution)/shard_map/all_to_all | solution.py:259
  51.3 19.8 %copy-start = (bf16[1,1024,384]{2,1,0:T(8,128)(2,1)S(1)}, bf16[1,1024,384]{2,1,0:T(8,128)(2,1)}, u32[]{:S(2)}) copy-start(bf16[1,1024,384]{2,1,0:T(8,128)(2,1)} %gate_ref.1) | copy-start | bytes 2359300
  51.3 19.8 %copy-start.1 = (bf16[1,1024,384]{2,1,0:T(8,128)(2,1)S(1)}, bf16[1,1024,384]{2,1,0:T(8,128)(2,1)}, u32[]{:S(2)}) copy-start(bf16[1,1024,384]{2,1,0:T(8,128)(2,1)} %up_ref.1) | copy-start | bytes 2359300
  51.3 19.8 %copy-start.2 = (bf16[1,384,1024]{2,1,0:T(8,128)(2,1)S(1)}, bf16[1,384,1024]{2,1,0:T(8,128)(2,1)}, u32[]{:S(2)}) copy-start(bf16[1,384,1024]{2,1,0:T(8,128)(2,1)} %down_ref.1) | copy-start | bytes 2359300
  74.8 5.0 %copy-start.3 = (bf16[1024,128]{1,0:T(8,128)(2,1)S(1)}, bf16[1024,128]{1,0:T(8,128)(2,1)}, u32[]{:S(2)}) copy-start(bf16[1024,128]{1,0:T(8,128)(2,1)} %router_ref.1) | copy-start | bytes 786436
  74.8 17.4 %all-to-all-start.2 = ((bf16[32,24,1024]{2,1,0:T(8,128)(2,1)}), bf16[32,24,1024]{2,1,0:T(8,128)(2,1)S(1)}, u32[]{:S(2)}, u32[]{:S(2)}) async-start(bf16[32,24,1024]{2,1,0:T(8,128)(2,1)} %bitcast.11), calls=%async_computation.2 | async-start | bytes 3145728 | tf_op jit(solution)/shard_map/all_to_all | solution.py:259
  93.0 6.8 %collective-permute-start.5 = (bf16[128,1024]{1,0:T(8,128)(2,1)S(1)}, bf16[128,1024]{1,0:T(8,128)(2,1)S(1)}, u32[]{:S(2)}, u32[]{:S(2)}) collective-permute-start(bf16[128,1024]{1,0:T(8,128)(2,1)S(1)} %get-tuple-element.36), channel_id=1, source_target_pairs={{128,130},{129,131},{2,4},{3,5},{132,134},{133,135},{6,0},{7,1},{1... | collective-permute-start | bytes 786440 | tf_op jit(solution)/shard_map/ppermute | solution.py:255
  96.2 10.7 %collective-permute-start.6 = (bf16[128,1024]{1,0:T(8,128)(2,1)S(1)}, bf16[128,1024]{1,0:T(8,128)(2,1)S(1)}, u32[]{:S(2)}, u32[]{:S(2)}) collective-permute-start(bf16[128,1024]{1,0:T(8,128)(2,1)S(1)} %get-tuple-element.37), channel_id=1, source_target_pairs={{128,134},{129,135},{2,0},{3,1},{132,130},{133,131},{6,4},{7,5},{1... | collective-permute-start | bytes 786440 | tf_op jit(solution)/shard_map/ppermute | solution.py:255
  98.0 8.9 %collective-permute-start.7 = (bf16[128,1024]{1,0:T(8,128)(2,1)S(1)}, bf16[128,1024]{1,0:T(8,128)(2,1)S(1)}, u32[]{:S(2)}, u32[]{:S(2)}) collective-permute-start(bf16[128,1024]{1,0:T(8,128)(2,1)S(1)} %get-tuple-element.38), channel_id=1, source_target_pairs={{0,4},{1,5},{130,134},{131,135},{4,0},{5,1},{134,130},{135,131},{8... | collective-permute-start | bytes 786440 | tf_op jit(solution)/shard_map/ppermute | solution.py:255
  107.0 3.2 %collective-permute-start.8 = (bf16[128,512]{1,0:T(8,128)(2,1)S(1)}, bf16[128,512]{1,0:T(8,128)(2,1)S(1)}, u32[]{:S(2)}, u32[]{:S(2)}) collective-permute-start(bf16[128,512]{1,0:T(8,128)(2,1)S(1)} %get-tuple-element.40), channel_id=1, source_target_pairs={{0,128},{1,129},{130,2},{131,3},{4,132},{5,133},{134,6},{135,7},{8... | collective-permute-start | bytes 393224 | tf_op jit(solution)/shard_map/ppermute | solution.py:255

commit v9 on v8

--- a/solution.py
+++ b/solution.py
@@ -196,21 +196,26 @@
 
 
 def expert_kernel(x_ref, gate_ref, up_ref, down_ref, out_hbm, hidden, stage, sems):
-    x = x_ref[...]
-
     def act(gate, up):
         return (gate / (1.0 + jnp.exp(-gate)) * up).astype(BF16)
 
-    hidden[:, 0:256] = act(dot(x, gate_ref[0, :, 0:256]), dot(x, up_ref[0, :, 0:256]))
     last = jnp.concatenate([gate_ref[0, :, 256:384], up_ref[0, :, 256:384]], axis=1)
-    both = dot(x, last)
-    hidden[:, 256:384] = act(both[:, 0:128], both[:, 128:256])
     copies = []
-    for i in range(4):
-        lanes = pl.ds(i * 256, 256)
-        stage[:, lanes] = dot(hidden[...], down_ref[0, :, lanes]).astype(BF16)
-        copies.append(pltpu.make_async_copy(stage.at[:, lanes], out_hbm.at[:, lanes], sems.at[i]))
-        copies[-1].start()
+    for i in range(2):
+        at = pl.ds(i * 384, 384)
+        x = x_ref[at, :]
+        hidden[at, 0:256] = act(dot(x, gate_ref[0, :, 0:256]), dot(x, up_ref[0, :, 0:256]))
+        both = dot(x, last)
+        hidden[at, 256:384] = act(both[:, 0:128], both[:, 128:256])
+        stage[at, :] = dot(hidden[at, :], down_ref[0]).astype(BF16)
+        for j in range(2):
+            rows = pl.ds(i * 384 + j * 192, 192)
+            copies.append(
+                pltpu.make_async_copy(
+                    stage.at[rows, :], out_hbm.at[rows, :], sems.at[i * 2 + j]
+                )
+            )
+            copies[-1].start()
     for copy in copies:
         copy.wait()
 

time: 111 us -> 111 us (level)
  no operation moved by 1% of the time
where the time goes in v9:
time: 111 us
  starting transfers between devices  43.7 us (39%)
  waiting for transfers between devices  34.4 us (31%)
  blocking collectives  19.8 us (18%)
  Pallas kernels  12 us (11%)
    all_to_all x2, waiting for transfers between devices, exchange(): return lax.all_to_all(x, 'ep', 0, 0, axis_index_groups=groups, tiled=True)  22.1 us
    ppermute x8, starting transfers between devices, send_to(): lax.ppermute(x, ('group', 'ep'), [(a * 128 + i, b * 128 + j) for (a, i),...  21.6 us
    all_to_all x1, blocking collectives, exchange(): return lax.all_to_all(x, 'ep', 0, 0, axis_index_groups=groups, tiled=True)  19.8 us
    all_to_all x2, starting transfers between devices, exchange(): return lax.all_to_all(x, 'ep', 0, 0, axis_index_groups=groups, tiled=True)  18.8 us
    ppermute x8, waiting for transfers between devices, send_to(): lax.ppermute(x, ('group', 'ep'), [(a * 128 + i, b * 128 + j) for (a, i),...  12.2 us
    pallas_call x9, Pallas kernels, call(): pl.pallas_call(kernel, out_shape=[jax.ShapeDtypeStruct(shape, dtype) for...  12 us
    ppermute x1, starting transfers between devices, body(): got = lax.ppermute(give, 'group', SWAP)  3.33 us
  transfers between devices with their start and end apart: 11, of which 7 were waited for; matrix products, arithmetic and copies ran while one was open for 0% of the time, Pallas kernels for 1%

profile of v9, /device:TPU:1, one launch (start us, length us, event | category | flops | bytes accessed | tf_op | source)
XLA Modules:
  0.0 110.8 jit_solution(4583452164760476808)
XLA Ops:
  0.0 0.0 copy-start.4
  0.0 3.1 %shard_map.82 = (f32[64,1024]{1,0:T(8,128)S(1)}, f32[64,1024]{1,0:T(8,128)S(1)}) custom-call(bf16[128,1024]{1,0:T(8,128)(2,1)} %x_ref.1, s32[1,128]{1,0:T(1,128)} %bitcast.26, bf16[1024,1024]{1,0:T(8,128)(2,1)} %w_hbm.1), custom_call_target="tpu_custom_call" | custom-call | tf_op jit(solution)/shard_map/pallas_call | solution.py:241
  3.2 3.3 %collective-permute-start = (f32[64,1024]{1,0:T(8,128)S(1)}, f32[64,1024]{1,0:T(8,128)S(1)}, u32[]{:S(2)}, u32[]{:S(2)}) collective-permute-start(f32[64,1024]{1,0:T(8,128)S(1)} %get-tuple-element.24), channel_id=1, source_target_pairs={{0,128},{128,0},{1,129},{129,1},{2,130},{130,2},{3,131},{131,3},{4... | collective-permute-start | bytes 786440 | tf_op jit(solution)/shard_map/ppermute | solution.py:285
  6.5 0.0 copy-done.4
  6.5 6.2 %collective-permute-start.3 = (s32[8,128]{1,0:T(8,128)S(1)}, s32[8,128]{1,0:T(8,128)S(1)}, u32[]{:S(2)}, u32[]{:S(2)}) collective-permute-start(s32[8,128]{1,0:T(8,128)S(1)} %bitcast.19), channel_id=1, source_target_pairs={{128,134},{129,135},{130,128},{131,129},{132,130},{133,131},{134,1... | collective-permute-start | bytes 12296 | tf_op jit(solution)/shard_map/ppermute | solution.py:260
  12.7 2.8 %collective-permute-start.2 = (s32[8,128]{1,0:T(8,128)S(1)}, s32[8,128]{1,0:T(8,128)S(1)}, u32[]{:S(2)}, u32[]{:S(2)}) collective-permute-start(s32[8,128]{1,0:T(8,128)S(1)} %bitcast.20), channel_id=1, source_target_pairs={{128,132},{129,133},{130,134},{131,135},{132,128},{133,129},{134,1... | collective-permute-start | bytes 12296 | tf_op jit(solution)/shard_map/ppermute | solution.py:260
  15.5 4.3 %collective-permute-start.1 = (s32[8,128]{1,0:T(8,128)S(1)}, s32[8,128]{1,0:T(8,128)S(1)}, u32[]{:S(2)}, u32[]{:S(2)}) collective-permute-start(s32[8,128]{1,0:T(8,128)S(1)} %bitcast.21), channel_id=1, source_target_pairs={{128,130},{129,131},{130,132},{131,133},{132,134},{133,135},{134,1... | collective-permute-start | bytes 12296 | tf_op jit(solution)/shard_map/ppermute | solution.py:260
  19.8 0.1 shard_map.83
  19.9 0.0 collective-permute-done.3
  19.9 1.0 collective-permute-done.2
  20.9 1.0 collective-permute-done.1
  22.0 0.0 collective-permute-done.got_ref
  22.0 1.4 %shard_map.84 = bf16[2048,128]{1,0:T(8,128)(2,1)} custom-call(f32[64,1024]{1,0:T(8,128)S(1)} %get-tuple-element.23.keep_ref, f32[64,1024]{1,0:T(8,128)S(1)} %collective-permute-done.got_ref, bf16[256,64]{1,0:T(8,128)(2,1)S(1)} %get-tuple-element.25.chosen_ref, bf16[256,256]{1,0:T(8,128)(2,1)S(1)} %get-tuple-element.26.order_ref), custom_call_target="tpu_custom_call" | custom-call | tf_op jit(solution)/shard_map/pallas_call | solution.py:241
  23.4 0.1 broadcast_in_dim.2
  23.5 1.4 %collective-permute-start.4 = (s32[64,4,8,128]{3,2,1,0:T(8,128)S(1)}, s32[64,4,8,128]{3,2,1,0:T(8,128)S(1)}, u32[]{:S(2)}, u32[]{:S(2)}) collective-permute-start(s32[64,4,8,128]{3,2,1,0:T(8,128)S(1)} %broadcast_in_dim.2), channel_id=1, source_target_pairs={{128,0},{129,1},{130,2},{131,3},{132,4},{133,5},{134,6},{135,7},{1... | collective-permute-start | bytes 3145736 | tf_op jit(solution)/shard_map/ppermute | solution.py:260
  24.9 13.8 %all-to-all-start = ((bf16[128,16,128]{2,1,0:T(8,128)(2,1)}), bf16[128,16,128]{2,1,0:T(8,128)(2,1)S(1)}, u32[]{:S(2)}, u32[]{:S(2)}) async-start(bf16[128,16,128]{2,1,0:T(8,128)(2,1)} %bitcast.6), calls=%async_computation | async-start | bytes 1048576 | tf_op jit(solution)/shard_map/all_to_all | solution.py:264
  38.7 0.4 shard_map.85
  39.0 10.6 %all-to-all-done = bf16[128,16,128]{2,1,0:T(8,128)(2,1)S(1)} async-done(((bf16[128,16,128]{2,1,0:T(8,128)(2,1)}), bf16[128,16,128]{2,1,0:T(8,128)(2,1)S(1)}, u32[]{:S(2)}, u32[]{:S(2)}) %all-to-all-start) | async-done | bytes 524320 | tf_op jit(solution)/shard_map/all_to_all | solution.py:264
  49.6 0.0 collective-permute-done.4
  49.6 1.6 %shard_map.86 = (bf16[768,1024]{1,0:T(8,128)(2,1)S(1)}, bf16[384,1152]{1,0:T(8,128)(2,1)S(1)}) custom-call(bf16[2048,128]{1,0:T(8,128)(2,1)S(1)} %bitcast.17, bf16[256,256]{1,0:T(8,128)(2,1)S(1)} %get-tuple-element.30.order_ref, bf16[768,256]{1,0:T(8,128)(2,1)S(1)} %get-tuple-element.31.expand_ref, s32[4,8,128]{2,1,0:T(8,128)S(1)} %pad_add_fusion.ids_ref, ...), custom_call_target="tpu_custom_call" | custom-call | tf_op jit(solution)/shard_map/pallas_call | solution.py:241
  51.3 0.0 copy-start
  51.3 0.0 copy-start.1
  51.3 0.0 copy-start.2
  51.3 19.8 %all_to_all.15 = bf16[32,24,1024]{2,1,0:T(8,128)(2,1)S(1)} all-to-all(bf16[32,24,1024]{2,1,0:T(8,128)(2,1)S(1)} %bitcast.18), channel_id=1, replica_groups={{41,49,57,65,73,81,89,97,105,113,121,0,8,16,24,32,40,48,56,64,72,80,88,..., dimensions={0} | all-to-all | bytes 3145728 | tf_op jit(solution)/shard_map/all_to_all | solution.py:264
  71.1 0.0 copy-done
  71.1 0.0 copy-done.1
  71.1 0.0 copy-done.2
  71.1 3.6 %shard_map.88 = bf16[768,1024]{1,0:T(8,128)(2,1)} custom-call(bf16[768,1024]{1,0:T(8,128)(2,1)S(1)} %bitcast.16, bf16[1,1024,384]{2,1,0:T(8,128)(2,1)S(1)} %copy-done, bf16[1,1024,384]{2,1,0:T(8,128)(2,1)S(1)} %copy-done.1, bf16[1,384,1024]{2,1,0:T(8,128)(2,1)S(1)} %copy-done.2), custom_call_target="tpu_custom_call" | custom-call | tf_op jit(solution)/shard_map/pallas_call | solution.py:241
  74.7 0.0 copy-start.3
  74.7 5.0 %all-to-all-start.2 = ((bf16[32,24,1024]{2,1,0:T(8,128)(2,1)}), bf16[32,24,1024]{2,1,0:T(8,128)(2,1)S(1)}, u32[]{:S(2)}, u32[]{:S(2)}) async-start(bf16[32,24,1024]{2,1,0:T(8,128)(2,1)} %bitcast.11), calls=%async_computation.2 | async-start | bytes 3145728 | tf_op jit(solution)/shard_map/all_to_all | solution.py:264
  79.7 0.0 copy-done.3
  79.7 0.9 shard_map.87.mix_ref
  80.6 11.6 %all-to-all-done.2 = bf16[32,24,1024]{2,1,0:T(8,128)(2,1)S(1)} async-done(((bf16[32,24,1024]{2,1,0:T(8,128)(2,1)}), bf16[32,24,1024]{2,1,0:T(8,128)(2,1)S(1)}, u32[]{:S(2)}, u32[]{:S(2)}) %all-to-all-start.2) | async-done | bytes 1572896 | tf_op jit(solution)/shard_map/all_to_all | solution.py:264
  92.1 0.8 shard_map.89
  92.9 3.2 %collective-permute-start.5 = (bf16[128,1024]{1,0:T(8,128)(2,1)S(1)}, bf16[128,1024]{1,0:T(8,128)(2,1)S(1)}, u32[]{:S(2)}, u32[]{:S(2)}) collective-permute-start(bf16[128,1024]{1,0:T(8,128)(2,1)S(1)} %get-tuple-element.36), channel_id=1, source_target_pairs={{128,130},{129,131},{2,4},{3,5},{132,134},{133,135},{6,0},{7,1},{1... | collective-permute-start | bytes 786440 | tf_op jit(solution)/shard_map/ppermute | solution.py:260
  96.1 1.8 %collective-permute-start.6 = (bf16[128,1024]{1,0:T(8,128)(2,1)S(1)}, bf16[128,1024]{1,0:T(8,128)(2,1)S(1)}, u32[]{:S(2)}, u32[]{:S(2)}) collective-permute-start(bf16[128,1024]{1,0:T(8,128)(2,1)S(1)} %get-tuple-element.37), channel_id=1, source_target_pairs={{128,134},{129,135},{2,0},{3,1},{132,130},{133,131},{6,4},{7,5},{1... | collective-permute-start | bytes 786440 | tf_op jit(solution)/shard_map/ppermute | solution.py:260
  97.9 0.7 collective-permute-start.7
  98.6 1.1 collective-permute-done.5.two_ref
  99.7 7.1 %collective-permute-done.6.one_ref = bf16[128,1024]{1,0:T(8,128)(2,1)S(1)} collective-permute-done((bf16[128,1024]{1,0:T(8,128)(2,1)S(1)}, bf16[128,1024]{1,0:T(8,128)(2,1)S(1)}, u32[]{:S(2)}, u32[]{:S(2)}) %collective-permute-start.6) | collective-permute-done | bytes 262176 | tf_op jit(solution)/shard_map/ppermute | solution.py:260
  106.8 0.0 collective-permute-done.7.three_ref
  106.8 0.1 shard_map.90
  106.9 1.3 %collective-permute-start.8 = (bf16[128,512]{1,0:T(8,128)(2,1)S(1)}, bf16[128,512]{1,0:T(8,128)(2,1)S(1)}, u32[]{:S(2)}, u32[]{:S(2)}) collective-permute-start(bf16[128,512]{1,0:T(8,128)(2,1)S(1)} %get-tuple-element.40), channel_id=1, source_target_pairs={{0,128},{1,129},{130,2},{131,3},{4,132},{5,133},{134,6},{135,7},{8... | collective-permute-start | bytes 393224 | tf_op jit(solution)/shard_map/ppermute | solution.py:260
  108.2 1.9 %collective-permute-done.8 = bf16[128,512]{1,0:T(8,128)(2,1)S(1)} collective-permute-done((bf16[128,512]{1,0:T(8,128)(2,1)S(1)}, bf16[128,512]{1,0:T(8,128)(2,1)S(1)}, u32[]{:S(2)}, u32[]{:S(2)}) %collective-permute-start.8) | collective-permute-done | bytes 131104 | tf_op jit(solution)/shard_map/ppermute | solution.py:260
  110.2 0.7 broadcast_select_fusion
  (2 shorter events, 0.0 us)
Async XLA Ops:
  0.0 6.5 %copy-start.4 = (s32[128,8]{0,1:T(8,128)S(1)}, s32[128,8]{0,1:T(8,128)}, u32[]{:S(2)}) copy-start(s32[128,8]{0,1:T(8,128)} %param.10) | copy-start | bytes 12292
  3.2 18.8 %collective-permute-start = (f32[64,1024]{1,0:T(8,128)S(1)}, f32[64,1024]{1,0:T(8,128)S(1)}, u32[]{:S(2)}, u32[]{:S(2)}) collective-permute-start(f32[64,1024]{1,0:T(8,128)S(1)} %get-tuple-element.24), channel_id=1, source_target_pairs={{0,128},{128,0},{1,129},{129,1},{2,130},{130,2},{3,131},{131,3},{4... | collective-permute-start | bytes 786440 | tf_op jit(solution)/shard_map/ppermute | solution.py:285
  6.5 13.4 %collective-permute-start.3 = (s32[8,128]{1,0:T(8,128)S(1)}, s32[8,128]{1,0:T(8,128)S(1)}, u32[]{:S(2)}, u32[]{:S(2)}) collective-permute-start(s32[8,128]{1,0:T(8,128)S(1)} %bitcast.19), channel_id=1, source_target_pairs={{128,134},{129,135},{130,128},{131,129},{132,130},{133,131},{134,1... | collective-permute-start | bytes 12296 | tf_op jit(solution)/shard_map/ppermute | solution.py:260
  12.7 8.3 %collective-permute-start.2 = (s32[8,128]{1,0:T(8,128)S(1)}, s32[8,128]{1,0:T(8,128)S(1)}, u32[]{:S(2)}, u32[]{:S(2)}) collective-permute-start(s32[8,128]{1,0:T(8,128)S(1)} %bitcast.20), channel_id=1, source_target_pairs={{128,132},{129,133},{130,134},{131,135},{132,128},{133,129},{134,1... | collective-permute-start | bytes 12296 | tf_op jit(solution)/shard_map/ppermute | solution.py:260
  15.5 6.5 %collective-permute-start.1 = (s32[8,128]{1,0:T(8,128)S(1)}, s32[8,128]{1,0:T(8,128)S(1)}, u32[]{:S(2)}, u32[]{:S(2)}) collective-permute-start(s32[8,128]{1,0:T(8,128)S(1)} %bitcast.21), channel_id=1, source_target_pairs={{128,130},{129,131},{130,132},{131,133},{132,134},{133,135},{134,1... | collective-permute-start | bytes 12296 | tf_op jit(solution)/shard_map/ppermute | solution.py:260
  23.5 26.1 %collective-permute-start.4 = (s32[64,4,8,128]{3,2,1,0:T(8,128)S(1)}, s32[64,4,8,128]{3,2,1,0:T(8,128)S(1)}, u32[]{:S(2)}, u32[]{:S(2)}) collective-permute-start(s32[64,4,8,128]{3,2,1,0:T(8,128)S(1)} %broadcast_in_dim.2), channel_id=1, source_target_pairs={{128,0},{129,1},{130,2},{131,3},{132,4},{133,5},{134,6},{135,7},{1... | collective-permute-start | bytes 3145736 | tf_op jit(solution)/shard_map/ppermute | solution.py:260
  24.9 24.7 %all-to-all-start = ((bf16[128,16,128]{2,1,0:T(8,128)(2,1)}), bf16[128,16,128]{2,1,0:T(8,128)(2,1)S(1)}, u32[]{:S(2)}, u32[]{:S(2)}) async-start(bf16[128,16,128]{2,1,0:T(8,128)(2,1)} %bitcast.6), calls=%async_computation | async-start | bytes 1048576 | tf_op jit(solution)/shard_map/all_to_all | solution.py:264
  51.3 19.8 %copy-start = (bf16[1,1024,384]{2,1,0:T(8,128)(2,1)S(1)}, bf16[1,1024,384]{2,1,0:T(8,128)(2,1)}, u32[]{:S(2)}) copy-start(bf16[1,1024,384]{2,1,0:T(8,128)(2,1)} %gate_ref.1) | copy-start | bytes 2359300
  51.3 19.8 %copy-start.1 = (bf16[1,1024,384]{2,1,0:T(8,128)(2,1)S(1)}, bf16[1,1024,384]{2,1,0:T(8,128)(2,1)}, u32[]{:S(2)}) copy-start(bf16[1,1024,384]{2,1,0:T(8,128)(2,1)} %up_ref.1) | copy-start | bytes 2359300
  51.3 19.8 %copy-start.2 = (bf16[1,384,1024]{2,1,0:T(8,128)(2,1)S(1)}, bf16[1,384,1024]{2,1,0:T(8,128)(2,1)}, u32[]{:S(2)}) copy-start(bf16[1,384,1024]{2,1,0:T(8,128)(2,1)} %down_ref.1) | copy-start | bytes 2359300
  74.7 5.0 %copy-start.3 = (bf16[1024,128]{1,0:T(8,128)(2,1)S(1)}, bf16[1024,128]{1,0:T(8,128)(2,1)}, u32[]{:S(2)}) copy-start(bf16[1024,128]{1,0:T(8,128)(2,1)} %router_ref.1) | copy-start | bytes 786436
  74.7 17.4 %all-to-all-start.2 = ((bf16[32,24,1024]{2,1,0:T(8,128)(2,1)}), bf16[32,24,1024]{2,1,0:T(8,128)(2,1)S(1)}, u32[]{:S(2)}, u32[]{:S(2)}) async-start(bf16[32,24,1024]{2,1,0:T(8,128)(2,1)} %bitcast.11), calls=%async_computation.2 | async-start | bytes 3145728 | tf_op jit(solution)/shard_map/all_to_all | solution.py:264
  92.9 6.8 %collective-permute-start.5 = (bf16[128,1024]{1,0:T(8,128)(2,1)S(1)}, bf16[128,1024]{1,0:T(8,128)(2,1)S(1)}, u32[]{:S(2)}, u32[]{:S(2)}) collective-permute-start(bf16[128,1024]{1,0:T(8,128)(2,1)S(1)} %get-tuple-element.36), channel_id=1, source_target_pairs={{128,130},{129,131},{2,4},{3,5},{132,134},{133,135},{6,0},{7,1},{1... | collective-permute-start | bytes 786440 | tf_op jit(solution)/shard_map/ppermute | solution.py:260
  96.1 10.7 %collective-permute-start.6 = (bf16[128,1024]{1,0:T(8,128)(2,1)S(1)}, bf16[128,1024]{1,0:T(8,128)(2,1)S(1)}, u32[]{:S(2)}, u32[]{:S(2)}) collective-permute-start(bf16[128,1024]{1,0:T(8,128)(2,1)S(1)} %get-tuple-element.37), channel_id=1, source_target_pairs={{128,134},{129,135},{2,0},{3,1},{132,130},{133,131},{6,4},{7,5},{1... | collective-permute-start | bytes 786440 | tf_op jit(solution)/shard_map/ppermute | solution.py:260
  97.9 8.9 %collective-permute-start.7 = (bf16[128,1024]{1,0:T(8,128)(2,1)S(1)}, bf16[128,1024]{1,0:T(8,128)(2,1)S(1)}, u32[]{:S(2)}, u32[]{:S(2)}) collective-permute-start(bf16[128,1024]{1,0:T(8,128)(2,1)S(1)} %get-tuple-element.38), channel_id=1, source_target_pairs={{0,4},{1,5},{130,134},{131,135},{4,0},{5,1},{134,130},{135,131},{8... | collective-permute-start | bytes 786440 | tf_op jit(solution)/shard_map/ppermute | solution.py:260
  106.9 3.2 %collective-permute-start.8 = (bf16[128,512]{1,0:T(8,128)(2,1)S(1)}, bf16[128,512]{1,0:T(8,128)(2,1)S(1)}, u32[]{:S(2)}, u32[]{:S(2)}) collective-permute-start(bf16[128,512]{1,0:T(8,128)(2,1)S(1)} %get-tuple-element.40), channel_id=1, source_target_pairs={{0,128},{1,129},{130,2},{131,3},{4,132},{5,133},{134,6},{135,7},{8... | collective-permute-start | bytes 393224 | tf_op jit(solution)/shard_map/ppermute | solution.py:260

commit v10 on v9

--- a/solution.py
+++ b/solution.py
@@ -1,3 +1,5 @@
+import functools
+
 import jax
 import jax.numpy as jnp
 from jax import lax
@@ -230,11 +232,11 @@
         ref[...] = value.astype(ref.dtype)
 
 
-def sum_kernel(own_ref, two_ref, one_ref, three_ref, mine_ref, other_ref):
-    for ref, lanes in zip((other_ref, mine_ref), halves()[::-1]):
-        total = own_ref[:, lanes] + two_ref[:, lanes].astype(F32)
-        total = total + one_ref[:, lanes].astype(F32)
-        ref[...] = (total + three_ref[:, lanes].astype(F32)).astype(BF16)
+def sum_kernel(whose, own_ref, two_ref, one_ref, three_ref, out_ref):
+    lanes = halves()[whose]
+    total = own_ref[:, lanes] + two_ref[:, lanes].astype(F32)
+    total = total + one_ref[:, lanes].astype(F32)
+    out_ref[...] = (total + three_ref[:, lanes].astype(F32)).astype(BF16)
 
 
 def call(kernel, outs, ins, scratch=(), specs=None, out_spec=VMEM):
@@ -326,8 +328,10 @@
     for k, part in ((1, one), (3, three), (2, two)):
         ends = [(i, further(i, k)) for i in chips]
         parts.append(send_to(part, [((j >> 1 & 1, i), (j >> 1 & 1, j)) for i, j in ends]))
-    mine, other = call(sum_kernel, [((128, 512), BF16)] * 2, (total, *parts))
+    half = [((128, 512), BF16)]
+    (other,) = call(functools.partial(sum_kernel, 1), half, (total, *parts))
     swapped = send_to(other, [((i >> 1 & 1, i), (1 - (i >> 1 & 1), i)) for i in chips])
+    (mine,) = call(functools.partial(sum_kernel, 0), half, (total, *parts))
     return jnp.where(lax.axis_index("group") == my_zp() & 1, mine, swapped)
 
 

time: 111 us -> 111 us (level)
    pallas_call x9 -> x10, Pallas kernels: 12 us -> 12.1 us  [call(): pl.pallas_call(kernel, out_shape=[jax.ShapeDtypeStruct(shape, dtype) for...]
where the time goes in v10:
time: 111 us
  starting transfers between devices  43.7 us (39%)
  waiting for transfers between devices  34.3 us (31%)
  blocking collectives  19.8 us (18%)
  Pallas kernels  12.1 us (11%)
    all_to_all x2, waiting for transfers between devices, exchange(): return lax.all_to_all(x, 'ep', 0, 0, axis_index_groups=groups, tiled=True)  22.1 us
    ppermute x8, starting transfers between devices, send_to(): lax.ppermute(x, ('group', 'ep'), [(a * 128 + i, b * 128 + j) for (a, i),...  21.6 us
    all_to_all x1, blocking collectives, exchange(): return lax.all_to_all(x, 'ep', 0, 0, axis_index_groups=groups, tiled=True)  19.8 us
    all_to_all x2, starting transfers between devices, exchange(): return lax.all_to_all(x, 'ep', 0, 0, axis_index_groups=groups, tiled=True)  18.8 us
    ppermute x8, waiting for transfers between devices, send_to(): lax.ppermute(x, ('group', 'ep'), [(a * 128 + i, b * 128 + j) for (a, i),...  12.1 us
    pallas_call x10, Pallas kernels, call(): pl.pallas_call(kernel, out_shape=[jax.ShapeDtypeStruct(shape, dtype) for...  12.1 us
    ppermute x1, starting transfers between devices, body(): got = lax.ppermute(give, 'group', SWAP)  3.33 us
  transfers between devices with their start and end apart: 11, of which 7 were waited for; matrix products, arithmetic and copies ran while one was open for 0% of the time, Pallas kernels for 1%

profile of v10, /device:TPU:1, one launch (start us, length us, event | category | flops | bytes accessed | tf_op | source)
XLA Modules:
  0.0 110.8 jit_solution(4087758518977293373)
XLA Ops:
  0.0 0.0 copy-start.4
  0.0 3.1 %shard_map.82 = (f32[64,1024]{1,0:T(8,128)S(1)}, f32[64,1024]{1,0:T(8,128)S(1)}) custom-call(bf16[128,1024]{1,0:T(8,128)(2,1)} %x_ref.1, s32[1,128]{1,0:T(1,128)} %bitcast.26, bf16[1024,1024]{1,0:T(8,128)(2,1)} %w_hbm.1), custom_call_target="tpu_custom_call" | custom-call | tf_op jit(solution)/shard_map/pallas_call | solution.py:243
  3.2 3.3 %collective-permute-start = (f32[64,1024]{1,0:T(8,128)S(1)}, f32[64,1024]{1,0:T(8,128)S(1)}, u32[]{:S(2)}, u32[]{:S(2)}) collective-permute-start(f32[64,1024]{1,0:T(8,128)S(1)} %get-tuple-element.22), channel_id=1, source_target_pairs={{0,128},{128,0},{1,129},{129,1},{2,130},{130,2},{3,131},{131,3},{4... | collective-permute-start | bytes 786440 | tf_op jit(solution)/shard_map/ppermute | solution.py:287
  6.5 0.0 copy-done.4
  6.5 6.2 %collective-permute-start.3 = (s32[8,128]{1,0:T(8,128)S(1)}, s32[8,128]{1,0:T(8,128)S(1)}, u32[]{:S(2)}, u32[]{:S(2)}) collective-permute-start(s32[8,128]{1,0:T(8,128)S(1)} %bitcast.19), channel_id=1, source_target_pairs={{128,134},{129,135},{130,128},{131,129},{132,130},{133,131},{134,1... | collective-permute-start | bytes 12296 | tf_op jit(solution)/shard_map/ppermute | solution.py:262
  12.7 2.8 %collective-permute-start.2 = (s32[8,128]{1,0:T(8,128)S(1)}, s32[8,128]{1,0:T(8,128)S(1)}, u32[]{:S(2)}, u32[]{:S(2)}) collective-permute-start(s32[8,128]{1,0:T(8,128)S(1)} %bitcast.20), channel_id=1, source_target_pairs={{128,132},{129,133},{130,134},{131,135},{132,128},{133,129},{134,1... | collective-permute-start | bytes 12296 | tf_op jit(solution)/shard_map/ppermute | solution.py:262
  15.5 4.3 %collective-permute-start.1 = (s32[8,128]{1,0:T(8,128)S(1)}, s32[8,128]{1,0:T(8,128)S(1)}, u32[]{:S(2)}, u32[]{:S(2)}) collective-permute-start(s32[8,128]{1,0:T(8,128)S(1)} %bitcast.21), channel_id=1, source_target_pairs={{128,130},{129,131},{130,132},{131,133},{132,134},{133,135},{134,1... | collective-permute-start | bytes 12296 | tf_op jit(solution)/shard_map/ppermute | solution.py:262
  19.8 0.1 shard_map.83
  19.9 0.0 collective-permute-done.3
  19.9 1.0 collective-permute-done.2
  20.9 1.0 collective-permute-done.1
  22.0 0.0 collective-permute-done.got_ref
  22.0 1.4 %shard_map.84 = bf16[2048,128]{1,0:T(8,128)(2,1)} custom-call(f32[64,1024]{1,0:T(8,128)S(1)} %get-tuple-element.21.keep_ref, f32[64,1024]{1,0:T(8,128)S(1)} %collective-permute-done.got_ref, bf16[256,64]{1,0:T(8,128)(2,1)S(1)} %get-tuple-element.23.chosen_ref, bf16[256,256]{1,0:T(8,128)(2,1)S(1)} %get-tuple-element.24.order_ref), custom_call_target="tpu_custom_call" | custom-call | tf_op jit(solution)/shard_map/pallas_call | solution.py:243
  23.4 0.1 broadcast_in_dim.2
  23.5 1.4 %collective-permute-start.4 = (s32[64,4,8,128]{3,2,1,0:T(8,128)S(1)}, s32[64,4,8,128]{3,2,1,0:T(8,128)S(1)}, u32[]{:S(2)}, u32[]{:S(2)}) collective-permute-start(s32[64,4,8,128]{3,2,1,0:T(8,128)S(1)} %broadcast_in_dim.2), channel_id=1, source_target_pairs={{128,0},{129,1},{130,2},{131,3},{132,4},{133,5},{134,6},{135,7},{1... | collective-permute-start | bytes 3145736 | tf_op jit(solution)/shard_map/ppermute | solution.py:262
  24.9 13.8 %all-to-all-start = ((bf16[128,16,128]{2,1,0:T(8,128)(2,1)}), bf16[128,16,128]{2,1,0:T(8,128)(2,1)S(1)}, u32[]{:S(2)}, u32[]{:S(2)}) async-start(bf16[128,16,128]{2,1,0:T(8,128)(2,1)} %bitcast.6), calls=%async_computation | async-start | bytes 1048576 | tf_op jit(solution)/shard_map/all_to_all | solution.py:266
  38.7 0.4 shard_map.85
  39.0 10.6 %all-to-all-done = bf16[128,16,128]{2,1,0:T(8,128)(2,1)S(1)} async-done(((bf16[128,16,128]{2,1,0:T(8,128)(2,1)}), bf16[128,16,128]{2,1,0:T(8,128)(2,1)S(1)}, u32[]{:S(2)}, u32[]{:S(2)}) %all-to-all-start) | async-done | bytes 524320 | tf_op jit(solution)/shard_map/all_to_all | solution.py:266
  49.6 0.0 collective-permute-done.4
  49.6 1.7 %shard_map.86 = (bf16[768,1024]{1,0:T(8,128)(2,1)S(1)}, bf16[384,1152]{1,0:T(8,128)(2,1)S(1)}) custom-call(bf16[2048,128]{1,0:T(8,128)(2,1)S(1)} %bitcast.17, bf16[256,256]{1,0:T(8,128)(2,1)S(1)} %get-tuple-element.28.order_ref, bf16[768,256]{1,0:T(8,128)(2,1)S(1)} %get-tuple-element.29.expand_ref, s32[4,8,128]{2,1,0:T(8,128)S(1)} %pad_add_fusion.ids_ref, ...), custom_call_target="tpu_custom_call" | custom-call | tf_op jit(solution)/shard_map/pallas_call | solution.py:243
  51.3 0.0 copy-start
  51.3 0.0 copy-start.1
  51.3 0.0 copy-start.2
  51.3 19.8 %all_to_all.15 = bf16[32,24,1024]{2,1,0:T(8,128)(2,1)S(1)} all-to-all(bf16[32,24,1024]{2,1,0:T(8,128)(2,1)S(1)} %bitcast.18), channel_id=1, replica_groups={{41,49,57,65,73,81,89,97,105,113,121,0,8,16,24,32,40,48,56,64,72,80,88,..., dimensions={0} | all-to-all | bytes 3145728 | tf_op jit(solution)/shard_map/all_to_all | solution.py:266
  71.1 0.0 copy-done
  71.1 0.0 copy-done.1
  71.1 0.0 copy-done.2
  71.1 3.6 %shard_map.88 = bf16[768,1024]{1,0:T(8,128)(2,1)} custom-call(bf16[768,1024]{1,0:T(8,128)(2,1)S(1)} %bitcast.16, bf16[1,1024,384]{2,1,0:T(8,128)(2,1)S(1)} %copy-done, bf16[1,1024,384]{2,1,0:T(8,128)(2,1)S(1)} %copy-done.1, bf16[1,384,1024]{2,1,0:T(8,128)(2,1)S(1)} %copy-done.2), custom_call_target="tpu_custom_call" | custom-call | tf_op jit(solution)/shard_map/pallas_call | solution.py:243
  74.7 0.0 copy-start.3
  74.7 5.0 %all-to-all-start.2 = ((bf16[32,24,1024]{2,1,0:T(8,128)(2,1)}), bf16[32,24,1024]{2,1,0:T(8,128)(2,1)S(1)}, u32[]{:S(2)}, u32[]{:S(2)}) async-start(bf16[32,24,1024]{2,1,0:T(8,128)(2,1)} %bitcast.11), calls=%async_computation.2 | async-start | bytes 3145728 | tf_op jit(solution)/shard_map/all_to_all | solution.py:266
  79.7 0.0 copy-done.3
  79.7 0.9 shard_map.87.mix_ref
  80.6 11.6 %all-to-all-done.2 = bf16[32,24,1024]{2,1,0:T(8,128)(2,1)S(1)} async-done(((bf16[32,24,1024]{2,1,0:T(8,128)(2,1)}), bf16[32,24,1024]{2,1,0:T(8,128)(2,1)S(1)}, u32[]{:S(2)}, u32[]{:S(2)}) %all-to-all-start.2) | async-done | bytes 1572896 | tf_op jit(solution)/shard_map/all_to_all | solution.py:266
  92.1 0.8 shard_map.89
  92.9 3.2 %collective-permute-start.5 = (bf16[128,1024]{1,0:T(8,128)(2,1)S(1)}, bf16[128,1024]{1,0:T(8,128)(2,1)S(1)}, u32[]{:S(2)}, u32[]{:S(2)}) collective-permute-start(bf16[128,1024]{1,0:T(8,128)(2,1)S(1)} %get-tuple-element.34), channel_id=1, source_target_pairs={{128,130},{129,131},{2,4},{3,5},{132,134},{133,135},{6,0},{7,1},{1... | collective-permute-start | bytes 786440 | tf_op jit(solution)/shard_map/ppermute | solution.py:262
  96.1 1.8 %collective-permute-start.6 = (bf16[128,1024]{1,0:T(8,128)(2,1)S(1)}, bf16[128,1024]{1,0:T(8,128)(2,1)S(1)}, u32[]{:S(2)}, u32[]{:S(2)}) collective-permute-start(bf16[128,1024]{1,0:T(8,128)(2,1)S(1)} %get-tuple-element.35), channel_id=1, source_target_pairs={{128,134},{129,135},{2,0},{3,1},{132,130},{133,131},{6,4},{7,5},{1... | collective-permute-start | bytes 786440 | tf_op jit(solution)/shard_map/ppermute | solution.py:262
  97.9 0.7 collective-permute-start.7
  98.6 1.1 collective-permute-done.5.two_ref
  99.7 7.1 %collective-permute-done.6.one_ref = bf16[128,1024]{1,0:T(8,128)(2,1)S(1)} collective-permute-done((bf16[128,1024]{1,0:T(8,128)(2,1)S(1)}, bf16[128,1024]{1,0:T(8,128)(2,1)S(1)}, u32[]{:S(2)}, u32[]{:S(2)}) %collective-permute-start.6) | collective-permute-done | bytes 262176 | tf_op jit(solution)/shard_map/ppermute | solution.py:262
  106.8 0.0 collective-permute-done.7.three_ref
  106.8 0.1 shard_map.91
  106.9 1.3 %collective-permute-start.8 = (bf16[128,512]{1,0:T(8,128)(2,1)S(1)}, bf16[128,512]{1,0:T(8,128)(2,1)S(1)}, u32[]{:S(2)}, u32[]{:S(2)}) collective-permute-start(bf16[128,512]{1,0:T(8,128)(2,1)S(1)} %shard_map.91), channel_id=1, source_target_pairs={{0,128},{1,129},{130,2},{131,3},{4,132},{5,133},{134,6},{135,7},{8... | collective-permute-start | bytes 393224 | tf_op jit(solution)/shard_map/ppermute | solution.py:262
  108.2 0.1 shard_map.90
  108.3 1.9 %collective-permute-done.8 = bf16[128,512]{1,0:T(8,128)(2,1)S(1)} collective-permute-done((bf16[128,512]{1,0:T(8,128)(2,1)S(1)}, bf16[128,512]{1,0:T(8,128)(2,1)S(1)}, u32[]{:S(2)}, u32[]{:S(2)}) %collective-permute-start.8) | collective-permute-done | bytes 131104 | tf_op jit(solution)/shard_map/ppermute | solution.py:262
  110.1 0.7 broadcast_select_fusion
  (2 shorter events, 0.0 us)
Async XLA Ops:
  0.0 6.5 %copy-start.4 = (s32[128,8]{0,1:T(8,128)S(1)}, s32[128,8]{0,1:T(8,128)}, u32[]{:S(2)}) copy-start(s32[128,8]{0,1:T(8,128)} %param.10) | copy-start | bytes 12292
  3.2 18.8 %collective-permute-start = (f32[64,1024]{1,0:T(8,128)S(1)}, f32[64,1024]{1,0:T(8,128)S(1)}, u32[]{:S(2)}, u32[]{:S(2)}) collective-permute-start(f32[64,1024]{1,0:T(8,128)S(1)} %get-tuple-element.22), channel_id=1, source_target_pairs={{0,128},{128,0},{1,129},{129,1},{2,130},{130,2},{3,131},{131,3},{4... | collective-permute-start | bytes 786440 | tf_op jit(solution)/shard_map/ppermute | solution.py:287
  6.5 13.4 %collective-permute-start.3 = (s32[8,128]{1,0:T(8,128)S(1)}, s32[8,128]{1,0:T(8,128)S(1)}, u32[]{:S(2)}, u32[]{:S(2)}) collective-permute-start(s32[8,128]{1,0:T(8,128)S(1)} %bitcast.19), channel_id=1, source_target_pairs={{128,134},{129,135},{130,128},{131,129},{132,130},{133,131},{134,1... | collective-permute-start | bytes 12296 | tf_op jit(solution)/shard_map/ppermute | solution.py:262
  12.7 8.3 %collective-permute-start.2 = (s32[8,128]{1,0:T(8,128)S(1)}, s32[8,128]{1,0:T(8,128)S(1)}, u32[]{:S(2)}, u32[]{:S(2)}) collective-permute-start(s32[8,128]{1,0:T(8,128)S(1)} %bitcast.20), channel_id=1, source_target_pairs={{128,132},{129,133},{130,134},{131,135},{132,128},{133,129},{134,1... | collective-permute-start | bytes 12296 | tf_op jit(solution)/shard_map/ppermute | solution.py:262
  15.5 6.5 %collective-permute-start.1 = (s32[8,128]{1,0:T(8,128)S(1)}, s32[8,128]{1,0:T(8,128)S(1)}, u32[]{:S(2)}, u32[]{:S(2)}) collective-permute-start(s32[8,128]{1,0:T(8,128)S(1)} %bitcast.21), channel_id=1, source_target_pairs={{128,130},{129,131},{130,132},{131,133},{132,134},{133,135},{134,1... | collective-permute-start | bytes 12296 | tf_op jit(solution)/shard_map/ppermute | solution.py:262
  23.5 26.1 %collective-permute-start.4 = (s32[64,4,8,128]{3,2,1,0:T(8,128)S(1)}, s32[64,4,8,128]{3,2,1,0:T(8,128)S(1)}, u32[]{:S(2)}, u32[]{:S(2)}) collective-permute-start(s32[64,4,8,128]{3,2,1,0:T(8,128)S(1)} %broadcast_in_dim.2), channel_id=1, source_target_pairs={{128,0},{129,1},{130,2},{131,3},{132,4},{133,5},{134,6},{135,7},{1... | collective-permute-start | bytes 3145736 | tf_op jit(solution)/shard_map/ppermute | solution.py:262
  24.9 24.7 %all-to-all-start = ((bf16[128,16,128]{2,1,0:T(8,128)(2,1)}), bf16[128,16,128]{2,1,0:T(8,128)(2,1)S(1)}, u32[]{:S(2)}, u32[]{:S(2)}) async-start(bf16[128,16,128]{2,1,0:T(8,128)(2,1)} %bitcast.6), calls=%async_computation | async-start | bytes 1048576 | tf_op jit(solution)/shard_map/all_to_all | solution.py:266
  51.3 19.8 %copy-start = (bf16[1,1024,384]{2,1,0:T(8,128)(2,1)S(1)}, bf16[1,1024,384]{2,1,0:T(8,128)(2,1)}, u32[]{:S(2)}) copy-start(bf16[1,1024,384]{2,1,0:T(8,128)(2,1)} %gate_ref.1) | copy-start | bytes 2359300
  51.3 19.8 %copy-start.1 = (bf16[1,1024,384]{2,1,0:T(8,128)(2,1)S(1)}, bf16[1,1024,384]{2,1,0:T(8,128)(2,1)}, u32[]{:S(2)}) copy-start(bf16[1,1024,384]{2,1,0:T(8,128)(2,1)} %up_ref.1) | copy-start | bytes 2359300
  51.3 19.8 %copy-start.2 = (bf16[1,384,1024]{2,1,0:T(8,128)(2,1)S(1)}, bf16[1,384,1024]{2,1,0:T(8,128)(2,1)}, u32[]{:S(2)}) copy-start(bf16[1,384,1024]{2,1,0:T(8,128)(2,1)} %down_ref.1) | copy-start | bytes 2359300
  74.7 5.0 %copy-start.3 = (bf16[1024,128]{1,0:T(8,128)(2,1)S(1)}, bf16[1024,128]{1,0:T(8,128)(2,1)}, u32[]{:S(2)}) copy-start(bf16[1024,128]{1,0:T(8,128)(2,1)} %router_ref.1) | copy-start | bytes 786436
  74.7 17.4 %all-to-all-start.2 = ((bf16[32,24,1024]{2,1,0:T(8,128)(2,1)}), bf16[32,24,1024]{2,1,0:T(8,128)(2,1)S(1)}, u32[]{:S(2)}, u32[]{:S(2)}) async-start(bf16[32,24,1024]{2,1,0:T(8,128)(2,1)} %bitcast.11), calls=%async_computation.2 | async-start | bytes 3145728 | tf_op jit(solution)/shard_map/all_to_all | solution.py:266
  92.9 6.8 %collective-permute-start.5 = (bf16[128,1024]{1,0:T(8,128)(2,1)S(1)}, bf16[128,1024]{1,0:T(8,128)(2,1)S(1)}, u32[]{:S(2)}, u32[]{:S(2)}) collective-permute-start(bf16[128,1024]{1,0:T(8,128)(2,1)S(1)} %get-tuple-element.34), channel_id=1, source_target_pairs={{128,130},{129,131},{2,4},{3,5},{132,134},{133,135},{6,0},{7,1},{1... | collective-permute-start | bytes 786440 | tf_op jit(solution)/shard_map/ppermute | solution.py:262
  96.1 10.7 %collective-permute-start.6 = (bf16[128,1024]{1,0:T(8,128)(2,1)S(1)}, bf16[128,1024]{1,0:T(8,128)(2,1)S(1)}, u32[]{:S(2)}, u32[]{:S(2)}) collective-permute-start(bf16[128,1024]{1,0:T(8,128)(2,1)S(1)} %get-tuple-element.35), channel_id=1, source_target_pairs={{128,134},{129,135},{2,0},{3,1},{132,130},{133,131},{6,4},{7,5},{1... | collective-permute-start | bytes 786440 | tf_op jit(solution)/shard_map/ppermute | solution.py:262
  97.9 8.9 %collective-permute-start.7 = (bf16[128,1024]{1,0:T(8,128)(2,1)S(1)}, bf16[128,1024]{1,0:T(8,128)(2,1)S(1)}, u32[]{:S(2)}, u32[]{:S(2)}) collective-permute-start(bf16[128,1024]{1,0:T(8,128)(2,1)S(1)} %get-tuple-element.36), channel_id=1, source_target_pairs={{0,4},{1,5},{130,134},{131,135},{4,0},{5,1},{134,130},{135,131},{8... | collective-permute-start | bytes 786440 | tf_op jit(solution)/shard_map/ppermute | solution.py:262
  106.9 3.2 %collective-permute-start.8 = (bf16[128,512]{1,0:T(8,128)(2,1)S(1)}, bf16[128,512]{1,0:T(8,128)(2,1)S(1)}, u32[]{:S(2)}, u32[]{:S(2)}) collective-permute-start(bf16[128,512]{1,0:T(8,128)(2,1)S(1)} %shard_map.91), channel_id=1, source_target_pairs={{0,128},{1,129},{130,2},{131,3},{4,132},{5,133},{134,6},{135,7},{8... | collective-permute-start | bytes 393224 | tf_op jit(solution)/shard_map/ppermute | solution.py:262
